TPU v7x, 32 devices: a whole 2x2x4 slice. The times are simulated.
32 devices in a mesh: pb: 2 (over y), pool: 4 (over z), ga: 2 (over x), pert: 2 (over core).
Axes of the slice: x: 2, y: 2, z: 4, core: 2. Of those that a mesh axis runs over, the one named last changes fastest.
Arguments:
- wavefunctions: bfloat16 [64, 12, 240, 128], P('pool', 'ga'), may hold values from -6 to 6
- potentials: float32 [12, 12, 240], P(('pb', 'pert'), 'ga'), parts along dimension 0, may hold values from -6 to 6
- pert_order: int32 [6], replicated, may hold values from 0 to 5, each once
- partners: int32 [128], P('pb'), parts along dimension 0, may hold values from 0 to 63, as said below
Outputs:
- couplings: bfloat16 [128, 6, 2, 128, 128], P(('pb', 'pool'), 'pert', None, 'ga'), parts along dimension 0
There are 2 independent parts, one for each index of `pb`. A program takes and returns all parts, laid end to end along the dimension named above; an argument that names none is the same for every part. Nothing has to cross between parts.
Inputs may be any that keep to these rules, and one draw needn't show every extreme that they name: `partners`: A permutation of the 64 k-points; k-point k is owned by pool k // 16. For any two pools (one pool with itself included), at most 5 k-points of the one have their k+q owned by the other, and exactly 5 for some pair in every draw. The numbers of k-points that one pool takes from each pool are the same list for every pool, up to order. `pert_order`: each number once.
All inputs are finite; a program needn't handle non-finite values.
Results may differ from a plain program's by a relative error of at most 0.0073.
Values may be sent and summed in bfloat16 or wider, within the bound.
No kernel may reach another device: no remote copies, remote signals or barrier semaphores. Data moves between devices by JAX's collectives and lax.ppermute only.
A program may use at most 128 MiB of HBM per device.

v0:
```python
import math

import jax
import jax.numpy as jnp
from jax import lax
from jax.sharding import PartitionSpec as P


def dft_table(length):
    positions = jnp.arange(length, dtype=jnp.int32)
    product = positions[:, None] * positions[None, :] % length
    angles = product.astype(jnp.float32) * (2.0 * math.pi / length)
    cosine = jnp.cos(angles) / math.sqrt(length)
    sine_part = jnp.sin(angles) / math.sqrt(length)
    upper_rows = jnp.concatenate([cosine, -sine_part], axis=1)
    bottom = jnp.concatenate([sine_part, cosine], axis=1)
    return jnp.concatenate([upper_rows, bottom], axis=0).astype(jnp.bfloat16)


def to_real(blocks, lookup_table):
    return jnp.einsum(
        "zg,...gn->...zn", lookup_table, blocks, preferred_element_type=jnp.float32
    ).astype(jnp.bfloat16)


def couple(own_real, other_real, chosen, z_points):
    own_re = own_real[..., :z_points, :].astype(jnp.float32)
    own_im = own_real[..., z_points:, :].astype(jnp.float32)
    pot_re = chosen[:, :z_points, None]
    pot_im = chosen[:, z_points:, None]
    weighted_re = pot_re * own_re - pot_im * own_im
    weighted_im = pot_re * own_im + pot_im * own_re
    weighted = jnp.concatenate([weighted_re, weighted_im], axis=-2).astype(jnp.bfloat16)
    turned = jnp.concatenate([weighted_im, -weighted_re], axis=-2).astype(jnp.bfloat16)
    real_part = jnp.einsum(
        "kcsm,kcsn->kmn", other_real, weighted, preferred_element_type=jnp.float32
    )
    imag_part = jnp.einsum("kcsm,kcsn->kmn", other_real, turned, preferred_element_type=jnp.float32)
    return jnp.stack([real_part, imag_part], axis=1)


def body(wavefunctions, potentials, pert_order, partners):
    local_k, columns, stacked, band_count = wavefunctions.shape
    z_points = stacked // 2
    pool_count = lax.axis_size("pool")
    my_pool = lax.axis_index("pool")
    pert_count = lax.axis_size("pert")
    my_pert = lax.axis_index("pert")
    capacity = max(2, local_k // pool_count + 1)
    lookup_table = dft_table(z_points)
    own_real = to_real(wavefunctions, lookup_table)
    holder_grid = (partners // local_k).reshape(pool_count, local_k)
    position_grid = (partners % local_k).reshape(pool_count, local_k)
    positions = jnp.arange(local_k, dtype=jnp.int32)
    before = positions[None, :] < positions[:, None]
    same_holder = holder_grid[:, :, None] == holder_grid[:, None, :]
    rank_grid = jnp.sum(same_holder & before[None], axis=2)
    slot_ids = jnp.arange(capacity, dtype=jnp.int32)
    matches = (
        (holder_grid == my_pool)[:, None, :] & (rank_grid[:, None, :] == slot_ids[None, :, None])
    ).astype(jnp.int32)
    send_from = jnp.sum(matches * position_grid[:, None, :], axis=2)
    filled = jnp.sum(matches, axis=2) > 0
    my_holder = lax.dynamic_index_in_dim(holder_grid, my_pool, 0, keepdims=False)
    my_rank = lax.dynamic_index_in_dim(rank_grid, my_pool, 0, keepdims=False)
    arrive_at = my_holder * capacity + my_rank
    half_width = columns // pert_count
    my_columns = lax.dynamic_slice_in_dim(wavefunctions, my_pert * half_width, half_width, 1)
    picked = jnp.take(my_columns, send_from.reshape(-1), axis=0)
    picked = picked.reshape((pool_count, capacity) + my_columns.shape[1:])
    received = to_real(
        lax.all_to_all(
            jnp.where(filled[:, :, None, None, None], picked, jnp.zeros((), picked.dtype)),
            "pool",
            split_axis=0,
            concat_axis=0,
            tiled=True,
        ),
        lookup_table,
    )
    flattened = received.reshape((pool_count * capacity,) + received.shape[2:])
    partner_real = lax.all_gather(
        jnp.take(flattened, arrive_at, axis=0), "pert", axis=1, tiled=True
    )
    every_potential = lax.all_gather(potentials, "pert", axis=0, tiled=True)
    per_device = potentials.shape[0]
    my_ids = lax.dynamic_slice_in_dim(pert_order, my_pert * per_device, per_device)
    options_range = jnp.arange(every_potential.shape[0], dtype=jnp.int32)
    selector = my_ids[:, None] == options_range[None, :]
    chosen = jnp.sum(
        jnp.where(selector[:, :, None, None], every_potential[None], jnp.zeros((), jnp.float32)),
        axis=1,
    )
    scaling = 1.0 / math.sqrt(columns * lax.axis_size("ga") * z_points)
    results = []
    for slot_index in range(per_device):
        results.append(couple(own_real, partner_real, chosen[slot_index], z_points))
    partial_sums = jnp.stack(results, axis=1) * scaling
    summed = lax.psum_scatter(partial_sums, "ga", scatter_dimension=3, tiled=True)
    return summed.astype(jnp.bfloat16)


def solution(mesh):
    return jax.shard_map(
        body,
        mesh=mesh,
        in_specs=(P("pool", "ga", None, None), P(("pb", "pert"), "ga", None), P(), P("pb")),
        out_specs=P(("pb", "pool"), "pert", None, "ga", None),
        check_vma=False,
    )
```

profile of v0, /device:TPU:0, one launch (start us, length us, event | category | flops | bytes accessed | tf_op | source)
XLA Modules:
  0.0 260.5 jit_solution(9340605334367735227)
XLA Ops:
  6.5 0.7 and_select_fusion
  7.3 0.2 convert_reduce_fusion
  7.6 0.3 convert_reduce_fusion.1
  8.0 0.1 copy.7
  8.1 0.1 copy.8
  8.3 2.0 constant_dynamic-slice_fusion
  10.3 3.0 %gather_fusion = bf16[20,3,240,128]{3,2,1,0:T(8,128)(2,1)} fusion(bf16[16,3,240,128]{3,2,1,0:T(8,128)(2,1)S(1)} %constant_dynamic-slice_fusion, s32[1024]{0:T(1024)S(1)} %pad_clamp_fusion.1), kind=kCustom, calls=%fused_computation | custom fusion | bytes 7372880 | tf_op jit(solution)/shard_map/jit(_take)/gather | solution.py:69
  13.4 4.4 %select_select_fusion = bf16[4,5,3,240,128]{4,3,2,1,0:T(8,128)(2,1)} fusion(bf16[4,5,3,240,128]{4,3,2,1,0:T(8,128)(2,1)} %bitcast.68, pred[4,5]{1,0:T(4,128)(4,1)S(1)} %copy.8, pred[4,5]{1,0:T(4,128)(4,1)S(1)} %copy.7), kind=kLoop, calls=%fused_computation.55 | loop fusion | flops 3686400 | bytes 7372840 | tf_op jit(solution)/shard_map/jit(_where)/select_n | solution.py:73
  17.7 6.3 %all-to-all-start = ((bf16[4,5,3,240,128]{4,3,2,1,0:T(8,128)(2,1)}), bf16[4,5,3,240,128]{4,3,2,1,0:T(8,128)(2,1)}, u32[]{:S(2)}, u32[]{:S(2)}) async-start(bf16[4,5,3,240,128]{4,3,2,1,0:T(8,128)(2,1)} %select_select_fusion), calls=%async_computation | async-start | bytes 7372800 | tf_op jit(solution)/shard_map/all_to_all | solution.py:72
  24.1 0.3 fusion.61
  24.3 0.3 negate_convert_fusion.3
  24.6 81.9 %all-to-all-done = bf16[4,5,3,240,128]{4,3,2,1,0:T(8,128)(2,1)} async-done(((bf16[4,5,3,240,128]{4,3,2,1,0:T(8,128)(2,1)}), bf16[4,5,3,240,128]{4,3,2,1,0:T(8,128)(2,1)}, u32[]{:S(2)}, u32[]{:S(2)}) %all-to-all-start) | async-done | bytes 3686432 | tf_op jit(solution)/shard_map/all_to_all | solution.py:72
  106.5 5.1 %convolution_convert_fusion = bf16[4,5,3,128,240]{3,4,2,1,0:T(8,128)(2,1)} fusion(bf16[4,5,3,240,128]{4,3,2,1,0:T(8,128)(2,1)} %all-to-all-done, bf16[120,120]{1,0:T(8,128)(2,1)S(1)} %get-tuple-element.35, bf16[120,120]{1,0:T(8,128)(2,1)S(1)} %fusion.61, bf16[120,120]{1,0:T(8,128)(2,1)S(1)} %get-tuple-element.34), kind=kOutput, calls=%fused_computation.57 | convolution fusion | flops 887040000 | bytes 7459200 | tf_op jit(solution)/shard_map/zg,...gn->...zn/dot_general | solution.py:21
  111.5 3.2 %gather_fusion.1 = bf16[16,3,240,128]{3,2,1,0:T(8,128)(2,1)S(1)} fusion(bf16[20,3,240,128]{3,2,1,0:T(8,128)(2,1)} %bitcast.69, s32[1024]{0:T(1024)S(1)} %pad_clamp_fusion), kind=kCustom, calls=%fused_computation.1 | custom fusion | bytes 5898304 | tf_op jit(solution)/shard_map/jit(_take)/gather | solution.py:83
  114.7 1.9 broadcast_select_fusion
  116.8 1.8 all_gather.7
  119.0 4.4 %convert_bitcast_fusion = bf16[16,6,240,128]{3,2,1,0:T(8,128)(2,1)S(1)} fusion(bf16[16,6,240,128]{3,2,1,0:T(8,128)(2,1)} %param.4, bf16[120,120]{1,0:T(8,128)(2,1)S(1)} %get-tuple-element.35, bf16[120,120]{1,0:T(8,128)(2,1)S(1)} %fusion.61, bf16[120,120]{1,0:T(8,128)(2,1)S(1)} %get-tuple-element.34), kind=kOutput, calls=%fused_computation.51 | convolution fusion | flops 1418987520 | bytes 11882880 | tf_op jit(solution)/shard_map/zg,...gn->...zn/dot_general | solution.py:21
  123.4 5.8 %fusion.34 = (bf16[16,6,120,128]{3,2,1,0:T(8,128)(2,1)}, bf16[16,6,120,128]{3,2,1,0:T(8,128)(2,1)}, bf16[16,6,120,128]{3,2,1,0:T(8,128)(2,1)}) fusion(f32[6,120]{1,0:T(8,128)S(1)} %get-tuple-element.36, f32[6,120]{1,0:T(8,128)S(1)} %get-tuple-element.37, bf16[16,6,240,128]{3,2,1,0:T(8,128)(2,1)S(1)} %convert_bitcast_fusion), kind=kLoop, calls=%fused_computation.53 | loop fusion | flops 17694720 | bytes 14751360 | tf_op jit(solution)/shard_map/convert.6
  129.2 7.4 %fusion.35 = (bf16[16,6,120,128]{3,2,1,0:T(8,128)(2,1)}, bf16[16,6,120,128]{3,2,1,0:T(8,128)(2,1)}, bf16[16,6,120,128]{3,2,1,0:T(8,128)(2,1)}, bf16[16,6,120,128...) fusion(f32[6,120]{1,0:T(8,128)S(1)} %get-tuple-element.25, ...), kind=kLoop, calls=%fused_computation.54 | loop fusion | flops 32440320 | bytes 23604480 | tf_op jit(solution)/shard_map/convert.10
  136.6 6.5 %fusion.51 = f32[16,1,128,128]{3,2,0,1:T(8,128)S(1)} fusion(bf16[16,6,240,128]{3,2,1,0:T(8,128)(2,1)} %all-gather.2.cloned.1.call-done, bf16[16,6,120,128]{3,2,1,0:T(8,128)(2,1)} %get-tuple-element.10, bf16[16,6,120,128]{3,2,1,0:T(8,128)(2,1)} %get-tuple-element.9), kind=kOutput, calls=%fused_computation.66 | convolution fusion | flops 766771200 | bytes 12845056 | tf_op jit(solution)/shard_map/kcsm,kcsn->kmn/dot_general | solution.py:35
  143.2 4.4 %fusion.48 = f32[16,1,128,128]{3,2,0,1:T(8,128)S(1)} fusion(bf16[16,6,240,128]{3,2,1,0:T(8,128)(2,1)} %all-gather.2.cloned.1.call-done, bf16[16,6,120,128]{3,2,1,0:T(8,128)(2,1)S(1)} %copy-done.3, bf16[16,6,120,128]{3,2,1,0:T(8,128)(2,1)S(1)} %copy-done.2), kind=kOutput, calls=%fused_computation.65 | convolution fusion | flops 766771200 | bytes 12845056 | tf_op jit(solution)/shard_map/kcsm,kcsn->kmn/dot_general | solution.py:38
  147.6 0.2 maximum_bitcast_fusion
  147.8 5.8 %fusion.42 = f32[16,1,128,128]{3,2,0,1:T(8,128)S(1)} fusion(bf16[16,6,240,128]{3,2,1,0:T(8,128)(2,1)} %all-gather.2.cloned.1.call-done, bf16[16,6,120,128]{3,2,1,0:T(8,128)(2,1)} %get-tuple-element.14, bf16[16,6,120,128]{3,2,1,0:T(8,128)(2,1)S(1)} %copy-done.5), kind=kOutput, calls=%fused_computation.63 | convolution fusion | flops 766771200 | bytes 12845056 | tf_op jit(solution)/shard_map/kcsm,kcsn->kmn/dot_general | solution.py:38
  153.6 6.7 %fusion.45 = f32[16,1,128,128]{3,2,0,1:T(8,128)} fusion(bf16[16,6,240,128]{3,2,1,0:T(8,128)(2,1)} %all-gather.2.cloned.1.call-done, bf16[16,6,120,128]{3,2,1,0:T(8,128)(2,1)} %get-tuple-element.13, bf16[16,6,120,128]{3,2,1,0:T(8,128)(2,1)S(1)} %copy-done.4), kind=kOutput, calls=%fused_computation.64 | convolution fusion | flops 766771200 | bytes 12845056 | tf_op jit(solution)/shard_map/kcsm,kcsn->kmn/dot_general | solution.py:35
  160.3 1.4 maximum_bitcast_fusion.1
  161.7 4.4 %fusion.39 = f32[16,1,128,128]{3,2,0,1:T(8,128)S(1)} fusion(bf16[16,6,240,128]{3,2,1,0:T(8,128)(2,1)} %all-gather.2.cloned.1.call-done, bf16[16,6,120,128]{3,2,1,0:T(8,128)(2,1)S(1)} %copy-done, bf16[16,6,120,128]{3,2,1,0:T(8,128)(2,1)S(1)} %copy-done.1), kind=kOutput, calls=%fused_computation.62 | convolution fusion | flops 766771200 | bytes 12845056 | tf_op jit(solution)/shard_map/kcsm,kcsn->kmn/dot_general | solution.py:35
  166.2 4.2 %fusion.36 = f32[16,1,128,128]{3,2,0,1:T(8,128)S(1)} fusion(bf16[16,6,240,128]{3,2,1,0:T(8,128)(2,1)} %all-gather.2.cloned.1.call-done, bf16[16,6,120,128]{3,2,1,0:T(8,128)(2,1)S(1)} %get-tuple-element.18, bf16[16,6,120,128]{3,2,1,0:T(8,128)(2,1)S(1)} %copy-done), kind=kOutput, calls=%fused_computation.61 | convolution fusion | flops 766771200 | bytes 12845056 | tf_op jit(solution)/shard_map/kcsm,kcsn->kmn/dot_general | solution.py:38
  170.3 0.2 maximum_bitcast_fusion.2
  170.6 3.4 %maximum_multiply_fusion = f32[16,3,2,128,128]{4,3,0,2,1:T(8,128)} fusion(f32[16,1,2,128,128]{4,3,0,2,1:T(8,128)S(1)} %maximum_bitcast_fusion.2, f32[16,1,2,128,128]{4,3,0,2,1:T(8,128)S(1)} %maximum_bitcast_fusion.1, f32[16,1,2,128,128]{4,3,0,2,1:T(8,128)S(1)} %maximum_bitcast_fusion), kind=kLoop, calls=%fused_computation.14 | loop fusion | flops 4718592 | bytes 12582912 | tf_op jit(solution)/shard_map/mul | solution.py:98
  174.0 76.2 %reduce-scatter.2.cloned.1.call-done = f32[16,3,2,64,128]{4,3,0,2,1:T(8,128)} async-done(((f32[16,3,2,128,128]{4,3,0,2,1:T(8,128)}), f32[16,3,2,64,128]{4,3,0,2,1:T(8,128)}) %reduce-scatter.2.cloned.1.call-update) | async-done | bytes 3145744 | tf_op jit(solution)/shard_map/reduce_scatter | solution.py:99
  250.2 2.2 convert_element_type.56
  252.4 1.3 copy.10
  (39 shorter events, 0.9 us)
Async XLA Ops:
  17.7 88.8 %all-to-all-start = ((bf16[4,5,3,240,128]{4,3,2,1,0:T(8,128)(2,1)}), bf16[4,5,3,240,128]{4,3,2,1,0:T(8,128)(2,1)}, u32[]{:S(2)}, u32[]{:S(2)}) async-start(bf16[4,5,3,240,128]{4,3,2,1,0:T(8,128)(2,1)} %select_select_fusion), calls=%async_computation | async-start | bytes 7372800 | tf_op jit(solution)/shard_map/all_to_all | solution.py:72
  24.0 112.6 %all-gather.2.cloned.1.call-start = ((), (), s32[]{:S(2)}) async-start(), calls=%async_computation.2 | async-start | bytes 8847360 | tf_op jit(solution)/shard_map/all_gather | solution.py:82
  114.7 2.0 copy-start.7
  114.7 2.1 copy-start.6
  116.7 133.5 %reduce-scatter.2.cloned.1.call-start = ((), (), s32[]{:S(2)}) async-start(), calls=%async_computation.3 | async-start | bytes 9437184 | tf_op jit(solution)/shard_map/reduce_scatter | solution.py:99
  136.6 6.6 %copy-start.2 = (bf16[16,6,120,128]{3,2,1,0:T(8,128)(2,1)S(1)}, bf16[16,6,120,128]{3,2,1,0:T(8,128)(2,1)}, u32[]{:S(2)}) copy-start(bf16[16,6,120,128]{3,2,1,0:T(8,128)(2,1)} %get-tuple-element.10) | copy-start | bytes 8847364
  136.6 6.6 %copy-start.3 = (bf16[16,6,120,128]{3,2,1,0:T(8,128)(2,1)S(1)}, bf16[16,6,120,128]{3,2,1,0:T(8,128)(2,1)}, u32[]{:S(2)}) copy-start(bf16[16,6,120,128]{3,2,1,0:T(8,128)(2,1)} %get-tuple-element.11) | copy-start | bytes 8847364
  143.2 4.6 %copy-start.5 = (bf16[16,6,120,128]{3,2,1,0:T(8,128)(2,1)S(1)}, bf16[16,6,120,128]{3,2,1,0:T(8,128)(2,1)}, u32[]{:S(2)}) copy-start(bf16[16,6,120,128]{3,2,1,0:T(8,128)(2,1)} %get-tuple-element.13) | copy-start | bytes 8847364
  147.8 5.8 %copy-start.4 = (bf16[16,6,120,128]{3,2,1,0:T(8,128)(2,1)S(1)}, bf16[16,6,120,128]{3,2,1,0:T(8,128)(2,1)}, u32[]{:S(2)}) copy-start(bf16[16,6,120,128]{3,2,1,0:T(8,128)(2,1)} %get-tuple-element.12) | copy-start | bytes 8847364
  153.6 8.1 %copy-start = (bf16[16,6,120,128]{3,2,1,0:T(8,128)(2,1)S(1)}, bf16[16,6,120,128]{3,2,1,0:T(8,128)(2,1)}, u32[]{:S(2)}) copy-start(bf16[16,6,120,128]{3,2,1,0:T(8,128)(2,1)} %get-tuple-element.19) | copy-start | bytes 8847364
  153.6 8.1 %copy-start.1 = (bf16[16,6,120,128]{3,2,1,0:T(8,128)(2,1)S(1)}, bf16[16,6,120,128]{3,2,1,0:T(8,128)(2,1)}, u32[]{:S(2)}) copy-start(bf16[16,6,120,128]{3,2,1,0:T(8,128)(2,1)} %get-tuple-element.20) | copy-start | bytes 8847364
Sparse Core Ops, SparseCore 0:
  116.8 15.2 all-gather.1
  174.1 76.0 reduce-scatter.1
where the time goes:
time: 261 us
  waiting for transfers between devices  158 us (61%)
  matrix products  41.4 us (16%)
  other arithmetic  28.8 us (11%)
  between operations  13.7 us (5%)
  local copies, waits for them, and re-layouts  10.3 us (4%)
  starting transfers between devices  6.36 us (2%)
    all_to_all x1, waiting for transfers between devices, body(): lax.all_to_all(jnp.where(filled[:, :, None, None, None], picked, jnp.zero...  81.9 us
    reduce_scatter x1, waiting for transfers between devices, body(): lax.psum_scatter(partial_sums, 'ga', scatter_dimension=3, tiled=True)  76.2 us
    dot_general x3, matrix products, couple(): jnp.einsum('kcsm,kcsn->kmn', other_real, weighted, preferred_element_type...  17.7 us
    dot_general x3, matrix products, couple(): jnp.einsum('kcsm,kcsn->kmn', other_real, turned, preferred_element_type=j...  14.3 us
    another operation x4, other arithmetic  13.7 us
    dot_general x2, matrix products, to_real(): jnp.einsum('zg,...gn->...zn', lookup_table, blocks, preferred_element_typ...  9.47 us
    all_to_all x1, starting transfers between devices, body(): lax.all_to_all(jnp.where(filled[:, :, None, None, None], picked, jnp.zero...  6.32 us
  transfers between devices with their start and end apart: 3, of which 2 were waited for; matrix products, arithmetic and copies ran while one was open for 7% of the time, Pallas kernels for 0%

commit v1 on v0

v1 whole, which is shorter than its diff:
```python
import functools
import math

import jax
import jax.numpy as jnp
from jax import lax
from jax.experimental import pallas as pl
from jax.experimental.pallas import tpu as pltpu
from jax.sharding import PartitionSpec as P

BF16 = jnp.bfloat16
F32 = jnp.float32
ANY = pl.BlockSpec(memory_space=pl.ANY)
SMEM = pl.BlockSpec(memory_space=pltpu.SMEM)
VMEM_LIMIT = 48 * 1024 * 1024


def dft_table(length):
    positions = jnp.arange(length, dtype=jnp.int32)
    product = positions[:, None] * positions[None, :] % length
    angles = product.astype(F32) * (2.0 * math.pi / length)
    cosine = jnp.cos(angles) / math.sqrt(length)
    sine_part = jnp.sin(angles) / math.sqrt(length)
    upper_rows = jnp.concatenate([cosine, -sine_part], axis=1)
    bottom = jnp.concatenate([sine_part, cosine], axis=1)
    return jnp.concatenate([upper_rows, bottom], axis=0).astype(BF16)


def plan_kernel(pools, local_k, cap, ids, partners, waves, plan, *rest):
    sends, sems = rest[:-1], rest[-1]
    me, core = ids[0], ids[1]
    places, counts = pools * cap, 2 * pools * cap

    def clear(i, carry):
        plan[i] = 0
        return carry

    lax.fori_loop(0, counts + 2 * pools, clear, 0)

    for shift in range(1, pools):
        taker = lax.rem(me + shift, pools)
        tally = counts + pools + shift

        def give(t, carry, shift=shift, taker=taker, tally=tally):
            want = partners[taker * local_k + t]

            @pl.when(lax.div(want, local_k) == me)
            def _():
                slot = plan[tally]
                pltpu.make_async_copy(
                    waves.at[lax.rem(want, local_k) * 2 + core],
                    sends[shift - 1].at[slot],
                    sems.at[shift - 1, slot],
                ).start()
                plan[tally] = slot + 1

            return carry

        lax.fori_loop(0, local_k, give, 0)

    def need(t, carry):
        want = partners[me * local_k + t]
        holder = lax.div(want, local_k)
        shift = lax.rem(me - holder + pools, pools)
        slot = plan[counts + shift]
        plan[shift * cap + slot] = t
        plan[places + shift * cap + slot] = want - holder * local_k
        plan[counts + shift] = slot + 1
        return carry

    lax.fori_loop(0, local_k, need, 0)

    for shift in range(1, pools):
        for slot in range(cap):

            @pl.when(slot < plan[counts + pools + shift])
            def _(shift=shift, slot=slot):
                pltpu.make_async_copy(
                    waves.at[0], sends[shift - 1].at[slot], sems.at[shift - 1, slot]
                ).wait()


def make_plan(ids, partners, waves, pools, local_k, cap):
    shape = (cap,) + waves.shape[1:]
    out = pl.pallas_call(
        functools.partial(plan_kernel, pools, local_k, cap),
        out_shape=[jax.ShapeDtypeStruct((2 * pools * cap + 2 * pools,), jnp.int32)]
        + [jax.ShapeDtypeStruct(shape, waves.dtype)] * (pools - 1),
        in_specs=[SMEM, SMEM, ANY],
        out_specs=[SMEM] + [ANY] * (pools - 1),
        scratch_shapes=[pltpu.SemaphoreType.DMA((pools - 1, cap))],
        name="plan_and_pick",
    )(ids, partners, waves)
    return out[0], out[1:]


def to_real(first, second, table, z_points):
    stacked = 2 * z_points
    cols = []
    for half in (first, second):
        for c in range(half.shape[0] // stacked):
            cols.append(half[c * stacked : (c + 1) * stacked])
    re, im = [], []
    for c in range(0, len(cols), 2):
        pair = jnp.concatenate(cols[c : c + 2], axis=1)
        out = jnp.dot(table, pair, preferred_element_type=F32)
        bands = pair.shape[1] // 2
        for side in range(2):
            lanes = slice(side * bands, (side + 1) * bands)
            re.append(out[:z_points, lanes])
            im.append(out[z_points:, lanes])
    return jnp.concatenate(re, axis=0).astype(BF16), jnp.concatenate(im, axis=0).astype(BF16)


def couple_kernel(pools, cap, shift, groups, z_points, scaling, plan, ids, table, pots,
                  own_a, own_b, other_a, other_b, keep, *rest):
    sends, whole = rest[:-1], rest[-1]
    slot = pl.program_id(0)
    my_group = ids[2]

    @pl.when(slot < plan[2 * pools * cap + shift])
    def _():
        lookup = table[...]
        own_re, own_im = to_real(own_a[0], own_b[0], lookup, z_points)
        u_re, u_im = own_re.astype(F32), own_im.astype(F32)
        o_re, o_im = to_real(other_a[0], other_b[0], lookup, z_points)
        other = jnp.concatenate([o_re, o_im], axis=1)
        bands = o_re.shape[1]
        share = bands // groups
        for j in range(pots.shape[0]):
            p_re, p_im = pots[j, 0], pots[j, 1]
            w_re = (p_re * u_re - p_im * u_im).astype(BF16)
            w_im = (p_re * u_im + p_im * u_re).astype(BF16)
            both = lax.dot_general(
                other, jnp.concatenate([w_re, w_im], axis=1),
                (((0,), (0,)), ((), ())), preferred_element_type=F32,
            )
            whole[2 * j] = (both[:bands, :bands] + both[bands:, bands:]) * scaling
            whole[2 * j + 1] = (both[:bands, bands:] - both[bands:, :bands]) * scaling
        for step in range(groups):
            start = pl.multiple_of(lax.rem(my_group + step, groups) * share, share)
            for part in range(2 * pots.shape[0]):
                block = whole[part, pl.ds(start, share), :]
                if step == 0:
                    keep[0, part] = block
                else:
                    sends[step - 1][0, part] = block.astype(BF16)


def couple(plan, ids, table, pots, waves, other_a, other_b, shift, pools, cap, groups, scaling):
    half, bands = waves.shape[1:]
    z_points = table.shape[0] // 2
    parts = 2 * pots.shape[0]
    share = bands // groups
    places = pools * cap
    block = (1, half, bands)

    def own(side):
        def where(i, plan, ids):
            core = ids[1] if side == 0 else 1 - ids[1]
            return plan[shift * cap + i] * 2 + core, 0, 0
        return pl.BlockSpec(block, where)

    def partner(side):
        def local(i, plan, ids):
            core = ids[1] if side == 0 else 1 - ids[1]
            return plan[places + i] * 2 + core, 0, 0

        def arrived(i, plan, ids):
            return i, 0, 0
        return pl.BlockSpec(block, local if shift == 0 else arrived)

    out_block = pl.BlockSpec((1, parts, share, bands), lambda i, plan, ids: (i, 0, 0, 0))
    rows = 2 * half // 2
    flops = cap * 2 * (parts // 2 * 4 * bands * bands * rows + 4 * half * 2 * z_points * bands)
    out = pl.pallas_call(
        functools.partial(couple_kernel, pools, cap, shift, groups, z_points, scaling),
        grid_spec=pltpu.PrefetchScalarGridSpec(
            num_scalar_prefetch=2,
            grid=(cap,),
            in_specs=[
                pl.BlockSpec(table.shape, lambda i, plan, ids: (0, 0)),
                pl.BlockSpec(pots.shape, lambda i, plan, ids: (0, 0, 0, 0)),
                own(0), own(1), partner(0), partner(1),
            ],
            out_specs=[out_block] * groups,
            scratch_shapes=[pltpu.VMEM((parts, bands, bands), F32)],
        ),
        out_shape=[jax.ShapeDtypeStruct((cap, parts, share, bands), F32)]
        + [jax.ShapeDtypeStruct((cap, parts, share, bands), BF16)] * (groups - 1),
        compiler_params=pltpu.CompilerParams(vmem_limit_bytes=VMEM_LIMIT),
        cost_estimate=pl.CostEstimate(
            flops=flops * 2, bytes_accessed=cap * 8 * half * bands, transcendentals=0
        ),
        name="couple",
    )(plan, ids, table, pots, waves, waves, other_a, other_b)
    return out[0], out[1:]


def combine_kernel(pools, cap, shift, terms, plan, *refs):
    result, stage, sems = refs[-3:]
    kept, arrived = refs[-4 - terms], refs[-3 - terms : -3]
    slot = pl.program_id(0)
    count = plan[2 * pools * cap + shift]

    def copy(i):
        return pltpu.make_async_copy(stage.at[i], result.at[plan[shift * cap + i]], sems.at[i])

    @pl.when(slot < count)
    def _():
        total = kept[0]
        for term in arrived:
            total = total + term[0].astype(F32)
        stage[slot] = total.astype(BF16)
        copy(slot).start()

    @pl.when(slot == cap - 1)
    def _():
        for i in range(cap):

            @pl.when(i < count)
            def _(i=i):
                copy(i).wait()


def combine(plan, before, kept, arrived, local_k, shift, pools, cap):
    shape = kept.shape[1:]
    block = pl.BlockSpec((1,) + shape, lambda i, plan: (i, 0, 0, 0))
    operands = ([] if before is None else [before]) + [kept, *arrived]
    return pl.pallas_call(
        functools.partial(combine_kernel, pools, cap, shift, len(arrived)),
        grid_spec=pltpu.PrefetchScalarGridSpec(
            num_scalar_prefetch=1,
            grid=(cap,),
            in_specs=([] if before is None else [ANY]) + [block] * (1 + len(arrived)),
            out_specs=ANY,
            scratch_shapes=[
                pltpu.VMEM((cap,) + shape, BF16), pltpu.SemaphoreType.DMA((cap,)),
            ],
        ),
        out_shape=jax.ShapeDtypeStruct((local_k,) + shape, BF16),
        input_output_aliases={} if before is None else {1: 0},
        compiler_params=pltpu.CompilerParams(vmem_limit_bytes=VMEM_LIMIT),
        cost_estimate=pl.CostEstimate(
            flops=0, bytes_accessed=8 * kept.size, transcendentals=0
        ),
        name="combine",
    )(plan, *operands)


def body(wavefunctions, potentials, pert_order, partners):
    local_k, columns, stacked, bands = wavefunctions.shape
    z_points = stacked // 2
    pools = lax.axis_size("pool")
    groups = lax.axis_size("ga")
    cores = lax.axis_size("pert")
    my_pool = lax.axis_index("pool")
    my_core = lax.axis_index("pert")
    my_group = lax.axis_index("ga")
    cap = max(2, local_k // pools + 1)
    half = columns // cores
    ids = jnp.stack([my_pool, my_core, my_group]).astype(jnp.int32)
    waves = wavefunctions.reshape(local_k * cores, half * stacked, bands)

    plan, sends = make_plan(ids, partners, waves, pools, local_k, cap)
    swap_cores = [(c, cores - 1 - c) for c in range(cores)]
    other_pots = lax.ppermute(potentials, "pert", swap_cores)

    arrivals = {0: (waves, waves)}
    for shift in range(1, pools):
        pairs = [(s, (s + shift) % pools) for s in range(pools)]
        got = lax.ppermute(sends[shift - 1], "pool", pairs)
        arrivals[shift] = (got, lax.ppermute(got, "pert", swap_cores))

    table = dft_table(z_points)
    per_device = potentials.shape[0]
    my_ids = lax.dynamic_slice_in_dim(pert_order, my_core * per_device, per_device)
    stored = jnp.where(my_core == 0, jnp.stack([potentials, other_pots]), jnp.stack([other_pots, potentials]))
    stored = stored.reshape((cores * per_device,) + potentials.shape[1:])
    options = jnp.arange(cores * per_device, dtype=jnp.int32)
    chosen = jnp.sum(
        jnp.where((my_ids[:, None] == options[None, :])[:, :, None, None], stored[None], jnp.zeros((), F32)),
        axis=1,
    )
    chosen = chosen.reshape(per_device, 2, half, 2, z_points)
    chosen = jnp.where(my_core == 0, chosen, chosen[:, ::-1])
    pots = jnp.moveaxis(chosen, 3, 1).reshape(per_device, 2, columns * z_points, 1)
    pots = jnp.broadcast_to(pots, (per_device, 2, columns * z_points, bands))

    scaling = 1.0 / math.sqrt(columns * groups * z_points)
    result = None
    for shift in range(pools):
        kept, gives = couple(
            plan, ids, table, pots, waves, *arrivals[shift], shift, pools, cap, groups, scaling
        )
        terms = [
            lax.ppermute(gives[step - 1], "ga", [(s, (s + step) % groups) for s in range(groups)])
            for step in range(1, groups)
        ]
        result = combine(plan, result, kept, terms, local_k, shift, pools, cap)
    share = bands // groups
    return result.reshape(local_k, per_device, 2, share, bands)


def solution(mesh):
    return jax.shard_map(
        body,
        mesh=mesh,
        in_specs=(P("pool", "ga", None, None), P(("pb", "pert"), "ga", None), P(), P("pb")),
        out_specs=P(("pb", "pool"), "pert", None, "ga", None),
        check_vma=False,
    )
```

time: 261 us -> 209 us (0.80)
  the two profiles are of different devices: /device:TPU:0 before, /device:TPU:14 now
where the time goes in v1:
time: 209 us; the launch traced here: 211 us
  Pallas kernels  105 us (50%)
  waiting for transfers between devices  95.1 us (46%)
  starting transfers between devices  9.02 us (4%)
    ppermute x3, waiting for transfers between devices, body(): got = lax.ppermute(sends[shift - 1], 'pool', pairs)  76.7 us
    pallas_call x1, Pallas kernels, make_plan(): pl.pallas_call(functools.partial(plan_kernel, pools, local_k, cap), out_s...  75.5 us
    pallas_call x4, Pallas kernels, couple(): pl.pallas_call(functools.partial(couple_kernel, pools, cap, shift, groups...  23.5 us
    ppermute x4, waiting for transfers between devices, body(): lax.ppermute(gives[step - 1], 'ga', [(s, (s + step) % groups) for s in ra...  18.4 us
    pallas_call x4, Pallas kernels, combine(): pl.pallas_call(functools.partial(combine_kernel, pools, cap, shift, len(a...  5.56 us
    ppermute x3, starting transfers between devices, body(): got = lax.ppermute(sends[shift - 1], 'pool', pairs)  4.69 us
    ppermute x4, starting transfers between devices, body(): lax.ppermute(gives[step - 1], 'ga', [(s, (s + step) % groups) for s in ra...  4.3 us
  transfers between devices with their start and end apart: 11, of which 6 were waited for; matrix products, arithmetic and copies ran while one was open for 1% of the time, Pallas kernels for 13%

profile of v1, /device:TPU:14, one launch (start us, length us, event | category | flops | bytes accessed | tf_op | source)
XLA Modules:
  0.0 211.2 jit_solution(16734573816847418391)
XLA Ops:
  0.0 0.7 pad_add_fusion.ids
  0.7 75.5 %plan_and_pick.1 = (s32[48]{0:T(128)}, bf16[5,720,128]{2,1,0:T(8,128)(2,1)}, bf16[5,720,128]{2,1,0:T(8,128)(2,1)}, bf16[5,720,128]{2,1,0:T(8,128)(2,1)}) custom-call(s32[3]{0:T(128)} %pad_add_fusion.ids, s32[64]{0:T(128)} %partners.1, bf16[32,720,128]{2,1,0:T(8,128)(2,1)} %bitcast.10), custom_call_target="tpu_custom_call" | custom-call | tf_op jit(solution)/shard_map/plan_and_pick/pallas_call | solution.py:85
  76.2 1.7 collective-permute-start.2
  77.8 1.2 collective-permute-start.5
  79.1 1.7 collective-permute-start.8
  80.8 0.3 fusion.5
  81.1 0.1 dynamic_slice.3
  81.2 0.3 negate_convert_fusion
  81.5 0.1 iota_compare_fusion
  81.6 57.0 %collective-permute-done.2.other_a = bf16[5,720,128]{2,1,0:T(8,128)(2,1)S(1)} collective-permute-done((bf16[5,720,128]{2,1,0:T(8,128)(2,1)}, bf16[5,720,128]{2,1,0:T(8,128)(2,1)S(1)}, u32[]{:S(2)}, u32[]{:S(2)}) %collective-permute-start.2) | collective-permute-done | bytes 921632 | tf_op jit(solution)/shard_map/ppermute | solution.py:272
  138.5 0.1 maximum_maximum_fusion.table
  138.7 0.1 select_reduce_fusion
  138.7 0.1 reshape.44
  138.8 18.3 %collective-permute-done.5.other_a = bf16[5,720,128]{2,1,0:T(8,128)(2,1)S(1)} collective-permute-done((bf16[5,720,128]{2,1,0:T(8,128)(2,1)}, bf16[5,720,128]{2,1,0:T(8,128)(2,1)S(1)}, u32[]{:S(2)}, u32[]{:S(2)}) %collective-permute-start.5) | collective-permute-done | bytes 921632 | tf_op jit(solution)/shard_map/ppermute | solution.py:272
  157.1 0.1 broadcast_in_dim.35
  157.2 1.5 collective-permute-done.8.other_a
  158.8 0.6 broadcast_in_dim.36.pots
  159.4 5.1 %couple.4 = (f32[5,6,64,128]{3,2,1,0:T(8,128)S(1)}, bf16[5,6,64,128]{3,2,1,0:T(8,128)(2,1)S(1)}) custom-call(s32[48]{0:T(128)S(1)} %copy-done, s32[3]{0:T(128)S(1)} %copy-done.1, bf16[240,240]{1,0:T(8,128)(2,1)S(1)} %maximum_maximum_fusion.table, f32[3,2,720,128]{3,2,1,0:T(8,128)S(1)} %broadcast_in_dim.36.pots, bf16[32,720,128]{2,1,0:T(8,128)(2,1)} %bitcast.11, ...), custom_call_target="tpu_custom_call" | custom-call | flops 4600627200 | bytes 3686400 | tf_op jit(solution)/shard_map/couple/pallas_call | solution.py:176
  164.6 0.6 collective-permute-start.1
  165.2 6.8 %couple.5 = (f32[5,6,64,128]{3,2,1,0:T(8,128)S(1)}, bf16[5,6,64,128]{3,2,1,0:T(8,128)(2,1)S(1)}) custom-call(s32[48]{0:T(128)S(1)} %copy-done, s32[3]{0:T(128)S(1)} %copy-done.1, bf16[240,240]{1,0:T(8,128)(2,1)S(1)} %maximum_maximum_fusion.table, f32[3,2,720,128]{3,2,1,0:T(8,128)S(1)} %broadcast_in_dim.36.pots, bf16[32,720,128]{2,1,0:T(8,128)(2,1)} %bitcast.15, ...), custom_call_target="tpu_custom_call" | custom-call | flops 4600627200 | bytes 3686400 | tf_op jit(solution)/shard_map/couple/pallas_call | solution.py:176
  172.0 1.6 collective-permute-start.4
  173.6 6.8 %couple.6 = (f32[5,6,64,128]{3,2,1,0:T(8,128)S(1)}, bf16[5,6,64,128]{3,2,1,0:T(8,128)(2,1)S(1)}) custom-call(s32[48]{0:T(128)S(1)} %copy-done, s32[3]{0:T(128)S(1)} %copy-done.1, bf16[240,240]{1,0:T(8,128)(2,1)S(1)} %maximum_maximum_fusion.table, f32[3,2,720,128]{3,2,1,0:T(8,128)S(1)} %broadcast_in_dim.36.pots, bf16[32,720,128]{2,1,0:T(8,128)(2,1)} %bitcast.17, ...), custom_call_target="tpu_custom_call" | custom-call | flops 4600627200 | bytes 3686400 | tf_op jit(solution)/shard_map/couple/pallas_call | solution.py:176
  180.4 0.6 collective-permute-start.7
  181.0 4.7 %couple.7 = (f32[5,6,64,128]{3,2,1,0:T(8,128)S(1)}, bf16[5,6,64,128]{3,2,1,0:T(8,128)(2,1)S(1)}) custom-call(s32[48]{0:T(128)S(1)} %copy-done, s32[3]{0:T(128)S(1)} %copy-done.1, bf16[240,240]{1,0:T(8,128)(2,1)S(1)} %maximum_maximum_fusion.table, f32[3,2,720,128]{3,2,1,0:T(8,128)S(1)} %broadcast_in_dim.36.pots, bf16[32,720,128]{2,1,0:T(8,128)(2,1)} %bitcast.19, ...), custom_call_target="tpu_custom_call" | custom-call | flops 4600627200 | bytes 3686400 | tf_op jit(solution)/shard_map/couple/pallas_call | solution.py:176
  185.7 1.6 collective-permute-start.10
  187.3 1.3 combine.4.refs_0_
  188.6 0.6 collective-permute-done.4.refs_2_
  189.2 1.4 combine.5.refs_0_
  190.6 9.1 %collective-permute-done.7.refs_2_ = bf16[5,6,64,128]{3,2,1,0:T(8,128)(2,1)S(1)} collective-permute-done((bf16[5,6,64,128]{3,2,1,0:T(8,128)(2,1)S(1)}, bf16[5,6,64,128]{3,2,1,0:T(8,128)(2,1)S(1)}, u32[]{:S(2)}, u32[]{:S(2)}) %collective-permute-start.7) | collective-permute-done | bytes 491552 | tf_op jit(solution)/shard_map/ppermute | solution.py:297
  199.7 1.4 combine.6.refs_0_
  201.1 8.7 %collective-permute-done.10.refs_2_ = bf16[5,6,64,128]{3,2,1,0:T(8,128)(2,1)S(1)} collective-permute-done((bf16[5,6,64,128]{3,2,1,0:T(8,128)(2,1)S(1)}, bf16[5,6,64,128]{3,2,1,0:T(8,128)(2,1)S(1)}, u32[]{:S(2)}, u32[]{:S(2)}) %collective-permute-start.10) | collective-permute-done | bytes 491552 | tf_op jit(solution)/shard_map/ppermute | solution.py:297
  209.8 1.4 combine.7
  (20 shorter events, 0.1 us)
Async XLA Ops:
  0.7 78.4 %copy-start.2 = (f32[3,6,240]{2,1,0:T(8,128)S(1)}, f32[3,6,240]{2,1,0:T(8,128)}, u32[]{:S(2)}) copy-start(f32[3,6,240]{2,1,0:T(8,128)} %param.5) | copy-start | bytes 51844
  0.7 80.4 %copy-start.3 = (s32[6]{0:T(128)S(1)}, s32[6]{0:T(128)}, u32[]{:S(2)}) copy-start(s32[6]{0:T(128)} %param.6) | copy-start | bytes 76
  76.1 83.3 %copy-start = (s32[48]{0:T(128)S(1)}, s32[48]{0:T(128)}, u32[]{:S(2)}) copy-start(s32[48]{0:T(128)} %get-tuple-element.17.plan) | copy-start | bytes 580
  76.1 83.3 %copy-start.1 = (s32[3]{0:T(128)S(1)}, s32[3]{0:T(128)}, u32[]{:S(2)}) copy-start(s32[3]{0:T(128)} %pad_add_fusion.ids) | copy-start | bytes 40
  76.2 62.4 %collective-permute-start.2 = (bf16[5,720,128]{2,1,0:T(8,128)(2,1)}, bf16[5,720,128]{2,1,0:T(8,128)(2,1)S(1)}, u32[]{:S(2)}, u32[]{:S(2)}) collective-permute-start(bf16[5,720,128]{2,1,0:T(8,128)(2,1)} %get-tuple-element.20), channel_id=1, source_target_pairs={{0,4},{4,8},{8,12},{12,0},{1,5},{5,9},{9,13},{13,1},{2,6},{6,10},{... | collective-permute-start | bytes 2764808 | tf_op jit(solution)/shard_map/ppermute | solution.py:272
  77.8 79.3 %collective-permute-start.5 = (bf16[5,720,128]{2,1,0:T(8,128)(2,1)}, bf16[5,720,128]{2,1,0:T(8,128)(2,1)S(1)}, u32[]{:S(2)}, u32[]{:S(2)}) collective-permute-start(bf16[5,720,128]{2,1,0:T(8,128)(2,1)} %get-tuple-element.23), channel_id=1, source_target_pairs={{0,8},{4,12},{8,0},{12,4},{1,9},{5,13},{9,1},{13,5},{2,10},{6,14},... | collective-permute-start | bytes 2764808 | tf_op jit(solution)/shard_map/ppermute | solution.py:272
  79.1 59.5 %collective-permute-start = (f32[3,6,240]{2,1,0:T(8,128)S(1)}, f32[3,6,240]{2,1,0:T(8,128)S(1)}, u32[]{:S(2)}, u32[]{:S(2)}) collective-permute-start(f32[3,6,240]{2,1,0:T(8,128)S(1)} %copy-done.2), channel_id=1, source_target_pairs={{0,1},{1,0},{2,3},{3,2},{4,5},{5,4},{6,7},{7,6},{8,9},{9,8},{10,11... | collective-permute-start | bytes 51848 | tf_op jit(solution)/shard_map/ppermute | solution.py:267
  79.1 79.7 %collective-permute-start.8 = (bf16[5,720,128]{2,1,0:T(8,128)(2,1)}, bf16[5,720,128]{2,1,0:T(8,128)(2,1)S(1)}, u32[]{:S(2)}, u32[]{:S(2)}) collective-permute-start(bf16[5,720,128]{2,1,0:T(8,128)(2,1)} %get-tuple-element.26), channel_id=1, source_target_pairs={{0,12},{4,0},{8,4},{12,8},{1,13},{5,1},{9,5},{13,9},{2,14},{6,2},{... | collective-permute-start | bytes 2764808 | tf_op jit(solution)/shard_map/ppermute | solution.py:272
  138.5 26.7 %collective-permute-start.3 = (bf16[5,720,128]{2,1,0:T(8,128)(2,1)S(1)}, bf16[5,720,128]{2,1,0:T(8,128)(2,1)}, u32[]{:S(2)}, u32[]{:S(2)}) collective-permute-start(bf16[5,720,128]{2,1,0:T(8,128)(2,1)S(1)} %collective-permute-done.2.other_a), channel_id=1, source_target_pairs={{0,1},{1,0},{2,3},{3,2},{4,5},{5,4},{6,7},{7,6},{8,9},{9,8},{10,11... | collective-permute-start | bytes 2764808 | tf_op jit(solution)/shard_map/ppermute | solution.py:273
  157.1 16.5 %collective-permute-start.6 = (bf16[5,720,128]{2,1,0:T(8,128)(2,1)S(1)}, bf16[5,720,128]{2,1,0:T(8,128)(2,1)}, u32[]{:S(2)}, u32[]{:S(2)}) collective-permute-start(bf16[5,720,128]{2,1,0:T(8,128)(2,1)S(1)} %collective-permute-done.5.other_a), channel_id=1, source_target_pairs={{0,1},{1,0},{2,3},{3,2},{4,5},{5,4},{6,7},{7,6},{8,9},{9,8},{10,11... | collective-permute-start | bytes 2764808 | tf_op jit(solution)/shard_map/ppermute | solution.py:273
  158.8 22.3 %collective-permute-start.9 = (bf16[5,720,128]{2,1,0:T(8,128)(2,1)S(1)}, bf16[5,720,128]{2,1,0:T(8,128)(2,1)S(1)}, u32[]{:S(2)}, u32[]{:S(2)}) collective-permute-start(bf16[5,720,128]{2,1,0:T(8,128)(2,1)S(1)} %collective-permute-done.8.other_a), channel_id=1, source_target_pairs={{0,1},{1,0},{2,3},{3,2},{4,5},{5,4},{6,7},{7,6},{8,9},{9,8},{10,11... | collective-permute-start | bytes 2764808 | tf_op jit(solution)/shard_map/ppermute | solution.py:273
  164.6 22.7 %collective-permute-start.1 = (bf16[5,6,64,128]{3,2,1,0:T(8,128)(2,1)S(1)}, bf16[5,6,64,128]{3,2,1,0:T(8,128)(2,1)S(1)}, u32[]{:S(2)}, u32[]{:S(2)}) collective-permute-start(bf16[5,6,64,128]{3,2,1,0:T(8,128)(2,1)S(1)} %get-tuple-element.19), channel_id=1, source_target_pairs={{0,2},{2,0},{1,3},{3,1},{4,6},{6,4},{5,7},{7,5},{8,10},{10,8},{9,1... | collective-permute-start | bytes 1474568 | tf_op jit(solution)/shard_map/ppermute | solution.py:297
  172.0 17.2 %collective-permute-start.4 = (bf16[5,6,64,128]{3,2,1,0:T(8,128)(2,1)S(1)}, bf16[5,6,64,128]{3,2,1,0:T(8,128)(2,1)S(1)}, u32[]{:S(2)}, u32[]{:S(2)}) collective-permute-start(bf16[5,6,64,128]{3,2,1,0:T(8,128)(2,1)S(1)} %get-tuple-element.22), channel_id=1, source_target_pairs={{0,2},{2,0},{1,3},{3,1},{4,6},{6,4},{5,7},{7,5},{8,10},{10,8},{9,1... | collective-permute-start | bytes 1474568 | tf_op jit(solution)/shard_map/ppermute | solution.py:297
  180.4 19.3 %collective-permute-start.7 = (bf16[5,6,64,128]{3,2,1,0:T(8,128)(2,1)S(1)}, bf16[5,6,64,128]{3,2,1,0:T(8,128)(2,1)S(1)}, u32[]{:S(2)}, u32[]{:S(2)}) collective-permute-start(bf16[5,6,64,128]{3,2,1,0:T(8,128)(2,1)S(1)} %get-tuple-element.25), channel_id=1, source_target_pairs={{0,2},{2,0},{1,3},{3,1},{4,6},{6,4},{5,7},{7,5},{8,10},{10,8},{9,1... | collective-permute-start | bytes 1474568 | tf_op jit(solution)/shard_map/ppermute | solution.py:297
  185.7 24.1 %collective-permute-start.10 = (bf16[5,6,64,128]{3,2,1,0:T(8,128)(2,1)S(1)}, bf16[5,6,64,128]{3,2,1,0:T(8,128)(2,1)S(1)}, u32[]{:S(2)}, u32[]{:S(2)}) collective-permute-start(bf16[5,6,64,128]{3,2,1,0:T(8,128)(2,1)S(1)} %get-tuple-element.28), channel_id=1, source_target_pairs={{0,2},{2,0},{1,3},{3,1},{4,6},{6,4},{5,7},{7,5},{8,10},{10,8},{9,1... | collective-permute-start | bytes 1474568 | tf_op jit(solution)/shard_map/ppermute | solution.py:297

commit v2 on v0

v2 whole, which is shorter than its diff:
```python
import functools
import math

import jax
import jax.numpy as jnp
from jax import lax
from jax.experimental import pallas as pl
from jax.experimental.pallas import tpu as pltpu
from jax.sharding import PartitionSpec as P

BF16 = jnp.bfloat16
F32 = jnp.float32
ANY = pl.BlockSpec(memory_space=pl.ANY)
SMEM = pl.BlockSpec(memory_space=pltpu.SMEM)
VMEM_LIMIT = 60 * 1024 * 1024
LAG_CORE, LAG_MERGE = 2, 3
LIGHT = pl.CostEstimate(flops=1, bytes_accessed=1024, transcendentals=0)


def dft_table(length):
    positions = jnp.arange(length, dtype=jnp.int32)
    product = positions[:, None] * positions[None, :] % length
    angles = product.astype(F32) * (2.0 * math.pi / length)
    cosine = jnp.cos(angles) / math.sqrt(length)
    sine_part = jnp.sin(angles) / math.sqrt(length)
    upper_rows = jnp.concatenate([cosine, -sine_part], axis=1)
    bottom = jnp.concatenate([sine_part, cosine], axis=1)
    return jnp.concatenate([upper_rows, bottom], axis=0).astype(BF16)


def plan_kernel(pools, local_k, cap, ids, partners, plan):
    me = ids[0]
    size = pools * cap
    counts = 3 * size

    def clear(i, carry):
        plan[i] = 0
        return carry

    lax.fori_loop(0, counts + pools, clear, 0, unroll=8)

    def visit(t, tally):
        want = partners[me * local_k + t]
        holder = lax.div(want, local_k)
        shift = lax.rem(me - holder + pools, pools)
        slot = plan[counts + shift]
        plan[shift * cap + slot] = t
        plan[size + shift * cap + slot] = want - holder * local_k
        plan[counts + shift] = slot + 1
        after = []
        for shift in range(1, pools):
            taker = lax.rem(me + shift, pools)
            want = partners[taker * local_k + t]
            slot = tally[shift - 1]
            plan[2 * size + shift * cap + jnp.minimum(slot, cap - 1)] = jnp.where(
                lax.div(want, local_k) == me,
                lax.rem(want, local_k),
                plan[2 * size + shift * cap + jnp.minimum(slot, cap - 1)],
            )
            after.append(slot + (lax.div(want, local_k) == me).astype(jnp.int32))
        return tuple(after)

    lax.fori_loop(0, local_k, visit, (jnp.int32(0),) * (pools - 1), unroll=2)


def make_plan(ids, partners, pools, local_k, cap):
    return pl.pallas_call(
        functools.partial(plan_kernel, pools, local_k, cap),
        out_shape=jax.ShapeDtypeStruct((3 * pools * cap + pools,), jnp.int32),
        in_specs=[SMEM, SMEM],
        out_specs=SMEM,
        name="plan",
    )(ids, partners)


def pick_kernel(plan, ids, source, target):
    target[...] = source[...]


def pick(plan, ids, waves, base, count):
    block = (1,) + waves.shape[1:]
    return pl.pallas_call(
        pick_kernel,
        grid_spec=pltpu.PrefetchScalarGridSpec(
            num_scalar_prefetch=2,
            grid=(count,),
            in_specs=[
                pl.BlockSpec(block, lambda i, plan, ids: (plan[base + i] * 2 + ids[1], 0, 0))
            ],
            out_specs=pl.BlockSpec(block, lambda i, plan, ids: (i, 0, 0)),
        ),
        out_shape=jax.ShapeDtypeStruct((count,) + waves.shape[1:], waves.dtype),
        compiler_params=pltpu.CompilerParams(vmem_limit_bytes=VMEM_LIMIT),
        cost_estimate=LIGHT,
        name="pick",
    )(plan, ids, waves)


def to_real(own, other, table, z_points):
    stacked = 2 * z_points
    bands = own.shape[1]
    parts = [[], [], [], []]
    for c in range(own.shape[0] // stacked):
        rows = slice(c * stacked, (c + 1) * stacked)
        pair = jnp.concatenate([own[rows], other[rows]], axis=1)
        out = jnp.dot(table, pair, preferred_element_type=F32)
        parts[0].append(out[:z_points, :bands])
        parts[1].append(out[z_points:, :bands])
        parts[2].append(out[:z_points, bands:])
        parts[3].append(out[z_points:, bands:])
    return [jnp.concatenate(part, axis=0).astype(BF16) for part in parts]


def couple_kernel(number, first, z_points, scaling, plan, ids, table, pots, own, other, keep, give):
    @pl.when(first + pl.program_id(0) < plan[number])
    def _():
        own_re, own_im, o_re, o_im = to_real(own[0], other[0], table[...], z_points)
        u_re, u_im = own_re.astype(F32), own_im.astype(F32)
        both_o = jnp.concatenate([o_re, o_im], axis=1)
        bands = o_re.shape[1]
        mine = pots.shape[0] // 2
        for j in range(2 * mine):
            p_re, p_im = pots[j, 0], pots[j, 1]
            w_re = (p_re * u_re - p_im * u_im).astype(BF16)
            w_im = (p_re * u_im + p_im * u_re).astype(BF16)
            both = lax.dot_general(
                both_o, jnp.concatenate([w_re, w_im], axis=1),
                (((0,), (0,)), ((), ())), preferred_element_type=F32,
            )
            real = (both[:bands, :bands] + both[bands:, bands:]) * scaling
            imag = (both[:bands, bands:] - both[bands:, :bands]) * scaling
            if j < mine:
                keep[0, 2 * j], keep[0, 2 * j + 1] = real, imag
            else:
                give[0, 2 * (j - mine)] = real.astype(BF16)
                give[0, 2 * (j - mine) + 1] = imag.astype(BF16)


def couple(plan, ids, table, pots, waves, other, chunk, pools, cap, scaling):
    shift, first, count = chunk
    half, bands = waves.shape[1:]
    parts = pots.shape[0]
    base = shift * cap + first
    places = pools * cap + base
    block = (1, half, bands)
    own_block = pl.BlockSpec(block, lambda i, plan, ids: (plan[base + i] * 2 + ids[1], 0, 0))
    if shift == 0:
        other_block = pl.BlockSpec(
            block, lambda i, plan, ids: (plan[places + i] * 2 + ids[1], 0, 0)
        )
    else:
        other_block = pl.BlockSpec(block, lambda i, plan, ids: (i, 0, 0))
    out_block = pl.BlockSpec((1, parts, bands, bands), lambda i, plan, ids: (i, 0, 0, 0))
    return pl.pallas_call(
        functools.partial(
            couple_kernel, 3 * pools * cap + shift, first, table.shape[0] // 2, scaling
        ),
        grid_spec=pltpu.PrefetchScalarGridSpec(
            num_scalar_prefetch=2,
            grid=(count,),
            in_specs=[
                pl.BlockSpec(table.shape, lambda i, plan, ids: (0, 0)),
                pl.BlockSpec(pots.shape, lambda i, plan, ids: (0, 0, 0, 0)),
                own_block, other_block,
            ],
            out_specs=[out_block] * 2,
        ),
        out_shape=[
            jax.ShapeDtypeStruct((count, parts, bands, bands), F32),
            jax.ShapeDtypeStruct((count, parts, bands, bands), BF16),
        ],
        compiler_params=pltpu.CompilerParams(vmem_limit_bytes=VMEM_LIMIT),
        cost_estimate=LIGHT,
        name="couple",
    )(plan, ids, table, pots, waves, other)


def merge_kernel(plan, ids, kept, got, *gives):
    steps = len(gives)
    for i in range(steps):
        gives[i][0] = (kept[0] + got[0].astype(F32)).astype(BF16)


def merge(plan, ids, kept, got, step, groups):
    count, parts, bands, _ = kept.shape
    share = bands // groups
    block = (1, parts, share, bands)
    theirs = pl.BlockSpec(block, lambda i, plan, ids: (i, 0, lax.rem(ids[2] + step, groups), 0))
    return pl.pallas_call(
        merge_kernel,
        grid_spec=pltpu.PrefetchScalarGridSpec(
            num_scalar_prefetch=2,
            grid=(count,),
            in_specs=[theirs, theirs],
            out_specs=[pl.BlockSpec(block, lambda i, plan, ids: (i, 0, 0, 0))],
        ),
        out_shape=[jax.ShapeDtypeStruct((count, parts, share, bands), BF16)],
        compiler_params=pltpu.CompilerParams(vmem_limit_bytes=VMEM_LIMIT),
        cost_estimate=LIGHT,
        name="merge",
    )(plan, ids, kept, got)[0]


def combine_kernel(number, first, length, base, terms, plan, ids, *refs):
    result, stage, sems = refs[-3:]
    summands = refs[-3 - terms : -3]
    slot = pl.program_id(0)
    count = plan[number] - first

    def copy(i):
        return pltpu.make_async_copy(stage.at[i], result.at[plan[base + i]], sems.at[i])

    @pl.when(slot < count)
    def _():
        total = summands[0][0]
        for term in summands[1:]:
            total = total + term[0].astype(F32)
        stage[slot] = total.astype(BF16)
        copy(slot).start()

    @pl.when(slot == length - 1)
    def _():
        for i in range(length):

            @pl.when(i < count)
            def _(i=i):
                copy(i).wait()


def combine(plan, ids, before, kept, got, arrived, local_k, chunk, pools, cap):
    shift, first, length = chunk
    shape = arrived[0].shape[1:]
    block = (1,) + shape
    mine = pl.BlockSpec(block, lambda i, plan, ids: (i, 0, ids[2], 0))
    whole = pl.BlockSpec(block, lambda i, plan, ids: (i, 0, 0, 0))
    terms = [kept, got, *arrived]
    operands = ([] if before is None else [before]) + terms
    return pl.pallas_call(
        functools.partial(
            combine_kernel, 3 * pools * cap + shift, first, length, shift * cap + first,
            len(terms),
        ),
        grid_spec=pltpu.PrefetchScalarGridSpec(
            num_scalar_prefetch=2,
            grid=(length,),
            in_specs=([] if before is None else [ANY]) + [mine] * 2 + [whole] * len(arrived),
            out_specs=ANY,
            scratch_shapes=[
                pltpu.VMEM((length,) + shape, BF16), pltpu.SemaphoreType.DMA((length,)),
            ],
        ),
        out_shape=jax.ShapeDtypeStruct((local_k,) + shape, BF16),
        input_output_aliases={} if before is None else {2: 0},
        compiler_params=pltpu.CompilerParams(vmem_limit_bytes=VMEM_LIMIT),
        cost_estimate=LIGHT,
        name="combine",
    )(plan, ids, *operands)


def body(wavefunctions, potentials, pert_order, partners):
    local_k, columns, stacked, bands = wavefunctions.shape
    z_points = stacked // 2
    pools = lax.axis_size("pool")
    groups = lax.axis_size("ga")
    cores = lax.axis_size("pert")
    my_pool = lax.axis_index("pool")
    my_core = lax.axis_index("pert")
    my_group = lax.axis_index("ga")
    cap = max(2, local_k // pools + 1)
    half = columns // cores
    ids = jnp.stack([my_pool, my_core, my_group]).astype(jnp.int32)
    waves = wavefunctions.reshape(local_k * cores, half * stacked, bands)

    plan = make_plan(ids, partners, pools, local_k, cap)
    swap_cores = [(c, cores - 1 - c) for c in range(cores)]
    per_device = potentials.shape[0]
    chunks = []
    for shift in sorted(range(1, pools), key=lambda d: min(d, pools - d)):
        cuts = [0, cap] if 2 * shift != pools else [0, (cap + 1) // 2, cap]
        chunks += [(shift, lo, hi - lo) for lo, hi in zip(cuts, cuts[1:])]
    landed, gives = [], []
    for shift, first, count in chunks:
        gives.append(pick(plan, ids, waves, 2 * pools * cap + shift * cap + first, count))
    here, potentials, *gives = lax.optimization_barrier((waves, potentials, *gives))
    for (shift, first, count), give in zip(chunks, gives):
        pairs = [(s, (s + shift) % pools) for s in range(pools)]
        landed.append(lax.ppermute(give, "pool", pairs))

    table = dft_table(z_points)
    by_half = potentials.reshape(per_device, cores, half, stacked)
    mine_now = lax.dynamic_index_in_dim(by_half, my_core, 1, keepdims=False)
    theirs_now = lax.dynamic_index_in_dim(by_half, 1 - my_core, 1, keepdims=False)
    other_pots = lax.ppermute(theirs_now, "pert", swap_cores)

    ordered = jnp.roll(pert_order.reshape(cores, per_device), -my_core, axis=0).reshape(-1)
    stored = jnp.where(
        my_core == 0, jnp.stack([mine_now, other_pots]), jnp.stack([other_pots, mine_now])
    ).reshape((cores * per_device,) + mine_now.shape[1:])
    options = jnp.arange(cores * per_device, dtype=jnp.int32)
    chosen = jnp.sum(
        jnp.where(
            (ordered[:, None] == options[None, :])[:, :, None, None], stored[None],
            jnp.zeros((), F32),
        ),
        axis=1,
    ).reshape(cores * per_device, half, 2, z_points)
    pots = jnp.moveaxis(chosen, 2, 1).reshape(cores * per_device, 2, half * z_points, 1)
    pots = jnp.broadcast_to(pots, pots.shape[:3] + (bands,))

    scaling = 1.0 / math.sqrt(columns * groups * z_points)

    result = None
    chunks = [(0, 0, cap)] + chunks
    landed = [here] + landed
    kept, got, terms = [], [], []

    def send_on(i):
        swapped = got[i]
        terms.append([
            lax.ppermute(
                merge(plan, ids, kept[i], swapped, step, groups), "ga",
                [(s, (s + step) % groups) for s in range(groups)],
            )
            for step in range(1, groups)
        ])

    def finish(i, result):
        return combine(
            plan, ids, result, kept[i], got[i], terms[i], local_k, chunks[i], pools, cap
        )

    last = len(chunks) - 1
    for i, chunk in enumerate(chunks):
        arrived = landed[i]
        if i >= 1:
            arrived, kept[i - 1] = lax.optimization_barrier((arrived, kept[i - 1]))
        if i >= LAG_CORE:
            arrived, got[i - LAG_CORE] = lax.optimization_barrier((arrived, got[i - LAG_CORE]))
            send_on(i - LAG_CORE)
        if i >= LAG_MERGE and i - LAG_MERGE < len(terms):
            arrived, terms[i - LAG_MERGE] = lax.optimization_barrier((arrived, terms[i - LAG_MERGE]))
        keep, give = couple(plan, ids, table, pots, waves, arrived, chunk, pools, cap, scaling)
        kept.append(keep)
        got.append(lax.ppermute(give, "pert", swap_cores))
    for i in range(len(terms), len(chunks)):
        send_on(i)
    for i in range(len(chunks)):
        result = finish(i, result)
    share = bands // groups
    return result.reshape(local_k, per_device, 2, share, bands)


def solution(mesh):
    return jax.shard_map(
        body,
        mesh=mesh,
        in_specs=(P("pool", "ga", None, None), P(("pb", "pert"), "ga", None), P(), P("pb")),
        out_specs=P(("pb", "pool"), "pert", None, "ga", None),
        check_vma=False,
    )
```

time: 261 us -> 165 us (0.63)
  waiting for transfers between devices: 158 us -> 32.2 us
  Pallas kernels: 0 us -> 88.8 us
  matrix products: 41.4 us -> 0 us
  other arithmetic: 28.8 us -> 2.18 us
  starting transfers between devices: 6.36 us -> 31.8 us
  between operations: 13.7 us -> 0.26 us
    pallas_call x0 -> x20, Pallas kernels: none -> 88.8 us  [the longest x5 34.5 us: couple(): pl.pallas_call(functools.partial(couple_kernel, 3 * pools * cap + shift,...]
    all_to_all x1 -> x0, waiting for transfers between devices: 81.9 us -> none  [body(): lax.all_to_all(jnp.where(filled[:, :, None, None, None], picked, jnp.zero...]
    reduce_scatter x1 -> x0, waiting for transfers between devices: 76.2 us -> none  [body(): lax.psum_scatter(partial_sums, 'ga', scatter_dimension=3, tiled=True)]
    dot_general x8 -> x0, matrix products: 41.4 us -> none  [the longest x3 17.7 us: couple(): jnp.einsum('kcsm,kcsn->kmn', other_real, weighted, preferred_element_type...]
    ppermute x0 -> x15, waiting for transfers between devices: none -> 32.2 us  [the longest x4 32.2 us: body(): landed.append(lax.ppermute(give, 'pool', pairs))]
    ppermute x0 -> x15, starting transfers between devices: none -> 31.8 us  [the longest x4 25.2 us: body(): landed.append(lax.ppermute(give, 'pool', pairs))]
    another operation x7 -> x3, other arithmetic: 15.6 us -> 1.15 us  [the longest x1 0.62 us: body(): ids = jnp.stack([my_pool, my_core, my_group]).astype(jnp.int32)]
    unnamed x16 -> x34, local copies, waits for them, and re-layouts: 0.04 us -> 7.29 us
  transfers between devices with their start and end apart: 3 -> 15, of which waited for: 2 -> 3; matrix products, arithmetic and copies ran while one was open for 7% -> 2% of each run, Pallas kernels for 0% -> 42%
where the time goes in v2:
time: 165 us
  Pallas kernels  88.8 us (54%)
  waiting for transfers between devices  32.2 us (20%)
  starting transfers between devices  31.8 us (19%)
  local copies, waits for them, and re-layouts  9.76 us (6%)
  other arithmetic  2.18 us (1%)
    pallas_call x5, Pallas kernels, couple(): pl.pallas_call(functools.partial(couple_kernel, 3 * pools * cap + shift,...  34.5 us
    ppermute x4, waiting for transfers between devices, body(): landed.append(lax.ppermute(give, 'pool', pairs))  32.2 us
    ppermute x4, starting transfers between devices, body(): landed.append(lax.ppermute(give, 'pool', pairs))  25.2 us
    pallas_call x5, Pallas kernels, merge(): pl.pallas_call(merge_kernel, grid_spec=pltpu.PrefetchScalarGridSpec(num_s...  19.7 us
    pallas_call x5, Pallas kernels, combine(): pl.pallas_call(functools.partial(combine_kernel, 3 * pools * cap + shift,...  18.4 us
    pallas_call x4, Pallas kernels, pick(): pl.pallas_call(pick_kernel, grid_spec=pltpu.PrefetchScalarGridSpec(num_sc...  14.5 us
    unnamed x34, local copies, waits for them, and re-layouts  7.29 us
    ppermute x5, starting transfers between devices, send_on(): lax.ppermute(merge(plan, ids, kept[i], swapped, step, groups), 'ga', [(s,...  5.55 us
  transfers between devices with their start and end apart: 15, of which 3 were waited for; matrix products, arithmetic and copies ran while one was open for 2% of the time, Pallas kernels for 42%

profile of v2, /device:TPU:0, one launch (start us, length us, event | category | flops | bytes accessed | tf_op | source)
XLA Modules:
  0.0 164.9 jit_solution(10668004418246917801)
XLA Ops:
  0.6 1.8 %plan.1 = s32[64]{0:T(128)} custom-call(s32[3]{0:T(128)} %pad_add_fusion.1.ids, s32[64]{0:T(128)} %partners.1), custom_call_target="tpu_custom_call" | custom-call | tf_op jit(solution)/shard_map/plan/pallas_call | solution.py:67
  2.4 2.4 %pick.7 = bf16[2,720,128]{2,1,0:T(8,128)(2,1)} custom-call(s32[64]{0:T(128)} %plan.1, s32[3]{0:T(128)} %pad_add_fusion.1.ids, bf16[32,720,128]{2,1,0:T(8,128)(2,1)} %bitcast.15), custom_call_target="tpu_custom_call" | custom-call | flops 1 | bytes 1024 | tf_op jit(solution)/shard_map/pick/pallas_call | solution.py:82
  4.8 3.4 %pick.6 = bf16[3,720,128]{2,1,0:T(8,128)(2,1)} custom-call(s32[64]{0:T(128)} %plan.1, s32[3]{0:T(128)} %pad_add_fusion.1.ids, bf16[32,720,128]{2,1,0:T(8,128)(2,1)} %bitcast.16), custom_call_target="tpu_custom_call" | custom-call | flops 1 | bytes 1024 | tf_op jit(solution)/shard_map/pick/pallas_call | solution.py:82
  8.2 4.1 %pick.5 = bf16[5,720,128]{2,1,0:T(8,128)(2,1)} custom-call(s32[64]{0:T(128)} %plan.1, s32[3]{0:T(128)} %pad_add_fusion.1.ids, bf16[32,720,128]{2,1,0:T(8,128)(2,1)} %bitcast.17), custom_call_target="tpu_custom_call" | custom-call | flops 1 | bytes 1024 | tf_op jit(solution)/shard_map/pick/pallas_call | solution.py:82
  12.3 4.6 %pick.4 = bf16[5,720,128]{2,1,0:T(8,128)(2,1)} custom-call(s32[64]{0:T(128)} %plan.1, s32[3]{0:T(128)} %pad_add_fusion.1.ids, bf16[32,720,128]{2,1,0:T(8,128)(2,1)} %bitcast.18), custom_call_target="tpu_custom_call" | custom-call | flops 1 | bytes 1024 | tf_op jit(solution)/shard_map/pick/pallas_call | solution.py:82
  17.5 2.6 %collective-permute-start = (bf16[5,720,128]{2,1,0:T(8,128)(2,1)}, bf16[5,720,128]{2,1,0:T(8,128)(2,1)S(1)}, u32[]{:S(2)}, u32[]{:S(2)}) collective-permute-start(bf16[5,720,128]{2,1,0:T(8,128)(2,1)} %pick.4), channel_id=1, source_target_pairs={{0,4},{4,8},{8,12},{12,0},{1,5},{5,9},{9,13},{13,1},{2,6},{6,10},{... | collective-permute-start | bytes 2764808 | tf_op jit(solution)/shard_map/ppermute | solution.py:287
  22.2 2.0 %broadcast_in_dim.35.pots = f32[6,2,360,128]{3,2,1,0:T(8,128)} broadcast(f32[6,2,360]{2,1,0:T(2,128)S(1)} %broadcast_in_dim.34), dimensions={0,1,2} | broadcast | bytes 2229120 | tf_op jit(solution)/shard_map/broadcast_in_dim | solution.py:308
  24.2 7.7 %couple.5 = (f32[5,6,128,128]{3,2,1,0:T(8,128)}, bf16[5,6,128,128]{3,2,1,0:T(8,128)(2,1)}) custom-call(s32[64]{0:T(128)} %plan.1, s32[3]{0:T(128)} %pad_add_fusion.1.ids, bf16[240,240]{1,0:T(8,128)(2,1)} %maximum_maximum_fusion.table, f32[6,2,360,128]{3,2,1,0:T(8,128)} %broadcast_in_dim.35.pots, bf16[32,720,128]{2,1,0:T(8,128)(2,1)} %bitcast.19, ...), custom_call_target="tpu_custom_call" | custom-call | flops 1 | bytes 1024 | tf_op jit(solution)/shard_map/couple/pallas_call | solution.py:154
  32.1 2.3 %collective-permute-start.2 = (bf16[5,720,128]{2,1,0:T(8,128)(2,1)S(1)}, bf16[5,720,128]{2,1,0:T(8,128)(2,1)S(1)}, u32[]{:S(2)}, u32[]{:S(2)}) collective-permute-start(bf16[5,720,128]{2,1,0:T(8,128)(2,1)S(1)} %copy-done.5), channel_id=1, source_target_pairs={{0,12},{4,0},{8,4},{12,8},{1,13},{5,1},{9,5},{13,9},{2,14},{6,2},{... | collective-permute-start | bytes 2764808 | tf_op jit(solution)/shard_map/ppermute | solution.py:287
  34.4 9.3 %collective-permute-done.other = bf16[5,720,128]{2,1,0:T(8,128)(2,1)S(1)} collective-permute-done((bf16[5,720,128]{2,1,0:T(8,128)(2,1)}, bf16[5,720,128]{2,1,0:T(8,128)(2,1)S(1)}, u32[]{:S(2)}, u32[]{:S(2)}) %collective-permute-start) | collective-permute-done | bytes 921632 | tf_op jit(solution)/shard_map/ppermute | solution.py:287
  44.6 7.6 %couple.6 = (f32[5,6,128,128]{3,2,1,0:T(8,128)}, bf16[5,6,128,128]{3,2,1,0:T(8,128)(2,1)}) custom-call(s32[64]{0:T(128)} %plan.1, s32[3]{0:T(128)} %pad_add_fusion.1.ids, bf16[240,240]{1,0:T(8,128)(2,1)} %maximum_maximum_fusion.table, f32[6,2,360,128]{3,2,1,0:T(8,128)} %broadcast_in_dim.35.pots, bf16[32,720,128]{2,1,0:T(8,128)(2,1)} %bitcast.21, ...), custom_call_target="tpu_custom_call" | custom-call | flops 1 | bytes 1024 | tf_op jit(solution)/shard_map/couple/pallas_call | solution.py:154
  52.2 20.3 %collective-permute-start.4 = (bf16[3,720,128]{2,1,0:T(8,128)(2,1)}, bf16[3,720,128]{2,1,0:T(8,128)(2,1)}, u32[]{:S(2)}, u32[]{:S(2)}) collective-permute-start(bf16[3,720,128]{2,1,0:T(8,128)(2,1)} %pick.6), channel_id=1, source_target_pairs={{0,8},{4,12},{8,0},{12,4},{1,9},{5,13},{9,1},{13,5},{2,10},{6,14},... | collective-permute-start | bytes 1658888 | tf_op jit(solution)/shard_map/ppermute | solution.py:287
  72.5 0.9 copy-done.7
  73.4 7.6 %couple.7 = (f32[5,6,128,128]{3,2,1,0:T(8,128)}, bf16[5,6,128,128]{3,2,1,0:T(8,128)(2,1)}) custom-call(s32[64]{0:T(128)} %plan.1, s32[3]{0:T(128)} %pad_add_fusion.1.ids, bf16[240,240]{1,0:T(8,128)(2,1)} %maximum_maximum_fusion.table, f32[6,2,360,128]{3,2,1,0:T(8,128)} %broadcast_in_dim.35.pots, bf16[32,720,128]{2,1,0:T(8,128)(2,1)} %bitcast.22, ...), custom_call_target="tpu_custom_call" | custom-call | flops 1 | bytes 1024 | tf_op jit(solution)/shard_map/couple/pallas_call | solution.py:154
  81.2 4.6 %merge.5 = bf16[5,6,64,128]{3,2,1,0:T(8,128)(2,1)} custom-call(s32[64]{0:T(128)} %plan.1, s32[3]{0:T(128)} %pad_add_fusion.1.ids, f32[5,6,128,128]{3,2,1,0:T(8,128)} %get-tuple-element.43.kept.refs_0_, bf16[5,6,128,128]{3,2,1,0:T(8,128)(2,1)} %copy-done), custom_call_target="tpu_custom_call" | custom-call | flops 1 | bytes 1024 | tf_op jit(solution)/shard_map/merge/pallas_call | solution.py:189
  85.8 1.5 collective-permute-start.6
  87.3 10.5 %collective-permute-done.4.other = bf16[3,720,128]{2,1,0:T(8,128)(2,1)} collective-permute-done((bf16[3,720,128]{2,1,0:T(8,128)(2,1)}, bf16[3,720,128]{2,1,0:T(8,128)(2,1)}, u32[]{:S(2)}, u32[]{:S(2)}) %collective-permute-start.4) | collective-permute-done | bytes 552992 | tf_op jit(solution)/shard_map/ppermute | solution.py:287
  97.8 0.9 copy-done.1
  98.7 4.6 %merge.6 = bf16[5,6,64,128]{3,2,1,0:T(8,128)(2,1)} custom-call(s32[64]{0:T(128)} %plan.1, s32[3]{0:T(128)} %pad_add_fusion.1.ids, f32[5,6,128,128]{3,2,1,0:T(8,128)} %get-tuple-element.57.kept.refs_1_, bf16[5,6,128,128]{3,2,1,0:T(8,128)(2,1)} %copy-done.1), custom_call_target="tpu_custom_call" | custom-call | flops 1 | bytes 1024 | tf_op jit(solution)/shard_map/merge/pallas_call | solution.py:189
  103.3 1.5 collective-permute-start.9
  104.8 6.4 %couple.8 = (f32[3,6,128,128]{3,2,1,0:T(8,128)}, bf16[3,6,128,128]{3,2,1,0:T(8,128)(2,1)}) custom-call(s32[64]{0:T(128)} %plan.1, s32[3]{0:T(128)} %pad_add_fusion.1.ids, bf16[240,240]{1,0:T(8,128)(2,1)} %maximum_maximum_fusion.table, f32[6,2,360,128]{3,2,1,0:T(8,128)} %broadcast_in_dim.35.pots, bf16[32,720,128]{2,1,0:T(8,128)(2,1)} %bitcast.23, ...), custom_call_target="tpu_custom_call" | custom-call | flops 1 | bytes 1024 | tf_op jit(solution)/shard_map/couple/pallas_call | solution.py:154
  111.2 12.4 %collective-permute-done.7.other = bf16[2,720,128]{2,1,0:T(8,128)(2,1)S(1)} collective-permute-done((bf16[2,720,128]{2,1,0:T(8,128)(2,1)S(1)}, bf16[2,720,128]{2,1,0:T(8,128)(2,1)S(1)}, u32[]{:S(2)}, u32[]{:S(2)}) %collective-permute-start.7) | collective-permute-done | bytes 368672 | tf_op jit(solution)/shard_map/ppermute | solution.py:287
  124.4 5.2 %couple.9 = (f32[2,6,128,128]{3,2,1,0:T(8,128)}, bf16[2,6,128,128]{3,2,1,0:T(8,128)(2,1)}) custom-call(s32[64]{0:T(128)} %plan.1, s32[3]{0:T(128)} %pad_add_fusion.1.ids, bf16[240,240]{1,0:T(8,128)(2,1)} %maximum_maximum_fusion.table, f32[6,2,360,128]{3,2,1,0:T(8,128)} %broadcast_in_dim.35.pots, bf16[32,720,128]{2,1,0:T(8,128)(2,1)} %bitcast.24, ...), custom_call_target="tpu_custom_call" | custom-call | flops 1 | bytes 1024 | tf_op jit(solution)/shard_map/couple/pallas_call | solution.py:154
  129.7 4.6 %merge.7 = bf16[5,6,64,128]{3,2,1,0:T(8,128)(2,1)} custom-call(s32[64]{0:T(128)} %plan.1, s32[3]{0:T(128)} %pad_add_fusion.1.ids, f32[5,6,128,128]{3,2,1,0:T(8,128)} %get-tuple-element.66.kept.refs_1_, bf16[5,6,128,128]{3,2,1,0:T(8,128)(2,1)} %copy-done.2), custom_call_target="tpu_custom_call" | custom-call | flops 1 | bytes 1024 | tf_op jit(solution)/shard_map/merge/pallas_call | solution.py:189
  135.6 3.5 %merge.8 = bf16[3,6,64,128]{3,2,1,0:T(8,128)(2,1)} custom-call(s32[64]{0:T(128)} %plan.1, s32[3]{0:T(128)} %pad_add_fusion.1.ids, f32[3,6,128,128]{3,2,1,0:T(8,128)} %get-tuple-element.68.kept.refs_1_, bf16[3,6,128,128]{3,2,1,0:T(8,128)(2,1)} %copy-done.3), custom_call_target="tpu_custom_call" | custom-call | flops 1 | bytes 1024 | tf_op jit(solution)/shard_map/merge/pallas_call | solution.py:189
  139.0 1.5 collective-permute-start.12
  141.3 2.5 %merge.9 = bf16[2,6,64,128]{3,2,1,0:T(8,128)(2,1)} custom-call(s32[64]{0:T(128)} %plan.1, s32[3]{0:T(128)} %pad_add_fusion.1.ids, f32[2,6,128,128]{3,2,1,0:T(8,128)} %get-tuple-element.71.kept.refs_1_, bf16[2,6,128,128]{3,2,1,0:T(8,128)(2,1)} %copy-done.4), custom_call_target="tpu_custom_call" | custom-call | flops 1 | bytes 1024 | tf_op jit(solution)/shard_map/merge/pallas_call | solution.py:189
  144.3 4.1 %combine.5.refs_0_ = bf16[16,6,64,128]{3,2,1,0:T(8,128)(2,1)} custom-call(s32[64]{0:T(128)} %plan.1, s32[3]{0:T(128)} %pad_add_fusion.1.ids, f32[5,6,128,128]{3,2,1,0:T(8,128)} %get-tuple-element.43.kept.refs_0_, bf16[5,6,128,128]{3,2,1,0:T(8,128)(2,1)} %copy-done, bf16[5,6,64,128]{3,2,1,0:T(8,128)(2,1)} %copy-done.8), custom_call_target="tpu_custom_call" | custom-call | flops 1 | bytes 1024 | tf_op jit(solution)/shard_map/combine/pallas_call | solution.py:238
  148.4 4.1 %combine.6.refs_0_ = bf16[16,6,64,128]{3,2,1,0:T(8,128)(2,1)} custom-call(s32[64]{0:T(128)} %plan.1, s32[3]{0:T(128)} %pad_add_fusion.1.ids, bf16[16,6,64,128]{3,2,1,0:T(8,128)(2,1)} %combine.5.refs_0_, f32[5,6,128,128]{3,2,1,0:T(8,128)} %get-tuple-element.57.kept.refs_1_, bf16[5,6,128,128]{3,2,1,0:T(8,128)(2,1)} %copy-done.1, ...), custom_call_target="tpu_custom_call", output_to_operand_aliasing={{}: (2, {})} | custom-call | flops 1 | bytes 1024 | tf_op jit(solution)/shard_map/combine/pallas_call | solution.py:238
  153.3 4.1 %combine.7.refs_0_ = bf16[16,6,64,128]{3,2,1,0:T(8,128)(2,1)} custom-call(s32[64]{0:T(128)} %plan.1, s32[3]{0:T(128)} %pad_add_fusion.1.ids, bf16[16,6,64,128]{3,2,1,0:T(8,128)(2,1)} %combine.6.refs_0_, f32[5,6,128,128]{3,2,1,0:T(8,128)} %get-tuple-element.66.kept.refs_1_, bf16[5,6,128,128]{3,2,1,0:T(8,128)(2,1)} %copy-done.2, ...), custom_call_target="tpu_custom_call", output_to_operand_aliasing={{}: (2, {})} | custom-call | flops 1 | bytes 1024 | tf_op jit(solution)/shard_map/combine/pallas_call | solution.py:238
  158.1 3.6 %combine.8.refs_0_ = bf16[16,6,64,128]{3,2,1,0:T(8,128)(2,1)} custom-call(s32[64]{0:T(128)} %plan.1, s32[3]{0:T(128)} %pad_add_fusion.1.ids, bf16[16,6,64,128]{3,2,1,0:T(8,128)(2,1)} %combine.7.refs_0_, f32[3,6,128,128]{3,2,1,0:T(8,128)} %get-tuple-element.68.kept.refs_1_, bf16[3,6,128,128]{3,2,1,0:T(8,128)(2,1)} %copy-done.3, ...), custom_call_target="tpu_custom_call", output_to_operand_aliasing={{}: (2, {})} | custom-call | flops 1 | bytes 1024 | tf_op jit(solution)/shard_map/combine/pallas_call | solution.py:238
  162.3 2.6 %combine.9 = bf16[16,6,64,128]{3,2,1,0:T(8,128)(2,1)} custom-call(s32[64]{0:T(128)} %plan.1, s32[3]{0:T(128)} %pad_add_fusion.1.ids, bf16[16,6,64,128]{3,2,1,0:T(8,128)(2,1)} %combine.8.refs_0_, f32[2,6,128,128]{3,2,1,0:T(8,128)} %get-tuple-element.71.kept.refs_1_, bf16[2,6,128,128]{3,2,1,0:T(8,128)(2,1)} %copy-done.4, ...), custom_call_target="tpu_custom_call", output_to_operand_aliasing={{}: (2, {})} | custom-call | flops 1 | bytes 1024 | tf_op jit(solution)/shard_map/combine/pallas_call | solution.py:238
  (74 shorter events, 10.2 us)
Async XLA Ops:
  12.3 4.6 %copy-start.15 = (f32[3,6,240]{2,1,0:T(8,128)S(1)}, f32[3,6,240]{2,1,0:T(8,128)}, u32[]{:S(2)}) copy-start(f32[3,6,240]{2,1,0:T(8,128)} %param.5) | copy-start | bytes 51844
  12.3 8.1 %copy-start.16 = (s32[6]{0:T(128)S(1)}, s32[6]{0:T(128)}, u32[]{:S(2)}) copy-start(s32[6]{0:T(128)} %param.6) | copy-start | bytes 76
  17.0 4.8 %collective-permute-start.1 = (f32[3,3,240]{2,1,0:T(4,128)S(1)}, f32[3,3,240]{2,1,0:T(4,128)S(1)}, u32[]{:S(2)}, u32[]{:S(2)}) collective-permute-start(f32[3,3,240]{2,1,0:T(4,128)S(1)} %bitcast.29), channel_id=1, source_target_pairs={{0,1},{1,0},{2,3},{3,2},{4,5},{5,4},{6,7},{7,6},{8,9},{9,8},{10,11... | collective-permute-start | bytes 25928 | tf_op jit(solution)/shard_map/ppermute | solution.py:293
  17.5 26.2 %collective-permute-start = (bf16[5,720,128]{2,1,0:T(8,128)(2,1)}, bf16[5,720,128]{2,1,0:T(8,128)(2,1)S(1)}, u32[]{:S(2)}, u32[]{:S(2)}) collective-permute-start(bf16[5,720,128]{2,1,0:T(8,128)(2,1)} %pick.4), channel_id=1, source_target_pairs={{0,4},{4,8},{8,12},{12,0},{1,5},{5,9},{9,13},{13,1},{2,6},{6,10},{... | collective-permute-start | bytes 2764808 | tf_op jit(solution)/shard_map/ppermute | solution.py:287
  24.2 7.9 %copy-start.5 = (bf16[5,720,128]{2,1,0:T(8,128)(2,1)S(1)}, bf16[5,720,128]{2,1,0:T(8,128)(2,1)}, u32[]{:S(2)}) copy-start(bf16[5,720,128]{2,1,0:T(8,128)(2,1)} %pick.5) | copy-start | bytes 2764804
  31.9 40.5 %collective-permute-start.3 = (bf16[5,6,128,128]{3,2,1,0:T(8,128)(2,1)}, bf16[5,6,128,128]{3,2,1,0:T(8,128)(2,1)S(1)}, u32[]{:S(2)}, u32[]{:S(2)}) collective-permute-start(bf16[5,6,128,128]{3,2,1,0:T(8,128)(2,1)} %get-tuple-element.48), channel_id=1, source_target_pairs={{0,1},{1,0},{2,3},{3,2},{4,5},{5,4},{6,7},{7,6},{8,9},{9,8},{10,11... | collective-permute-start | bytes 2949128 | tf_op jit(solution)/shard_map/ppermute | solution.py:344
  32.1 40.3 %collective-permute-start.2 = (bf16[5,720,128]{2,1,0:T(8,128)(2,1)S(1)}, bf16[5,720,128]{2,1,0:T(8,128)(2,1)S(1)}, u32[]{:S(2)}, u32[]{:S(2)}) collective-permute-start(bf16[5,720,128]{2,1,0:T(8,128)(2,1)S(1)} %copy-done.5), channel_id=1, source_target_pairs={{0,12},{4,0},{8,4},{12,8},{1,13},{5,1},{9,5},{13,9},{2,14},{6,2},{... | collective-permute-start | bytes 2764808 | tf_op jit(solution)/shard_map/ppermute | solution.py:287
  43.7 0.9 copy-start.6
  52.2 45.6 %collective-permute-start.5 = (bf16[5,6,128,128]{3,2,1,0:T(8,128)(2,1)}, bf16[5,6,128,128]{3,2,1,0:T(8,128)(2,1)S(1)}, u32[]{:S(2)}, u32[]{:S(2)}) collective-permute-start(bf16[5,6,128,128]{3,2,1,0:T(8,128)(2,1)} %get-tuple-element.54), channel_id=1, source_target_pairs={{0,1},{1,0},{2,3},{3,2},{4,5},{5,4},{6,7},{7,6},{8,9},{9,8},{10,11... | collective-permute-start | bytes 2949128 | tf_op jit(solution)/shard_map/ppermute | solution.py:344
  52.2 45.6 %collective-permute-start.4 = (bf16[3,720,128]{2,1,0:T(8,128)(2,1)}, bf16[3,720,128]{2,1,0:T(8,128)(2,1)}, u32[]{:S(2)}, u32[]{:S(2)}) collective-permute-start(bf16[3,720,128]{2,1,0:T(8,128)(2,1)} %pick.6), channel_id=1, source_target_pairs={{0,8},{4,12},{8,0},{12,4},{1,9},{5,13},{9,1},{13,5},{2,10},{6,14},... | collective-permute-start | bytes 1658888 | tf_op jit(solution)/shard_map/ppermute | solution.py:287
  72.5 0.9 copy-start.7
  73.4 7.6 %copy-start = (bf16[5,6,128,128]{3,2,1,0:T(8,128)(2,1)}, bf16[5,6,128,128]{3,2,1,0:T(8,128)(2,1)S(1)}, u32[]{:S(2)}) copy-start(bf16[5,6,128,128]{3,2,1,0:T(8,128)(2,1)S(1)} %collective-permute-done.3.got.refs_1_) | copy-start | bytes 2949124
  81.0 42.6 %collective-permute-start.8 = (bf16[5,6,128,128]{3,2,1,0:T(8,128)(2,1)}, bf16[5,6,128,128]{3,2,1,0:T(8,128)(2,1)S(1)}, u32[]{:S(2)}, u32[]{:S(2)}) collective-permute-start(bf16[5,6,128,128]{3,2,1,0:T(8,128)(2,1)} %get-tuple-element.63), channel_id=1, source_target_pairs={{0,1},{1,0},{2,3},{3,2},{4,5},{5,4},{6,7},{7,6},{8,9},{9,8},{10,11... | collective-permute-start | bytes 2949128 | tf_op jit(solution)/shard_map/ppermute | solution.py:344
  85.8 19.0 %collective-permute-start.6 = (bf16[5,6,64,128]{3,2,1,0:T(8,128)(2,1)}, bf16[5,6,64,128]{3,2,1,0:T(8,128)(2,1)S(1)}, u32[]{:S(2)}, u32[]{:S(2)}) collective-permute-start(bf16[5,6,64,128]{3,2,1,0:T(8,128)(2,1)} %merge.5), channel_id=1, source_target_pairs={{0,2},{2,0},{1,3},{3,1},{4,6},{6,4},{5,7},{7,5},{8,10},{10,8},{9,1... | collective-permute-start | bytes 1474568 | tf_op jit(solution)/shard_map/ppermute | solution.py:320
  97.8 7.0 %copy-start.11 = (bf16[2,720,128]{2,1,0:T(8,128)(2,1)S(1)}, bf16[2,720,128]{2,1,0:T(8,128)(2,1)}, u32[]{:S(2)}) copy-start(bf16[2,720,128]{2,1,0:T(8,128)(2,1)} %pick.7) | copy-start | bytes 1105924
  97.8 1.0 copy-start.1
  103.3 20.4 %collective-permute-start.9 = (bf16[5,6,64,128]{3,2,1,0:T(8,128)(2,1)}, bf16[5,6,64,128]{3,2,1,0:T(8,128)(2,1)S(1)}, u32[]{:S(2)}, u32[]{:S(2)}) collective-permute-start(bf16[5,6,64,128]{3,2,1,0:T(8,128)(2,1)} %merge.6), channel_id=1, source_target_pairs={{0,2},{2,0},{1,3},{3,1},{4,6},{6,4},{5,7},{7,5},{8,10},{10,8},{9,1... | collective-permute-start | bytes 1474568 | tf_op jit(solution)/shard_map/ppermute | solution.py:320
  104.8 18.9 %collective-permute-start.7 = (bf16[2,720,128]{2,1,0:T(8,128)(2,1)S(1)}, bf16[2,720,128]{2,1,0:T(8,128)(2,1)S(1)}, u32[]{:S(2)}, u32[]{:S(2)}) collective-permute-start(bf16[2,720,128]{2,1,0:T(8,128)(2,1)S(1)} %copy-done.11), channel_id=1, source_target_pairs={{0,8},{4,12},{8,0},{12,4},{1,9},{5,13},{9,1},{13,5},{2,10},{6,14},... | collective-permute-start | bytes 1105928 | tf_op jit(solution)/shard_map/ppermute | solution.py:287
  104.8 6.4 %copy-start.8 = (bf16[5,6,64,128]{3,2,1,0:T(8,128)(2,1)}, bf16[5,6,64,128]{3,2,1,0:T(8,128)(2,1)S(1)}, u32[]{:S(2)}) copy-start(bf16[5,6,64,128]{3,2,1,0:T(8,128)(2,1)S(1)} %collective-permute-done.6.refs_2_) | copy-start | bytes 1474564
  111.2 23.6 %collective-permute-start.11 = (bf16[3,6,128,128]{3,2,1,0:T(8,128)(2,1)}, bf16[3,6,128,128]{3,2,1,0:T(8,128)(2,1)S(1)}, u32[]{:S(2)}, u32[]{:S(2)}) collective-permute-start(bf16[3,6,128,128]{3,2,1,0:T(8,128)(2,1)} %get-tuple-element.69), channel_id=1, source_target_pairs={{0,1},{1,0},{2,3},{3,2},{4,5},{5,4},{6,7},{7,6},{8,9},{9,8},{10,11... | collective-permute-start | bytes 1769480 | tf_op jit(solution)/shard_map/ppermute | solution.py:344
  123.7 0.7 copy-start.12
  123.7 5.9 %copy-start.2 = (bf16[5,6,128,128]{3,2,1,0:T(8,128)(2,1)}, bf16[5,6,128,128]{3,2,1,0:T(8,128)(2,1)S(1)}, u32[]{:S(2)}) copy-start(bf16[5,6,128,128]{3,2,1,0:T(8,128)(2,1)S(1)} %collective-permute-done.8.got.refs_2_) | copy-start | bytes 2949124
  124.4 5.2 %copy-start.9 = (bf16[5,6,64,128]{3,2,1,0:T(8,128)(2,1)}, bf16[5,6,64,128]{3,2,1,0:T(8,128)(2,1)S(1)}, u32[]{:S(2)}) copy-start(bf16[5,6,64,128]{3,2,1,0:T(8,128)(2,1)S(1)} %collective-permute-done.9.refs_3_) | copy-start | bytes 1474564
  129.6 11.0 %collective-permute-start.13 = (bf16[2,6,128,128]{3,2,1,0:T(8,128)(2,1)}, bf16[2,6,128,128]{3,2,1,0:T(8,128)(2,1)S(1)}, u32[]{:S(2)}, u32[]{:S(2)}) collective-permute-start(bf16[2,6,128,128]{3,2,1,0:T(8,128)(2,1)} %get-tuple-element.72), channel_id=1, source_target_pairs={{0,1},{1,0},{2,3},{3,2},{4,5},{5,4},{6,7},{7,6},{8,9},{9,8},{10,11... | collective-permute-start | bytes 1179656 | tf_op jit(solution)/shard_map/ppermute | solution.py:344
  134.2 18.2 %collective-permute-start.10 = (bf16[5,6,64,128]{3,2,1,0:T(8,128)(2,1)}, bf16[5,6,64,128]{3,2,1,0:T(8,128)(2,1)S(1)}, u32[]{:S(2)}, u32[]{:S(2)}) collective-permute-start(bf16[5,6,64,128]{3,2,1,0:T(8,128)(2,1)} %merge.7), channel_id=1, source_target_pairs={{0,2},{2,0},{1,3},{3,1},{4,6},{6,4},{5,7},{7,5},{8,10},{10,8},{9,1... | collective-permute-start | bytes 1474568 | tf_op jit(solution)/shard_map/ppermute | solution.py:320
  134.8 0.8 copy-start.3
  139.0 18.3 %collective-permute-start.12 = (bf16[3,6,64,128]{3,2,1,0:T(8,128)(2,1)}, bf16[3,6,64,128]{3,2,1,0:T(8,128)(2,1)S(1)}, u32[]{:S(2)}, u32[]{:S(2)}) collective-permute-start(bf16[3,6,64,128]{3,2,1,0:T(8,128)(2,1)} %merge.8), channel_id=1, source_target_pairs={{0,2},{2,0},{1,3},{3,1},{4,6},{6,4},{5,7},{7,5},{8,10},{10,8},{9,1... | collective-permute-start | bytes 884744 | tf_op jit(solution)/shard_map/ppermute | solution.py:320
  140.5 0.7 copy-start.4
  143.8 17.9 %collective-permute-start.14 = (bf16[2,6,64,128]{3,2,1,0:T(8,128)(2,1)}, bf16[2,6,64,128]{3,2,1,0:T(8,128)(2,1)S(1)}, u32[]{:S(2)}, u32[]{:S(2)}) collective-permute-start(bf16[2,6,64,128]{3,2,1,0:T(8,128)(2,1)} %merge.9), channel_id=1, source_target_pairs={{0,2},{2,0},{1,3},{3,1},{4,6},{6,4},{5,7},{7,5},{8,10},{10,8},{9,1... | collective-permute-start | bytes 589832 | tf_op jit(solution)/shard_map/ppermute | solution.py:320
  152.5 0.8 copy-start.10
  157.4 0.7 copy-start.13
  161.7 0.7 copy-start.14

commit v3 on v2

v3 whole, which is shorter than its diff:
```python
import functools
import math

import jax
import jax.numpy as jnp
from jax import lax
from jax.experimental import pallas as pl
from jax.experimental.pallas import tpu as pltpu
from jax.sharding import PartitionSpec as P

BF16 = jnp.bfloat16
F32 = jnp.float32
ANY = pl.BlockSpec(memory_space=pl.ANY)
SMEM = pl.BlockSpec(memory_space=pltpu.SMEM)
VMEM_LIMIT = 60 * 1024 * 1024
LIGHT = pl.CostEstimate(flops=1, bytes_accessed=1024, transcendentals=0)
PARAMS = pltpu.CompilerParams(vmem_limit_bytes=VMEM_LIMIT)


def dft_table(length):
    positions = jnp.arange(length, dtype=jnp.int32)
    product = positions[:, None] * positions[None, :] % length
    angles = product.astype(F32) * (2.0 * math.pi / length)
    cosine = jnp.cos(angles) / math.sqrt(length)
    sine_part = jnp.sin(angles) / math.sqrt(length)
    upper_rows = jnp.concatenate([cosine, -sine_part], axis=1)
    bottom = jnp.concatenate([sine_part, cosine], axis=1)
    return jnp.concatenate([upper_rows, bottom], axis=0).astype(BF16)


def plan_kernel(pools, local_k, cap, ids, partners, plan):
    me = ids[0]
    size = pools * cap
    counts = 3 * size

    def clear(i, carry):
        plan[i] = 0
        return carry

    lax.fori_loop(0, counts + pools, clear, 0, unroll=8)

    def visit(t, tally):
        want = partners[me * local_k + t]
        holder = lax.div(want, local_k)
        shift = lax.rem(me - holder + pools, pools)
        slot = plan[counts + shift]
        plan[shift * cap + slot] = t
        plan[size + shift * cap + slot] = want - holder * local_k
        plan[counts + shift] = slot + 1
        after = []
        for shift in range(1, pools):
            taker = lax.rem(me + shift, pools)
            want = partners[taker * local_k + t]
            slot = tally[shift - 1]
            mine = lax.div(want, local_k) == me
            entry = 2 * size + shift * cap + jnp.minimum(slot, cap - 1)
            plan[entry] = jnp.where(mine, lax.rem(want, local_k), plan[entry])
            after.append(slot + mine.astype(jnp.int32))
        return tuple(after)

    lax.fori_loop(0, local_k, visit, (jnp.int32(0),) * (pools - 1), unroll=2)


def make_plan(ids, partners, pools, local_k, cap):
    return pl.pallas_call(
        functools.partial(plan_kernel, pools, local_k, cap),
        out_shape=jax.ShapeDtypeStruct((3 * pools * cap + pools,), jnp.int32),
        in_specs=[SMEM, SMEM],
        out_specs=SMEM,
        cost_estimate=LIGHT,
        name="plan",
    )(ids, partners)


def pick_kernel(base, cap, count, pools, plan, ids, waves, give, sems):
    copies = []
    for shift in range(1, pools):
        taker = lax.rem(ids[0] + shift, pools)
        for i in range(count):
            place = plan[base + shift * cap + i] * 2 + ids[1]
            copies.append(
                pltpu.make_async_copy(waves.at[place], give.at[taker, i], sems.at[shift - 1, i])
            )
    for copy in copies:
        copy.start()
    for copy in copies:
        copy.wait()


def pick(plan, ids, waves, pools, cap, first, count):
    return pl.pallas_call(
        functools.partial(pick_kernel, 2 * pools * cap + first, cap, count, pools),
        out_shape=jax.ShapeDtypeStruct((pools, count) + waves.shape[1:], waves.dtype),
        in_specs=[SMEM, SMEM, ANY],
        out_specs=pl.BlockSpec(memory_space=pltpu.VMEM),
        scratch_shapes=[pltpu.SemaphoreType.DMA((pools - 1, count))],
        compiler_params=PARAMS,
        cost_estimate=LIGHT,
        name="pick",
    )(plan, ids, waves)


def to_real(own, other, table, z_points):
    stacked = 2 * z_points
    bands = own.shape[1]
    parts = [[], [], [], []]
    for c in range(own.shape[0] // stacked):
        rows = slice(c * stacked, (c + 1) * stacked)
        pair = jnp.concatenate([own[rows], other[rows]], axis=1)
        out = jnp.dot(table, pair, preferred_element_type=F32)
        parts[0].append(out[:z_points, :bands])
        parts[1].append(out[z_points:, :bands])
        parts[2].append(out[:z_points, bands:])
        parts[3].append(out[z_points:, bands:])
    return [jnp.concatenate(part, axis=0).astype(BF16) for part in parts]


def couple_kernel(shape, plan, ids, table, pots, own, *rest):
    counts, cap, shift, first, count, groups, z_points = shape
    other, keep, give = rest
    i = pl.program_id(0)
    source = i // count

    @pl.when(first + i - source * count < plan[counts + shift + source])
    def _():
        own_re, own_im, o_re, o_im = to_real(
            own[0], other[...].reshape(own.shape[1:]), table[...], z_points
        )
        u_re, u_im = own_re.astype(F32), own_im.astype(F32)
        both_o = jnp.concatenate([o_re, o_im], axis=1).T
        bands = o_re.shape[1]
        share = bands // groups
        mine = pots.shape[0] // 2
        starts = [
            pl.multiple_of(lax.rem(g - ids[2] + groups, groups) * share, share)
            for g in range(groups)
        ]
        for j in range(2 * mine):
            p_re, p_im = pots[j, 0], pots[j, 1]
            w_re = (p_re * u_re - p_im * u_im).astype(BF16)
            w_im = (p_re * u_im + p_im * u_re).astype(BF16)
            both = jnp.dot(
                both_o, jnp.concatenate([w_re, w_im], axis=1), preferred_element_type=F32
            )
            real = both[:bands, :bands] + both[bands:, bands:]
            imag = both[:bands, bands:] - both[bands:, :bands]
            for part, value in ((0, real), (1, imag)):
                for g in range(groups):
                    rows = value[g * share : (g + 1) * share]
                    if j < mine:
                        keep[0, 2 * j + part, pl.ds(starts[g], share), :] = rows
                    else:
                        place = 2 * (j - mine) + part
                        give[0, place, pl.ds(starts[g], share), :] = rows.astype(BF16)


def couple(plan, ids, table, pots, waves, other, chunk, pools, cap, groups):
    shift, first, count = chunk
    half, bands = waves.shape[1:]
    parts = pots.shape[0]
    sources = 1 if shift == 0 else pools - 1
    block = (1, half, bands)

    def entry(i):
        return (shift + i // count) * cap + first + i % count

    own_block = pl.BlockSpec(block, lambda i, plan, ids: (plan[entry(i)] * 2 + ids[1], 0, 0))
    if shift == 0:
        other_block = pl.BlockSpec(
            block, lambda i, plan, ids: (plan[pools * cap + entry(i)] * 2 + ids[1], 0, 0)
        )
    else:
        other_block = pl.BlockSpec(
            (1,) + block,
            lambda i, plan, ids: (
                lax.rem(ids[0] - shift - i // count + pools, pools), i % count, 0, 0
            ),
        )
    out_block = pl.BlockSpec((1, parts, bands, bands), lambda i, plan, ids: (i, 0, 0, 0))
    shape = (3 * pools * cap, cap, shift, first, count, groups, table.shape[0] // 2)
    total = sources * count
    return pl.pallas_call(
        functools.partial(couple_kernel, shape),
        grid_spec=pltpu.PrefetchScalarGridSpec(
            num_scalar_prefetch=2,
            grid=(total,),
            in_specs=[
                pl.BlockSpec(table.shape, lambda i, plan, ids: (0, 0)),
                pl.BlockSpec(pots.shape, lambda i, plan, ids: (0, 0, 0, 0)),
                own_block, other_block,
            ],
            out_specs=[out_block] * 2,
        ),
        out_shape=[
            jax.ShapeDtypeStruct((total, parts, bands, bands), F32),
            jax.ShapeDtypeStruct((total, parts, bands, bands), BF16),
        ],
        compiler_params=PARAMS,
        cost_estimate=LIGHT,
        name="couple",
    )(plan, ids, table, pots, waves, other)


def combine_kernel(shape, scaling, plan, *refs):
    counts, cap, shift, first, count, total, terms = shape
    result, stage, sems = refs[-3:]
    summands = refs[-3 - terms : -3]

    def each(action):
        for i in range(total):
            source, slot = shift + i // count, first + i % count

            @pl.when(slot < plan[counts + source])
            def _(i=i, source=source, slot=slot):
                action(i, pltpu.make_async_copy(
                    stage.at[i], result.at[plan[source * cap + slot]], sems.at[i]
                ))

    def add(i, copy):
        value = summands[0][i]
        for term in summands[1:]:
            value = value + term[i].astype(F32)
        stage[i] = (value * scaling).astype(BF16)
        copy.start()

    each(add)
    each(lambda i, copy: copy.wait())


def combine(plan, before, kept, got, arrived, local_k, chunk, pools, cap, scaling):
    shift, first, count = chunk
    total = kept.shape[0]
    shape = arrived[0].shape
    block = pl.BlockSpec(shape, lambda i, plan: (0, 0, 0, 0))
    terms = [kept, got, *arrived]
    operands = ([] if before is None else [before]) + terms
    return pl.pallas_call(
        functools.partial(
            combine_kernel, (3 * pools * cap, cap, shift, first, count, total, len(terms)), scaling
        ),
        grid_spec=pltpu.PrefetchScalarGridSpec(
            num_scalar_prefetch=1,
            grid=(1,),
            in_specs=([] if before is None else [ANY]) + [block] * len(terms),
            out_specs=ANY,
            scratch_shapes=[pltpu.VMEM(shape, BF16), pltpu.SemaphoreType.DMA((total,))],
        ),
        out_shape=jax.ShapeDtypeStruct((local_k,) + shape[1:], BF16),
        input_output_aliases={} if before is None else {1: 0},
        compiler_params=PARAMS,
        cost_estimate=LIGHT,
        name="combine",
    )(plan, *operands)


def after(value, *others):
    return lax.optimization_barrier((value, *others))[0]


def body(wavefunctions, potentials, pert_order, partners):
    local_k, columns, stacked, bands = wavefunctions.shape
    z_points = stacked // 2
    pools = lax.axis_size("pool")
    groups = lax.axis_size("ga")
    cores = lax.axis_size("pert")
    my_pool = lax.axis_index("pool")
    my_core = lax.axis_index("pert")
    my_group = lax.axis_index("ga")
    cap = max(2, local_k // pools + 1)
    half = columns // cores
    share = bands // groups
    ids = jnp.stack([my_pool, my_core, my_group]).astype(jnp.int32)
    waves = wavefunctions.reshape(local_k * cores, half * stacked, bands)
    swap_cores = [(c, cores - 1 - c) for c in range(cores)]

    plan = make_plan(ids, partners, pools, local_k, cap)
    step = -(-cap // 3)
    phases = [(first, min(step, cap - first)) for first in range(0, cap, step)]
    gives = [pick(plan, ids, waves, pools, cap, first, count) for first, count in phases]
    potentials = after(potentials, gives[0])

    per_device = potentials.shape[0]
    by_half = potentials.reshape(per_device, cores, half, stacked)
    mine_now = lax.dynamic_index_in_dim(by_half, my_core, 1, keepdims=False)
    theirs_now = lax.dynamic_index_in_dim(by_half, 1 - my_core, 1, keepdims=False)
    other_pots = lax.ppermute(theirs_now, "pert", swap_cores)
    ordered = jnp.roll(pert_order.reshape(cores, per_device), -my_core, axis=0).reshape(-1)
    stored = jnp.where(
        my_core == 0, jnp.stack([mine_now, other_pots]), jnp.stack([other_pots, mine_now])
    ).reshape((cores * per_device,) + mine_now.shape[1:])
    options = jnp.arange(cores * per_device, dtype=jnp.int32)
    chosen = jnp.sum(
        jnp.where(
            (ordered[:, None] == options[None, :])[:, :, None, None], stored[None],
            jnp.zeros((), F32),
        ),
        axis=1,
    ).reshape(cores * per_device, half, 2, z_points)
    pots = jnp.moveaxis(chosen, 2, 1).reshape(cores * per_device, 2, half * z_points, 1)
    pots = jnp.broadcast_to(pots, pots.shape[:3] + (bands,))
    table = dft_table(z_points)
    scaling = 1.0 / math.sqrt(columns * groups * z_points)

    landed = []
    for phase, give in enumerate(gives):
        if phase >= WINDOW:
            give = after(give, landed[phase - WINDOW])
        landed.append(lax.all_to_all(give, "pool", 0, 0, tiled=True))

    chunks = [((0, 0, cap), waves)]
    chunks += [((1, first, count), row) for (first, count), row in zip(phases, landed)]
    kept, got, terms = [], [], []
    result = None

    def exchange(i):
        sent = []
        for step in range(1, groups):
            rows = slice(step * share, (step + 1) * share)
            total = (kept[i][:, :, rows] + got[i][:, :, rows].astype(F32)).astype(BF16)
            pairs = [(g, (g + step) % groups) for g in range(groups)]
            sent.append(lax.ppermute(total, "ga", pairs))
        terms.append(sent)

    def finish(i, result):
        return combine(
            plan, result, kept[i], got[i], terms[i], local_k, chunks[i][0], pools, cap, scaling
        )

    for i, (chunk, other) in enumerate(chunks):
        if i >= 1:
            other = after(other, kept[i - 1])
        if i >= LAG_CORE:
            exchange(i - LAG_CORE)
            other = after(other, got[i - LAG_CORE])
        if i >= LAG_GROUP:
            result = finish(i - LAG_GROUP, result)
            other = after(other, result)
        keep, give = couple(plan, ids, table, pots, waves, other, chunk, pools, cap, groups)
        kept.append(keep)
        got.append(lax.ppermute(give, "pert", swap_cores))
    for i in range(len(terms), len(chunks)):
        exchange(i)
    for i in range(max(0, len(chunks) - LAG_GROUP), len(chunks)):
        result = finish(i, result)
    return result.reshape(local_k, per_device, 2, share, bands)


WINDOW = 1
LAG_CORE, LAG_GROUP = 1, 2


def solution(mesh):
    return jax.shard_map(
        body,
        mesh=mesh,
        in_specs=(P("pool", "ga", None, None), P(("pb", "pert"), "ga", None), P(), P("pb")),
        out_specs=P(("pb", "pool"), "pert", None, "ga", None),
        check_vma=False,
    )
```

time: 165 us -> 165 us (level); the launches traced: 165 us -> 163 us
  waiting for transfers between devices: 32.2 us -> 74.1 us
  Pallas kernels: 88.8 us -> 54 us
  starting transfers between devices: 31.8 us -> 20.7 us
  other arithmetic: 2.18 us -> 6 us
  local copies, waits for them, and re-layouts: 9.76 us -> 7.7 us
    pallas_call x19 -> x11, Pallas kernels: 87 us -> 52.3 us  [the longest x4 31.1 us: couple(): pl.pallas_call(functools.partial(couple_kernel, shape), grid_spec=pltpu.P...]
    all_to_all x0 -> x3, waiting for transfers between devices: none -> 29.7 us  [body(): landed.append(lax.all_to_all(give, 'pool', 0, 0, tiled=True))]
    ppermute x9 -> x4, starting transfers between devices: 30.8 us -> 5.53 us  [exchange(): sent.append(lax.ppermute(total, 'ga', pairs))]
    all_to_all x0 -> x3, starting transfers between devices: none -> 14.9 us  [body(): landed.append(lax.all_to_all(give, 'pool', 0, 0, tiled=True))]
    ppermute x9 -> x4, waiting for transfers between devices: 32.2 us -> 41.5 us  [exchange(): sent.append(lax.ppermute(total, 'ga', pairs))]
    convert_element_type x0 -> x4, other arithmetic: none -> 3.85 us  [exchange(): total = (kept[i][:, :, rows] + got[i][:, :, rows].astype(F32)).astype(BF16)]
    ppermute x5 -> x4, waiting for transfers between devices: 0.01 us -> 2.91 us  [body(): got.append(lax.ppermute(give, 'pert', swap_cores))]
    unnamed x34 -> x28, local copies, waits for them, and re-layouts: 7.29 us -> 5.24 us
  transfers between devices with their start and end apart: 15 -> 12, of which waited for: 3 -> 6; matrix products, arithmetic and copies ran while one was open for 2% -> 5% of each run, Pallas kernels for 42% -> 19%
where the time goes in v3:
time: 165 us; the launch traced here: 163 us
  waiting for transfers between devices  74.1 us (45%)
  Pallas kernels  54 us (33%)
  starting transfers between devices  20.7 us (13%)
  local copies, waits for them, and re-layouts  7.7 us (5%)
  other arithmetic  6 us (4%)
    ppermute x4, waiting for transfers between devices, exchange(): sent.append(lax.ppermute(total, 'ga', pairs))  41.5 us
    pallas_call x4, Pallas kernels, couple(): pl.pallas_call(functools.partial(couple_kernel, shape), grid_spec=pltpu.P...  31.1 us
    all_to_all x3, waiting for transfers between devices, body(): landed.append(lax.all_to_all(give, 'pool', 0, 0, tiled=True))  29.7 us
    all_to_all x3, starting transfers between devices, body(): landed.append(lax.all_to_all(give, 'pool', 0, 0, tiled=True))  14.9 us
    pallas_call x4, Pallas kernels, combine(): pl.pallas_call(functools.partial(combine_kernel, (3 * pools * cap, cap, s...  12 us
    pallas_call x3, Pallas kernels, pick(): pl.pallas_call(functools.partial(pick_kernel, 2 * pools * cap + first, ca...  9.2 us
    ppermute x4, starting transfers between devices, exchange(): sent.append(lax.ppermute(total, 'ga', pairs))  5.53 us
    unnamed x28, local copies, waits for them, and re-layouts  5.24 us
  transfers between devices with their start and end apart: 12, of which 6 were waited for; matrix products, arithmetic and copies ran while one was open for 5% of the time, Pallas kernels for 19%

profile of v3, /device:TPU:0, one launch (start us, length us, event | category | flops | bytes accessed | tf_op | source)
XLA Modules:
  0.0 162.9 jit_solution(1532356083707078160)
XLA Ops:
  0.6 1.8 %plan.1 = s32[64]{0:T(128)} custom-call(s32[3]{0:T(128)} %pad_add_fusion.1.ids, s32[64]{0:T(128)} %partners.1), custom_call_target="tpu_custom_call" | custom-call | flops 1 | bytes 1024 | tf_op jit(solution)/shard_map/plan/pallas_call | solution.py:65
  2.4 3.2 %pick.3 = bf16[4,2,720,128]{3,2,1,0:T(8,128)(2,1)} custom-call(s32[64]{0:T(128)} %plan.1, s32[3]{0:T(128)} %pad_add_fusion.1.ids, bf16[32,720,128]{2,1,0:T(8,128)(2,1)} %bitcast.15), custom_call_target="tpu_custom_call" | custom-call | flops 1 | bytes 1024 | tf_op jit(solution)/shard_map/pick/pallas_call | solution.py:91
  5.6 6.3 %all-to-all-start = ((bf16[4,2,720,128]{3,2,1,0:T(8,128)(2,1)}), bf16[4,2,720,128]{3,2,1,0:T(8,128)(2,1)S(1)}, u32[]{:S(2)}, u32[]{:S(2)}) async-start(bf16[4,2,720,128]{3,2,1,0:T(8,128)(2,1)} %pick.3), calls=%async_computation | async-start | bytes 2949120 | tf_op jit(solution)/shard_map/all_to_all | solution.py:308
  13.6 3.3 %pick.4 = bf16[4,2,720,128]{3,2,1,0:T(8,128)(2,1)} custom-call(s32[64]{0:T(128)} %plan.1, s32[3]{0:T(128)} %pad_add_fusion.1.ids, bf16[32,720,128]{2,1,0:T(8,128)(2,1)} %bitcast.16), custom_call_target="tpu_custom_call" | custom-call | flops 1 | bytes 1024 | tf_op jit(solution)/shard_map/pick/pallas_call | solution.py:91
  17.0 29.7 %all-to-all-done.rest_0_ = bf16[4,2,720,128]{3,2,1,0:T(8,128)(2,1)S(1)} async-done(((bf16[4,2,720,128]{3,2,1,0:T(8,128)(2,1)}), bf16[4,2,720,128]{3,2,1,0:T(8,128)(2,1)S(1)}, u32[]{:S(2)}, u32[]{:S(2)}) %all-to-all-start) | async-done | bytes 1474592 | tf_op jit(solution)/shard_map/all_to_all | solution.py:308
  46.8 3.6 %all-to-all-start.1 = ((bf16[4,2,720,128]{3,2,1,0:T(8,128)(2,1)}), bf16[4,2,720,128]{3,2,1,0:T(8,128)(2,1)S(1)}, u32[]{:S(2)}, u32[]{:S(2)}) async-start(bf16[4,2,720,128]{3,2,1,0:T(8,128)(2,1)} %pick.4), calls=%async_computation.1 | async-start | bytes 2949120 | tf_op jit(solution)/shard_map/all_to_all | solution.py:308
  50.7 2.0 %broadcast_in_dim.35.pots = f32[6,2,360,128]{3,2,1,0:T(8,128)} broadcast(f32[6,2,360]{2,1,0:T(2,128)S(1)} %broadcast_in_dim.34), dimensions={0,1,2} | broadcast | bytes 2229120 | tf_op jit(solution)/shard_map/broadcast_in_dim | solution.py:300
  52.7 6.4 %couple.4 = (f32[5,6,128,128]{3,2,1,0:T(8,128)}, bf16[5,6,128,128]{3,2,1,0:T(8,128)(2,1)}) custom-call(s32[64]{0:T(128)} %plan.1, s32[3]{0:T(128)} %pad_add_fusion.1.ids, bf16[240,240]{1,0:T(8,128)(2,1)} %maximum_maximum_fusion.table, f32[6,2,360,128]{3,2,1,0:T(8,128)} %broadcast_in_dim.35.pots, bf16[32,720,128]{2,1,0:T(8,128)(2,1)} %bitcast.17, ...), custom_call_target="tpu_custom_call" | custom-call | flops 1 | bytes 1024 | tf_op jit(solution)/shard_map/couple/pallas_call | solution.py:182
  59.1 2.9 %collective-permute-done.1.refs_1_ = bf16[5,6,128,128]{3,2,1,0:T(8,128)(2,1)} collective-permute-done((bf16[5,6,128,128]{3,2,1,0:T(8,128)(2,1)}, bf16[5,6,128,128]{3,2,1,0:T(8,128)(2,1)}, u32[]{:S(2)}, u32[]{:S(2)}) %collective-permute-start.1) | collective-permute-done | bytes 983072 | tf_op jit(solution)/shard_map/ppermute | solution.py:340
  62.0 9.6 %couple.5 = (f32[6,6,128,128]{3,2,1,0:T(8,128)}, bf16[6,6,128,128]{3,2,1,0:T(8,128)(2,1)}) custom-call(s32[64]{0:T(128)} %plan.1, s32[3]{0:T(128)} %pad_add_fusion.1.ids, bf16[240,240]{1,0:T(8,128)(2,1)} %maximum_maximum_fusion.table, f32[6,2,360,128]{3,2,1,0:T(8,128)} %broadcast_in_dim.35.pots, bf16[32,720,128]{2,1,0:T(8,128)(2,1)} %bitcast.19, ...), custom_call_target="tpu_custom_call" | custom-call | flops 1 | bytes 1024 | tf_op jit(solution)/shard_map/couple/pallas_call | solution.py:182
  71.7 1.2 add_convert_fusion.2
  72.9 1.6 collective-permute-start.2
  74.4 12.0 %collective-permute-done.2.refs_2_ = bf16[5,6,64,128]{3,2,1,0:T(8,128)(2,1)S(1)} collective-permute-done((bf16[5,6,64,128]{3,2,1,0:T(8,128)(2,1)S(1)}, bf16[5,6,64,128]{3,2,1,0:T(8,128)(2,1)S(1)}, u32[]{:S(2)}, u32[]{:S(2)}) %collective-permute-start.2) | collective-permute-done | bytes 491552 | tf_op jit(solution)/shard_map/ppermute | solution.py:321
  87.2 2.9 %combine.4.refs_0_ = bf16[16,6,64,128]{3,2,1,0:T(8,128)(2,1)} custom-call(s32[64]{0:T(128)} %plan.1, f32[5,6,128,128]{3,2,1,0:T(8,128)} %get-tuple-element.25.refs_0_, bf16[5,6,128,128]{3,2,1,0:T(8,128)(2,1)} %collective-permute-done.1.refs_1_, bf16[5,6,64,128]{3,2,1,0:T(8,128)(2,1)} %copy-done.10), custom_call_target="tpu_custom_call" | custom-call | flops 1 | bytes 1024 | tf_op jit(solution)/shard_map/combine/pallas_call | solution.py:237
  90.2 1.2 copy-done.1
  91.4 9.5 %couple.6 = (f32[6,6,128,128]{3,2,1,0:T(8,128)}, bf16[6,6,128,128]{3,2,1,0:T(8,128)(2,1)}) custom-call(s32[64]{0:T(128)} %plan.1, s32[3]{0:T(128)} %pad_add_fusion.1.ids, bf16[240,240]{1,0:T(8,128)(2,1)} %maximum_maximum_fusion.table, f32[6,2,360,128]{3,2,1,0:T(8,128)} %broadcast_in_dim.35.pots, bf16[32,720,128]{2,1,0:T(8,128)(2,1)} %bitcast.20, ...), custom_call_target="tpu_custom_call" | custom-call | flops 1 | bytes 1024 | tf_op jit(solution)/shard_map/couple/pallas_call | solution.py:182
  100.9 2.8 %pick.5 = bf16[4,1,720,128]{3,2,1,0:T(8,128)(2,1)} custom-call(s32[64]{0:T(128)} %plan.1, s32[3]{0:T(128)} %pad_add_fusion.1.ids, bf16[32,720,128]{2,1,0:T(8,128)(2,1)} %bitcast.21), custom_call_target="tpu_custom_call" | custom-call | flops 1 | bytes 1024 | tf_op jit(solution)/shard_map/pick/pallas_call | solution.py:91
  103.7 5.1 %all-to-all-start.2 = ((bf16[4,1,720,128]{3,2,1,0:T(8,128)(2,1)}), bf16[4,1,720,128]{3,2,1,0:T(8,128)(2,1)S(1)}, u32[]{:S(2)}, u32[]{:S(2)}) async-start(bf16[4,1,720,128]{3,2,1,0:T(8,128)(2,1)} %pick.5), calls=%async_computation.2 | async-start | bytes 1474560 | tf_op jit(solution)/shard_map/all_to_all | solution.py:308
  108.7 1.3 add_convert_fusion.1
  110.0 1.6 collective-permute-start.4
  111.6 14.0 %collective-permute-done.4.refs_3_ = bf16[6,6,64,128]{3,2,1,0:T(8,128)(2,1)S(1)} collective-permute-done((bf16[6,6,64,128]{3,2,1,0:T(8,128)(2,1)S(1)}, bf16[6,6,64,128]{3,2,1,0:T(8,128)(2,1)S(1)}, u32[]{:S(2)}, u32[]{:S(2)}) %collective-permute-start.4) | collective-permute-done | bytes 589856 | tf_op jit(solution)/shard_map/ppermute | solution.py:321
  126.3 3.2 %combine.5.refs_0_ = bf16[16,6,64,128]{3,2,1,0:T(8,128)(2,1)} custom-call(s32[64]{0:T(128)} %plan.1, bf16[16,6,64,128]{3,2,1,0:T(8,128)(2,1)} %combine.4.refs_0_, f32[6,6,128,128]{3,2,1,0:T(8,128)} %get-tuple-element.29.refs_1_, bf16[6,6,128,128]{3,2,1,0:T(8,128)(2,1)} %collective-permute-done.3.refs_2_, ...), custom_call_target="tpu_custom_call", output_to_operand_aliasing={{}: (1, {})} | custom-call | flops 1 | bytes 1024 | tf_op jit(solution)/shard_map/combine/pallas_call | solution.py:237
  129.6 0.8 copy-done.5
  130.4 5.7 %couple.7 = (f32[3,6,128,128]{3,2,1,0:T(8,128)}, bf16[3,6,128,128]{3,2,1,0:T(8,128)(2,1)}) custom-call(s32[64]{0:T(128)} %plan.1, s32[3]{0:T(128)} %pad_add_fusion.1.ids, bf16[240,240]{1,0:T(8,128)(2,1)} %maximum_maximum_fusion.table, f32[6,2,360,128]{3,2,1,0:T(8,128)} %broadcast_in_dim.35.pots, bf16[32,720,128]{2,1,0:T(8,128)(2,1)} %bitcast.22, ...), custom_call_target="tpu_custom_call" | custom-call | flops 1 | bytes 1024 | tf_op jit(solution)/shard_map/couple/pallas_call | solution.py:182
  136.2 1.3 add_convert_fusion
  137.5 1.6 collective-permute-start.6
  139.2 0.8 collective-permute-start.8
  140.0 13.7 %collective-permute-done.6.refs_3_ = bf16[6,6,64,128]{3,2,1,0:T(8,128)(2,1)S(1)} collective-permute-done((bf16[6,6,64,128]{3,2,1,0:T(8,128)(2,1)S(1)}, bf16[6,6,64,128]{3,2,1,0:T(8,128)(2,1)S(1)}, u32[]{:S(2)}, u32[]{:S(2)}) %collective-permute-start.6) | collective-permute-done | bytes 589856 | tf_op jit(solution)/shard_map/ppermute | solution.py:321
  153.7 0.8 copy-done.8
  154.5 3.2 %combine.6.refs_0_ = bf16[16,6,64,128]{3,2,1,0:T(8,128)(2,1)} custom-call(s32[64]{0:T(128)} %plan.1, bf16[16,6,64,128]{3,2,1,0:T(8,128)(2,1)} %combine.5.refs_0_, f32[6,6,128,128]{3,2,1,0:T(8,128)} %get-tuple-element.35.refs_1_, bf16[6,6,128,128]{3,2,1,0:T(8,128)(2,1)} %collective-permute-done.5.refs_2_, ...), custom_call_target="tpu_custom_call", output_to_operand_aliasing={{}: (1, {})} | custom-call | flops 1 | bytes 1024 | tf_op jit(solution)/shard_map/combine/pallas_call | solution.py:237
  157.8 1.8 %collective-permute-done.8.refs_3_ = bf16[3,6,64,128]{3,2,1,0:T(8,128)(2,1)S(1)} collective-permute-done((bf16[3,6,64,128]{3,2,1,0:T(8,128)(2,1)S(1)}, bf16[3,6,64,128]{3,2,1,0:T(8,128)(2,1)S(1)}, u32[]{:S(2)}, u32[]{:S(2)}) %collective-permute-start.8) | collective-permute-done | bytes 294944 | tf_op jit(solution)/shard_map/ppermute | solution.py:321
  160.3 2.6 %combine.7 = bf16[16,6,64,128]{3,2,1,0:T(8,128)(2,1)} custom-call(s32[64]{0:T(128)} %plan.1, bf16[16,6,64,128]{3,2,1,0:T(8,128)(2,1)} %combine.6.refs_0_, f32[3,6,128,128]{3,2,1,0:T(8,128)} %get-tuple-element.41.refs_1_, bf16[3,6,128,128]{3,2,1,0:T(8,128)(2,1)} %copy-done.7, bf16[3,6,64,128]{3,2,1,0:T(8,128)(2,1)} %copy-done.11), custom_call_target="tpu_custom_call", output_to_operand_aliasing={{}: (1, {})} | custom-call | flops 1 | bytes 1024 | tf_op jit(solution)/shard_map/combine/pallas_call | solution.py:237
  (58 shorter events, 5.3 us)
Async XLA Ops:
  5.5 6.4 %copy-start.12 = (f32[3,6,240]{2,1,0:T(8,128)S(1)}, f32[3,6,240]{2,1,0:T(8,128)}, u32[]{:S(2)}) copy-start(f32[3,6,240]{2,1,0:T(8,128)} %param.5) | copy-start | bytes 51844
  5.6 6.5 %copy-start.13 = (s32[6]{0:T(128)S(1)}, s32[6]{0:T(128)}, u32[]{:S(2)}) copy-start(s32[6]{0:T(128)} %param.6) | copy-start | bytes 76
  5.6 41.2 %all-to-all-start = ((bf16[4,2,720,128]{3,2,1,0:T(8,128)(2,1)}), bf16[4,2,720,128]{3,2,1,0:T(8,128)(2,1)S(1)}, u32[]{:S(2)}, u32[]{:S(2)}) async-start(bf16[4,2,720,128]{3,2,1,0:T(8,128)(2,1)} %pick.3), calls=%async_computation | async-start | bytes 2949120 | tf_op jit(solution)/shard_map/all_to_all | solution.py:308
  12.0 5.0 %collective-permute-start = (f32[3,3,240]{2,1,0:T(4,128)S(1)}, f32[3,3,240]{2,1,0:T(4,128)S(1)}, u32[]{:S(2)}, u32[]{:S(2)}) collective-permute-start(f32[3,3,240]{2,1,0:T(4,128)S(1)} %bitcast.27), channel_id=1, source_target_pairs={{0,1},{1,0},{2,3},{3,2},{4,5},{5,4},{6,7},{7,6},{8,9},{9,8},{10,11... | collective-permute-start | bytes 25928 | tf_op jit(solution)/shard_map/ppermute | solution.py:286
  46.8 3.7 %copy-start = (bf16[4,2,720,128]{3,2,1,0:T(8,128)(2,1)}, bf16[4,2,720,128]{3,2,1,0:T(8,128)(2,1)S(1)}, u32[]{:S(2)}) copy-start(bf16[4,2,720,128]{3,2,1,0:T(8,128)(2,1)S(1)} %all-to-all-done.rest_0_) | copy-start | bytes 4423684
  46.8 43.4 %all-to-all-start.1 = ((bf16[4,2,720,128]{3,2,1,0:T(8,128)(2,1)}), bf16[4,2,720,128]{3,2,1,0:T(8,128)(2,1)S(1)}, u32[]{:S(2)}, u32[]{:S(2)}) async-start(bf16[4,2,720,128]{3,2,1,0:T(8,128)(2,1)} %pick.4), calls=%async_computation.1 | async-start | bytes 2949120 | tf_op jit(solution)/shard_map/all_to_all | solution.py:308
  59.1 2.9 %collective-permute-start.1 = (bf16[5,6,128,128]{3,2,1,0:T(8,128)(2,1)}, bf16[5,6,128,128]{3,2,1,0:T(8,128)(2,1)}, u32[]{:S(2)}, u32[]{:S(2)}) collective-permute-start(bf16[5,6,128,128]{3,2,1,0:T(8,128)(2,1)} %get-tuple-element.26), channel_id=1, source_target_pairs={{0,1},{1,0},{2,3},{3,2},{4,5},{5,4},{6,7},{7,6},{8,9},{9,8},{10,11... | collective-permute-start | bytes 2949128 | tf_op jit(solution)/shard_map/ppermute | solution.py:340
  59.1 12.6 %copy-start.4 = (f32[5,6,128,128]{3,2,1,0:T(8,128)S(1)}, f32[5,6,128,128]{3,2,1,0:T(8,128)}, u32[]{:S(2)}) copy-start(f32[5,6,128,128]{3,2,1,0:T(8,128)} %get-tuple-element.25.refs_0_) | copy-start | bytes 5898244
  71.5 18.6 %collective-permute-start.3 = (bf16[6,6,128,128]{3,2,1,0:T(8,128)(2,1)}, bf16[6,6,128,128]{3,2,1,0:T(8,128)(2,1)}, u32[]{:S(2)}, u32[]{:S(2)}) collective-permute-start(bf16[6,6,128,128]{3,2,1,0:T(8,128)(2,1)} %get-tuple-element.30), channel_id=1, source_target_pairs={{0,1},{1,0},{2,3},{3,2},{4,5},{5,4},{6,7},{7,6},{8,9},{9,8},{10,11... | collective-permute-start | bytes 3538952 | tf_op jit(solution)/shard_map/ppermute | solution.py:340
  72.9 13.6 %collective-permute-start.2 = (bf16[5,6,64,128]{3,2,1,0:T(8,128)(2,1)S(1)}, bf16[5,6,64,128]{3,2,1,0:T(8,128)(2,1)S(1)}, u32[]{:S(2)}, u32[]{:S(2)}) collective-permute-start(bf16[5,6,64,128]{3,2,1,0:T(8,128)(2,1)S(1)} %add_convert_fusion.2), channel_id=1, source_target_pairs={{0,2},{2,0},{1,3},{3,1},{4,6},{6,4},{5,7},{7,5},{8,10},{10,8},{9,1... | collective-permute-start | bytes 1474568 | tf_op jit(solution)/shard_map/ppermute | solution.py:321
  86.4 0.8 copy-start.10
  90.1 1.2 copy-start.1
  100.9 28.7 %collective-permute-start.5 = (bf16[6,6,128,128]{3,2,1,0:T(8,128)(2,1)}, bf16[6,6,128,128]{3,2,1,0:T(8,128)(2,1)}, u32[]{:S(2)}, u32[]{:S(2)}) collective-permute-start(bf16[6,6,128,128]{3,2,1,0:T(8,128)(2,1)} %get-tuple-element.36), channel_id=1, source_target_pairs={{0,1},{1,0},{2,3},{3,2},{4,5},{5,4},{6,7},{7,6},{8,9},{9,8},{10,11... | collective-permute-start | bytes 3538952 | tf_op jit(solution)/shard_map/ppermute | solution.py:340
  100.9 7.9 %copy-start.3 = (f32[6,6,128,128]{3,2,1,0:T(8,128)S(1)}, f32[6,6,128,128]{3,2,1,0:T(8,128)}, u32[]{:S(2)}) copy-start(f32[6,6,128,128]{3,2,1,0:T(8,128)} %get-tuple-element.29.refs_1_) | copy-start | bytes 7077892
  103.7 25.9 %all-to-all-start.2 = ((bf16[4,1,720,128]{3,2,1,0:T(8,128)(2,1)}), bf16[4,1,720,128]{3,2,1,0:T(8,128)(2,1)S(1)}, u32[]{:S(2)}, u32[]{:S(2)}) async-start(bf16[4,1,720,128]{3,2,1,0:T(8,128)(2,1)} %pick.5), calls=%async_computation.2 | async-start | bytes 1474560 | tf_op jit(solution)/shard_map/all_to_all | solution.py:308
  110.0 15.5 %collective-permute-start.4 = (bf16[6,6,64,128]{3,2,1,0:T(8,128)(2,1)S(1)}, bf16[6,6,64,128]{3,2,1,0:T(8,128)(2,1)S(1)}, u32[]{:S(2)}, u32[]{:S(2)}) collective-permute-start(bf16[6,6,64,128]{3,2,1,0:T(8,128)(2,1)S(1)} %add_convert_fusion.1), channel_id=1, source_target_pairs={{0,2},{2,0},{1,3},{3,1},{4,6},{6,4},{5,7},{7,5},{8,10},{10,8},{9,1... | collective-permute-start | bytes 1769480 | tf_op jit(solution)/shard_map/ppermute | solution.py:321
  125.5 0.8 copy-start.9
  129.6 0.9 copy-start.5
  129.6 6.6 %copy-start.2 = (f32[6,6,128,128]{3,2,1,0:T(8,128)S(1)}, f32[6,6,128,128]{3,2,1,0:T(8,128)}, u32[]{:S(2)}) copy-start(f32[6,6,128,128]{3,2,1,0:T(8,128)} %get-tuple-element.35.refs_1_) | copy-start | bytes 7077892
  136.1 3.0 %copy-start.6 = (f32[3,6,128,128]{3,2,1,0:T(8,128)S(1)}, f32[3,6,128,128]{3,2,1,0:T(8,128)}, u32[]{:S(2)}) copy-start(f32[3,6,128,128]{3,2,1,0:T(8,128)} %get-tuple-element.41.refs_1_) | copy-start | bytes 3538948
  136.1 3.0 %collective-permute-start.7 = (bf16[3,6,128,128]{3,2,1,0:T(8,128)(2,1)}, bf16[3,6,128,128]{3,2,1,0:T(8,128)(2,1)S(1)}, u32[]{:S(2)}, u32[]{:S(2)}) collective-permute-start(bf16[3,6,128,128]{3,2,1,0:T(8,128)(2,1)} %get-tuple-element.42), channel_id=1, source_target_pairs={{0,1},{1,0},{2,3},{3,2},{4,5},{5,4},{6,7},{7,6},{8,9},{9,8},{10,11... | collective-permute-start | bytes 1769480 | tf_op jit(solution)/shard_map/ppermute | solution.py:340
  137.5 16.2 %collective-permute-start.6 = (bf16[6,6,64,128]{3,2,1,0:T(8,128)(2,1)S(1)}, bf16[6,6,64,128]{3,2,1,0:T(8,128)(2,1)S(1)}, u32[]{:S(2)}, u32[]{:S(2)}) collective-permute-start(bf16[6,6,64,128]{3,2,1,0:T(8,128)(2,1)S(1)} %add_convert_fusion), channel_id=1, source_target_pairs={{0,2},{2,0},{1,3},{3,1},{4,6},{6,4},{5,7},{7,5},{8,10},{10,8},{9,1... | collective-permute-start | bytes 1769480 | tf_op jit(solution)/shard_map/ppermute | solution.py:321
  139.1 18.7 %copy-start.7 = (bf16[3,6,128,128]{3,2,1,0:T(8,128)(2,1)}, bf16[3,6,128,128]{3,2,1,0:T(8,128)(2,1)S(1)}, u32[]{:S(2)}) copy-start(bf16[3,6,128,128]{3,2,1,0:T(8,128)(2,1)S(1)} %collective-permute-done.7.refs_2_) | copy-start | bytes 1769476
  139.2 20.4 %collective-permute-start.8 = (bf16[3,6,64,128]{3,2,1,0:T(8,128)(2,1)S(1)}, bf16[3,6,64,128]{3,2,1,0:T(8,128)(2,1)S(1)}, u32[]{:S(2)}, u32[]{:S(2)}) collective-permute-start(bf16[3,6,64,128]{3,2,1,0:T(8,128)(2,1)S(1)} %add_convert_fusion.3), channel_id=1, source_target_pairs={{0,2},{2,0},{1,3},{3,1},{4,6},{6,4},{5,7},{7,5},{8,10},{10,8},{9,1... | collective-permute-start | bytes 884744 | tf_op jit(solution)/shard_map/ppermute | solution.py:321
  153.7 0.8 copy-start.8
  159.6 0.7 copy-start.11

commit v4 on v3

--- a/solution.py
+++ b/solution.py
@@ -72,28 +72,25 @@
     )(ids, partners)
 
 
-def pick_kernel(base, cap, count, pools, plan, ids, waves, give, sems):
-    copies = []
-    for shift in range(1, pools):
-        taker = lax.rem(ids[0] + shift, pools)
-        for i in range(count):
-            place = plan[base + shift * cap + i] * 2 + ids[1]
-            copies.append(
-                pltpu.make_async_copy(waves.at[place], give.at[taker, i], sems.at[shift - 1, i])
-            )
+def pick_kernel(base, plan, ids, waves, give, sems):
+    copies = [
+        pltpu.make_async_copy(waves.at[plan[base + i] * 2 + ids[1]], give.at[i], sems.at[i])
+        for i in range(give.shape[0])
+    ]
     for copy in copies:
         copy.start()
     for copy in copies:
         copy.wait()
 
 
-def pick(plan, ids, waves, pools, cap, first, count):
+def pick(plan, ids, waves, pools, cap, chunk):
+    shift, first, count = chunk
     return pl.pallas_call(
-        functools.partial(pick_kernel, 2 * pools * cap + first, cap, count, pools),
-        out_shape=jax.ShapeDtypeStruct((pools, count) + waves.shape[1:], waves.dtype),
+        functools.partial(pick_kernel, (2 * pools + shift) * cap + first),
+        out_shape=jax.ShapeDtypeStruct((count,) + waves.shape[1:], waves.dtype),
         in_specs=[SMEM, SMEM, ANY],
         out_specs=pl.BlockSpec(memory_space=pltpu.VMEM),
-        scratch_shapes=[pltpu.SemaphoreType.DMA((pools - 1, count))],
+        scratch_shapes=[pltpu.SemaphoreType.DMA((count,))],
         compiler_params=PARAMS,
         cost_estimate=LIGHT,
         name="pick",
@@ -115,17 +112,12 @@
     return [jnp.concatenate(part, axis=0).astype(BF16) for part in parts]
 
 
-def couple_kernel(shape, plan, ids, table, pots, own, *rest):
-    counts, cap, shift, first, count, groups, z_points = shape
-    other, keep, give = rest
-    i = pl.program_id(0)
-    source = i // count
-
-    @pl.when(first + i - source * count < plan[counts + shift + source])
+def couple_kernel(shape, plan, ids, table, pots, own, other, keep, give):
+    number, first, groups, z_points = shape
+
+    @pl.when(first + pl.program_id(0) < plan[number])
     def _():
-        own_re, own_im, o_re, o_im = to_real(
-            own[0], other[...].reshape(own.shape[1:]), table[...], z_points
-        )
+        own_re, own_im, o_re, o_im = to_real(own[0], other[0], table[...], z_points)
         u_re, u_im = own_re.astype(F32), own_im.astype(F32)
         both_o = jnp.concatenate([o_re, o_im], axis=1).T
         bands = o_re.shape[1]
@@ -158,32 +150,22 @@
     shift, first, count = chunk
     half, bands = waves.shape[1:]
     parts = pots.shape[0]
-    sources = 1 if shift == 0 else pools - 1
+    base = shift * cap + first
     block = (1, half, bands)
-
-    def entry(i):
-        return (shift + i // count) * cap + first + i % count
-
-    own_block = pl.BlockSpec(block, lambda i, plan, ids: (plan[entry(i)] * 2 + ids[1], 0, 0))
+    own_block = pl.BlockSpec(block, lambda i, plan, ids: (plan[base + i] * 2 + ids[1], 0, 0))
     if shift == 0:
         other_block = pl.BlockSpec(
-            block, lambda i, plan, ids: (plan[pools * cap + entry(i)] * 2 + ids[1], 0, 0)
+            block, lambda i, plan, ids: (plan[pools * cap + base + i] * 2 + ids[1], 0, 0)
         )
     else:
-        other_block = pl.BlockSpec(
-            (1,) + block,
-            lambda i, plan, ids: (
-                lax.rem(ids[0] - shift - i // count + pools, pools), i % count, 0, 0
-            ),
-        )
+        other_block = pl.BlockSpec(block, lambda i, plan, ids: (i, 0, 0))
     out_block = pl.BlockSpec((1, parts, bands, bands), lambda i, plan, ids: (i, 0, 0, 0))
-    shape = (3 * pools * cap, cap, shift, first, count, groups, table.shape[0] // 2)
-    total = sources * count
+    shape = (3 * pools * cap + shift, first, groups, table.shape[0] // 2)
     return pl.pallas_call(
         functools.partial(couple_kernel, shape),
         grid_spec=pltpu.PrefetchScalarGridSpec(
             num_scalar_prefetch=2,
-            grid=(total,),
+            grid=(count,),
             in_specs=[
                 pl.BlockSpec(table.shape, lambda i, plan, ids: (0, 0)),
                 pl.BlockSpec(pots.shape, lambda i, plan, ids: (0, 0, 0, 0)),
@@ -192,8 +174,8 @@
             out_specs=[out_block] * 2,
         ),
         out_shape=[
-            jax.ShapeDtypeStruct((total, parts, bands, bands), F32),
-            jax.ShapeDtypeStruct((total, parts, bands, bands), BF16),
+            jax.ShapeDtypeStruct((count, parts, bands, bands), F32),
+            jax.ShapeDtypeStruct((count, parts, bands, bands), BF16),
         ],
         compiler_params=PARAMS,
         cost_estimate=LIGHT,
@@ -202,24 +184,24 @@
 
 
 def combine_kernel(shape, scaling, plan, *refs):
-    counts, cap, shift, first, count, total, terms = shape
+    number, base, first, total, pieces, others = shape
     result, stage, sems = refs[-3:]
-    summands = refs[-3 - terms : -3]
+    summands = refs[-3 - 1 - pieces * (1 + others) : -3]
+    size = summands[1].shape[0]
 
     def each(action):
         for i in range(total):
-            source, slot = shift + i // count, first + i % count
-
-            @pl.when(slot < plan[counts + source])
-            def _(i=i, source=source, slot=slot):
+
+            @pl.when(first + i < plan[number])
+            def _(i=i):
                 action(i, pltpu.make_async_copy(
-                    stage.at[i], result.at[plan[source * cap + slot]], sems.at[i]
+                    stage.at[i], result.at[plan[base + i]], sems.at[i]
                 ))
 
     def add(i, copy):
         value = summands[0][i]
-        for term in summands[1:]:
-            value = value + term[i].astype(F32)
+        for group in range(1 + others):
+            value = value + summands[1 + group * pieces + i // size][i % size].astype(F32)
         stage[i] = (value * scaling).astype(BF16)
         copy.start()
 
@@ -229,23 +211,31 @@
 
 def combine(plan, before, kept, got, arrived, local_k, chunk, pools, cap, scaling):
     shift, first, count = chunk
-    total = kept.shape[0]
-    shape = arrived[0].shape
-    block = pl.BlockSpec(shape, lambda i, plan: (0, 0, 0, 0))
-    terms = [kept, got, *arrived]
+    _, parts, _, bands = kept.shape
+    share = arrived[0].shape[2]
+    terms = [kept, *got, *arrived]
+    blocks = [
+        pl.BlockSpec((term.shape[0], parts, share, bands), lambda i, plan: (0, 0, 0, 0))
+        for term in terms
+    ]
     operands = ([] if before is None else [before]) + terms
+    shape = (
+        3 * pools * cap + shift, shift * cap + first, first, count, len(got),
+        len(arrived) // len(got),
+    )
     return pl.pallas_call(
-        functools.partial(
-            combine_kernel, (3 * pools * cap, cap, shift, first, count, total, len(terms)), scaling
-        ),
+        functools.partial(combine_kernel, shape, scaling),
         grid_spec=pltpu.PrefetchScalarGridSpec(
             num_scalar_prefetch=1,
             grid=(1,),
-            in_specs=([] if before is None else [ANY]) + [block] * len(terms),
+            in_specs=([] if before is None else [ANY]) + blocks,
             out_specs=ANY,
-            scratch_shapes=[pltpu.VMEM(shape, BF16), pltpu.SemaphoreType.DMA((total,))],
+            scratch_shapes=[
+                pltpu.VMEM((count, parts, share, bands), BF16),
+                pltpu.SemaphoreType.DMA((count,)),
+            ],
         ),
-        out_shape=jax.ShapeDtypeStruct((local_k,) + shape[1:], BF16),
+        out_shape=jax.ShapeDtypeStruct((local_k, parts, share, bands), BF16),
         input_output_aliases={} if before is None else {1: 0},
         compiler_params=PARAMS,
         cost_estimate=LIGHT,
@@ -255,6 +245,20 @@
 
 def after(value, *others):
     return lax.optimization_barrier((value, *others))[0]
+
+
+def transfers(pools, cap):
+    moves, waits = [], []
+    for s in range(1, (pools + 1) // 2):
+        for shift in (s, pools - s):
+            moves.append((shift, 0, cap))
+            waits.append(len(moves) - 3 if s > 1 else None)
+    if pools % 2 == 0:
+        large = (3 * cap + 2) // 5
+        for first, count in ((0, large), (large, cap - large)):
+            moves.append((pools // 2, first, count))
+            waits.append(len(moves) - 2 if len(moves) > 1 else None)
+    return moves, waits
 
 
 def body(wavefunctions, potentials, pert_order, partners):
@@ -274,9 +278,8 @@
     swap_cores = [(c, cores - 1 - c) for c in range(cores)]
 
     plan = make_plan(ids, partners, pools, local_k, cap)
-    step = -(-cap // 3)
-    phases = [(first, min(step, cap - first)) for first in range(0, cap, step)]
-    gives = [pick(plan, ids, waves, pools, cap, first, count) for first, count in phases]
+    moves, waits = transfers(pools, cap)
+    gives = [pick(plan, ids, waves, pools, cap, move) for move in moves]
     potentials = after(potentials, gives[0])
 
     per_device = potentials.shape[0]
@@ -302,23 +305,31 @@
     scaling = 1.0 / math.sqrt(columns * groups * z_points)
 
     landed = []
-    for phase, give in enumerate(gives):
-        if phase >= WINDOW:
-            give = after(give, landed[phase - WINDOW])
-        landed.append(lax.all_to_all(give, "pool", 0, 0, tiled=True))
-
-    chunks = [((0, 0, cap), waves)]
-    chunks += [((1, first, count), row) for (first, count), row in zip(phases, landed)]
+    for move, wait, give in zip(moves, waits, gives):
+        if wait is not None:
+            give = after(give, landed[wait])
+        pairs = [(p, (p + move[0]) % pools) for p in range(pools)]
+        landed.append(lax.ppermute(give, "pool", pairs))
+
+    chunks = [((0, 0, cap), waves), *zip(moves, landed)]
     kept, got, terms = [], [], []
     result = None
+
+    def swap(give):
+        return [
+            lax.ppermute(give[first : first + PIECE], "pert", swap_cores)
+            for first in range(0, give.shape[0], PIECE)
+        ]
 
     def exchange(i):
         sent = []
         for step in range(1, groups):
             rows = slice(step * share, (step + 1) * share)
-            total = (kept[i][:, :, rows] + got[i][:, :, rows].astype(F32)).astype(BF16)
             pairs = [(g, (g + step) % groups) for g in range(groups)]
-            sent.append(lax.ppermute(total, "ga", pairs))
+            for at, piece in enumerate(got[i]):
+                mine = kept[i][at * PIECE : at * PIECE + piece.shape[0]]
+                total = (mine[:, :, rows] + piece[:, :, rows].astype(F32)).astype(BF16)
+                sent.append(lax.ppermute(total, "ga", pairs))
         terms.append(sent)
 
     def finish(i, result):
@@ -331,13 +342,13 @@
             other = after(other, kept[i - 1])
         if i >= LAG_CORE:
             exchange(i - LAG_CORE)
-            other = after(other, got[i - LAG_CORE])
+            other = after(other, *got[i - LAG_CORE])
         if i >= LAG_GROUP:
             result = finish(i - LAG_GROUP, result)
             other = after(other, result)
         keep, give = couple(plan, ids, table, pots, waves, other, chunk, pools, cap, groups)
         kept.append(keep)
-        got.append(lax.ppermute(give, "pert", swap_cores))
+        got.append(swap(give))
     for i in range(len(terms), len(chunks)):
         exchange(i)
     for i in range(max(0, len(chunks) - LAG_GROUP), len(chunks)):
@@ -345,8 +356,8 @@
     return result.reshape(local_k, per_device, 2, share, bands)
 
 
-WINDOW = 1
 LAG_CORE, LAG_GROUP = 1, 2
+PIECE = 3
 
 
 def solution(mesh):

time: 165 us -> 138 us (0.84)
  waiting for transfers between devices: 74.1 us -> 35.1 us
  local copies, waits for them, and re-layouts: 7.7 us -> 17.4 us
  Pallas kernels: 54 us -> 61.4 us
  starting transfers between devices: 20.7 us -> 16.6 us
    all_to_all x3 -> x0, waiting for transfers between devices: 29.7 us -> none  [body(): landed.append(lax.all_to_all(give, 'pool', 0, 0, tiled=True))]
    ppermute x4 -> x8, waiting for transfers between devices: 41.5 us -> 18.2 us  [exchange(): sent.append(lax.ppermute(total, 'ga', pairs))]
    all_to_all x3 -> x0, starting transfers between devices: 14.9 us -> none  [body(): landed.append(lax.all_to_all(give, 'pool', 0, 0, tiled=True))]
    ppermute x4 -> x12, waiting for transfers between devices: 2.91 us -> 16.9 us  [the longest x4 16.6 us: body(): landed.append(lax.ppermute(give, 'pool', pairs))]
    slice x0 -> x6, local copies, waits for them, and re-layouts: none -> 9.78 us  [swap(): give[first:first + PIECE]]
    ppermute x4 -> x12, starting transfers between devices: 0.15 us -> 7.02 us  [the longest x4 5.98 us: body(): landed.append(lax.ppermute(give, 'pool', pairs))]
    pallas_call x4 -> x5, Pallas kernels: 31.1 us -> 35.2 us  [couple(): pl.pallas_call(functools.partial(couple_kernel, shape), grid_spec=pltpu.P...]
    ppermute x4 -> x8, starting transfers between devices: 5.53 us -> 9.51 us  [exchange(): sent.append(lax.ppermute(total, 'ga', pairs))]
  transfers between devices with their start and end apart: 12 -> 21, of which waited for: 6 -> 8; matrix products, arithmetic and copies ran while one was open for 5% -> 12% of each run, Pallas kernels for 19% -> 37%
where the time goes in v4:
time: 138 us; the launch traced here: 136 us
  Pallas kernels  61.4 us (44%)
  waiting for transfers between devices  35.1 us (25%)
  local copies, waits for them, and re-layouts  17.4 us (13%)
  starting transfers between devices  16.6 us (12%)
  other arithmetic  5.29 us (4%)
    pallas_call x5, Pallas kernels, couple(): pl.pallas_call(functools.partial(couple_kernel, shape), grid_spec=pltpu.P...  35.2 us
    ppermute x8, waiting for transfers between devices, exchange(): sent.append(lax.ppermute(total, 'ga', pairs))  18.2 us
    ppermute x4, waiting for transfers between devices, body(): landed.append(lax.ppermute(give, 'pool', pairs))  16.6 us
    pallas_call x5, Pallas kernels, combine(): pl.pallas_call(functools.partial(combine_kernel, shape, scaling), grid_sp...  13.5 us
    pallas_call x4, Pallas kernels, pick(): pl.pallas_call(functools.partial(pick_kernel, (2 * pools + shift) * cap +...  11 us
    slice x6, local copies, waits for them, and re-layouts, swap(): give[first:first + PIECE]  9.78 us
    ppermute x8, starting transfers between devices, exchange(): sent.append(lax.ppermute(total, 'ga', pairs))  9.51 us
    ppermute x4, starting transfers between devices, body(): landed.append(lax.ppermute(give, 'pool', pairs))  5.98 us
  transfers between devices with their start and end apart: 21, of which 8 were waited for; matrix products, arithmetic and copies ran while one was open for 12% of the time, Pallas kernels for 37%

profile of v4, /device:TPU:0, one launch (start us, length us, event | category | flops | bytes accessed | tf_op | source)
XLA Modules:
  0.0 136.4 jit_solution(5666471153996099723)
XLA Ops:
  0.7 1.8 %plan.1 = s32[64]{0:T(128)} custom-call(s32[3]{0:T(128)} %pad_add_fusion.1.ids, s32[64]{0:T(128)} %partners.1), custom_call_target="tpu_custom_call" | custom-call | flops 1 | bytes 1024 | tf_op jit(solution)/shard_map/plan/pallas_call | solution.py:65
  2.5 3.0 %pick.4 = bf16[5,720,128]{2,1,0:T(8,128)(2,1)} custom-call(s32[64]{0:T(128)} %plan.1, s32[3]{0:T(128)} %pad_add_fusion.1.ids, bf16[32,720,128]{2,1,0:T(8,128)(2,1)} %bitcast.15), custom_call_target="tpu_custom_call" | custom-call | flops 1 | bytes 1024 | tf_op jit(solution)/shard_map/pick/pallas_call | solution.py:88
  5.5 3.1 %collective-permute-start.5 = (bf16[5,720,128]{2,1,0:T(8,128)(2,1)}, bf16[5,720,128]{2,1,0:T(8,128)(2,1)S(1)}, u32[]{:S(2)}, u32[]{:S(2)}) collective-permute-start(bf16[5,720,128]{2,1,0:T(8,128)(2,1)} %pick.4), channel_id=1, source_target_pairs={{0,4},{4,8},{8,12},{12,0},{1,5},{5,9},{9,13},{13,1},{2,6},{6,10},{... | collective-permute-start | bytes 2764808 | tf_op jit(solution)/shard_map/ppermute | solution.py:312
  10.8 2.0 %broadcast_in_dim.35.pots = f32[6,2,360,128]{3,2,1,0:T(8,128)} broadcast(f32[6,2,360]{2,1,0:T(2,128)S(1)} %broadcast_in_dim.34), dimensions={0,1,2} | broadcast | bytes 2229120 | tf_op jit(solution)/shard_map/broadcast_in_dim | solution.py:303
  12.8 8.5 %couple.5 = (f32[5,6,128,128]{3,2,1,0:T(8,128)}, bf16[5,6,128,128]{3,2,1,0:T(8,128)(2,1)}) custom-call(s32[64]{0:T(128)} %plan.1, s32[3]{0:T(128)} %pad_add_fusion.1.ids, bf16[240,240]{1,0:T(8,128)(2,1)} %maximum_maximum_fusion.table, f32[6,2,360,128]{3,2,1,0:T(8,128)} %broadcast_in_dim.35.pots, bf16[32,720,128]{2,1,0:T(8,128)(2,1)} %bitcast.16, ...), custom_call_target="tpu_custom_call" | custom-call | flops 1 | bytes 1024 | tf_op jit(solution)/shard_map/couple/pallas_call | solution.py:164
  21.3 1.9 %slice.78 = bf16[3,6,128,128]{3,2,1,0:T(8,128)(2,1)} slice(bf16[5,6,128,128]{3,2,1,0:T(8,128)(2,1)} %get-tuple-element.31), slice={[0:3], [0:6], [0:128], [0:128]} | slice | bytes 1179648 | tf_op jit(solution)/shard_map/slice | solution.py:320
  23.7 1.8 %slice.79 = bf16[2,6,128,128]{3,2,1,0:T(8,128)(2,1)} slice(bf16[5,6,128,128]{3,2,1,0:T(8,128)(2,1)} %get-tuple-element.31), slice={[3:5], [0:6], [0:128], [0:128]} | slice | bytes 786432 | tf_op jit(solution)/shard_map/slice | solution.py:320
  25.5 2.9 %pick.5 = bf16[5,720,128]{2,1,0:T(8,128)(2,1)} custom-call(s32[64]{0:T(128)} %plan.1, s32[3]{0:T(128)} %pad_add_fusion.1.ids, bf16[32,720,128]{2,1,0:T(8,128)(2,1)} %bitcast.18), custom_call_target="tpu_custom_call" | custom-call | flops 1 | bytes 1024 | tf_op jit(solution)/shard_map/pick/pallas_call | solution.py:88
  28.4 2.1 %collective-permute-start.10 = (bf16[5,720,128]{2,1,0:T(8,128)(2,1)}, bf16[5,720,128]{2,1,0:T(8,128)(2,1)}, u32[]{:S(2)}, u32[]{:S(2)}) collective-permute-start(bf16[5,720,128]{2,1,0:T(8,128)(2,1)} %pick.5), channel_id=1, source_target_pairs={{0,12},{4,0},{8,4},{12,8},{1,13},{5,1},{9,5},{13,9},{2,14},{6,2},{... | collective-permute-start | bytes 2764808 | tf_op jit(solution)/shard_map/ppermute | solution.py:312
  32.3 8.6 %couple.6 = (f32[5,6,128,128]{3,2,1,0:T(8,128)}, bf16[5,6,128,128]{3,2,1,0:T(8,128)(2,1)}) custom-call(s32[64]{0:T(128)} %plan.1, s32[3]{0:T(128)} %pad_add_fusion.1.ids, bf16[240,240]{1,0:T(8,128)(2,1)} %maximum_maximum_fusion.table, f32[6,2,360,128]{3,2,1,0:T(8,128)} %broadcast_in_dim.35.pots, bf16[32,720,128]{2,1,0:T(8,128)(2,1)} %bitcast.19, ...), custom_call_target="tpu_custom_call" | custom-call | flops 1 | bytes 1024 | tf_op jit(solution)/shard_map/couple/pallas_call | solution.py:164
  40.9 2.1 %slice.84 = bf16[3,6,128,128]{3,2,1,0:T(8,128)(2,1)} slice(bf16[5,6,128,128]{3,2,1,0:T(8,128)(2,1)} %get-tuple-element.35), slice={[0:3], [0:6], [0:128], [0:128]} | slice | bytes 1179648 | tf_op jit(solution)/shard_map/slice | solution.py:320
  43.8 1.5 %collective-permute-start.3 = (bf16[3,6,64,128]{3,2,1,0:T(8,128)(2,1)}, bf16[3,6,64,128]{3,2,1,0:T(8,128)(2,1)}, u32[]{:S(2)}, u32[]{:S(2)}) collective-permute-start(bf16[3,6,64,128]{3,2,1,0:T(8,128)(2,1)} %add_convert_fusion.3), channel_id=1, source_target_pairs={{0,2},{2,0},{1,3},{3,1},{4,6},{6,4},{5,7},{7,5},{8,10},{10,8},{9,1... | collective-permute-start | bytes 884744 | tf_op jit(solution)/shard_map/ppermute | solution.py:332
  47.2 2.6 %pick.6 = bf16[3,720,128]{2,1,0:T(8,128)(2,1)} custom-call(s32[64]{0:T(128)} %plan.1, s32[3]{0:T(128)} %pad_add_fusion.1.ids, bf16[32,720,128]{2,1,0:T(8,128)(2,1)} %bitcast.20), custom_call_target="tpu_custom_call" | custom-call | flops 1 | bytes 1024 | tf_op jit(solution)/shard_map/pick/pallas_call | solution.py:88
  49.9 7.7 %collective-permute-done.4.refs_4_ = bf16[2,6,64,128]{3,2,1,0:T(8,128)(2,1)S(1)} collective-permute-done((bf16[2,6,64,128]{3,2,1,0:T(8,128)(2,1)S(1)}, bf16[2,6,64,128]{3,2,1,0:T(8,128)(2,1)S(1)}, u32[]{:S(2)}, u32[]{:S(2)}) %collective-permute-start.4) | collective-permute-done | bytes 196640 | tf_op jit(solution)/shard_map/ppermute | solution.py:332
  58.3 3.0 %combine.5.refs_0_ = bf16[16,6,64,128]{3,2,1,0:T(8,128)(2,1)} custom-call(s32[64]{0:T(128)} %plan.1, f32[5,6,128,128]{3,2,1,0:T(8,128)} %get-tuple-element.30.refs_0_, bf16[3,6,128,128]{3,2,1,0:T(8,128)(2,1)} %copy-done.7, bf16[2,6,128,128]{3,2,1,0:T(8,128)(2,1)} %copy-done.12, bf16[3,6,64,128]{3,2,1,0:T(8,128)(2,1)} %collective-permute-done.3.refs_3_, ...), custom_call_target="tpu_custom_call" | custom-call | flops 1 | bytes 1024 | tf_op jit(solution)/shard_map/combine/pallas_call | solution.py:226
  62.1 7.8 %couple.7 = (f32[5,6,128,128]{3,2,1,0:T(8,128)}, bf16[5,6,128,128]{3,2,1,0:T(8,128)(2,1)}) custom-call(s32[64]{0:T(128)} %plan.1, s32[3]{0:T(128)} %pad_add_fusion.1.ids, bf16[240,240]{1,0:T(8,128)(2,1)} %maximum_maximum_fusion.table, f32[6,2,360,128]{3,2,1,0:T(8,128)} %broadcast_in_dim.35.pots, bf16[32,720,128]{2,1,0:T(8,128)(2,1)} %bitcast.21, ...), custom_call_target="tpu_custom_call" | custom-call | flops 1 | bytes 1024 | tf_op jit(solution)/shard_map/couple/pallas_call | solution.py:164
  69.9 2.0 %slice.90 = bf16[3,6,128,128]{3,2,1,0:T(8,128)(2,1)} slice(bf16[5,6,128,128]{3,2,1,0:T(8,128)(2,1)} %get-tuple-element.40), slice={[0:3], [0:6], [0:128], [0:128]} | slice | bytes 1179648 | tf_op jit(solution)/shard_map/slice | solution.py:320
  73.7 1.6 %collective-permute-start.8 = (bf16[3,6,64,128]{3,2,1,0:T(8,128)(2,1)}, bf16[3,6,64,128]{3,2,1,0:T(8,128)(2,1)}, u32[]{:S(2)}, u32[]{:S(2)}) collective-permute-start(bf16[3,6,64,128]{3,2,1,0:T(8,128)(2,1)} %add_convert_fusion.2), channel_id=1, source_target_pairs={{0,2},{2,0},{1,3},{3,1},{4,6},{6,4},{5,7},{7,5},{8,10},{10,8},{9,1... | collective-permute-start | bytes 884744 | tf_op jit(solution)/shard_map/ppermute | solution.py:332
  76.2 2.4 %pick.7 = bf16[2,720,128]{2,1,0:T(8,128)(2,1)} custom-call(s32[64]{0:T(128)} %plan.1, s32[3]{0:T(128)} %pad_add_fusion.1.ids, bf16[32,720,128]{2,1,0:T(8,128)(2,1)} %bitcast.22), custom_call_target="tpu_custom_call" | custom-call | flops 1 | bytes 1024 | tf_op jit(solution)/shard_map/pick/pallas_call | solution.py:88
  78.6 9.2 %collective-permute-done.15.other = bf16[3,720,128]{2,1,0:T(8,128)(2,1)} collective-permute-done((bf16[3,720,128]{2,1,0:T(8,128)(2,1)}, bf16[3,720,128]{2,1,0:T(8,128)(2,1)}, u32[]{:S(2)}, u32[]{:S(2)}) %collective-permute-start.15) | collective-permute-done | bytes 552992 | tf_op jit(solution)/shard_map/ppermute | solution.py:312
  88.5 3.0 %combine.6.refs_0_ = bf16[16,6,64,128]{3,2,1,0:T(8,128)(2,1)} custom-call(s32[64]{0:T(128)} %plan.1, bf16[16,6,64,128]{3,2,1,0:T(8,128)(2,1)} %combine.5.refs_0_, f32[5,6,128,128]{3,2,1,0:T(8,128)} %get-tuple-element.34.refs_1_, bf16[3,6,128,128]{3,2,1,0:T(8,128)(2,1)} %copy-done.4, ...), custom_call_target="tpu_custom_call", output_to_operand_aliasing={{}: (1, {})} | custom-call | flops 1 | bytes 1024 | tf_op jit(solution)/shard_map/combine/pallas_call | solution.py:226
  91.5 6.6 %couple.8 = (f32[3,6,128,128]{3,2,1,0:T(8,128)}, bf16[3,6,128,128]{3,2,1,0:T(8,128)(2,1)}) custom-call(s32[64]{0:T(128)} %plan.1, s32[3]{0:T(128)} %pad_add_fusion.1.ids, bf16[240,240]{1,0:T(8,128)(2,1)} %maximum_maximum_fusion.table, f32[6,2,360,128]{3,2,1,0:T(8,128)} %broadcast_in_dim.35.pots, bf16[32,720,128]{2,1,0:T(8,128)(2,1)} %bitcast.23, ...), custom_call_target="tpu_custom_call" | custom-call | flops 1 | bytes 1024 | tf_op jit(solution)/shard_map/couple/pallas_call | solution.py:164
  98.2 1.6 %collective-permute-start.13 = (bf16[3,6,64,128]{3,2,1,0:T(8,128)(2,1)S(1)}, bf16[3,6,64,128]{3,2,1,0:T(8,128)(2,1)S(1)}, u32[]{:S(2)}, u32[]{:S(2)}) collective-permute-start(bf16[3,6,64,128]{3,2,1,0:T(8,128)(2,1)S(1)} %add_convert_fusion.1), channel_id=1, source_target_pairs={{0,2},{2,0},{1,3},{3,1},{4,6},{6,4},{5,7},{7,5},{8,10},{10,8},{9,1... | collective-permute-start | bytes 884744 | tf_op jit(solution)/shard_map/ppermute | solution.py:332
  100.4 6.7 %collective-permute-done.18.other = bf16[2,720,128]{2,1,0:T(8,128)(2,1)S(1)} collective-permute-done((bf16[2,720,128]{2,1,0:T(8,128)(2,1)}, bf16[2,720,128]{2,1,0:T(8,128)(2,1)S(1)}, u32[]{:S(2)}, u32[]{:S(2)}) %collective-permute-start.18) | collective-permute-done | bytes 368672 | tf_op jit(solution)/shard_map/ppermute | solution.py:312
  107.1 4.8 %collective-permute-done.14.refs_5_ = bf16[2,6,64,128]{3,2,1,0:T(8,128)(2,1)S(1)} collective-permute-done((bf16[2,6,64,128]{3,2,1,0:T(8,128)(2,1)S(1)}, bf16[2,6,64,128]{3,2,1,0:T(8,128)(2,1)S(1)}, u32[]{:S(2)}, u32[]{:S(2)}) %collective-permute-start.14) | collective-permute-done | bytes 196640 | tf_op jit(solution)/shard_map/ppermute | solution.py:332
  113.3 2.9 %combine.7.refs_0_ = bf16[16,6,64,128]{3,2,1,0:T(8,128)(2,1)} custom-call(s32[64]{0:T(128)} %plan.1, bf16[16,6,64,128]{3,2,1,0:T(8,128)(2,1)} %combine.6.refs_0_, f32[5,6,128,128]{3,2,1,0:T(8,128)} %get-tuple-element.39.refs_1_, bf16[3,6,128,128]{3,2,1,0:T(8,128)(2,1)} %copy-done.5, ...), custom_call_target="tpu_custom_call", output_to_operand_aliasing={{}: (1, {})} | custom-call | flops 1 | bytes 1024 | tf_op jit(solution)/shard_map/combine/pallas_call | solution.py:226
  116.3 3.8 %couple.9 = (f32[2,6,128,128]{3,2,1,0:T(8,128)}, bf16[2,6,128,128]{3,2,1,0:T(8,128)(2,1)}) custom-call(s32[64]{0:T(128)} %plan.1, s32[3]{0:T(128)} %pad_add_fusion.1.ids, bf16[240,240]{1,0:T(8,128)(2,1)} %maximum_maximum_fusion.table, f32[6,2,360,128]{3,2,1,0:T(8,128)} %broadcast_in_dim.35.pots, bf16[32,720,128]{2,1,0:T(8,128)(2,1)} %bitcast.24, ...), custom_call_target="tpu_custom_call" | custom-call | flops 1 | bytes 1024 | tf_op jit(solution)/shard_map/couple/pallas_call | solution.py:164
  120.2 1.6 %collective-permute-start.17 = (bf16[3,6,64,128]{3,2,1,0:T(8,128)(2,1)S(1)}, bf16[3,6,64,128]{3,2,1,0:T(8,128)(2,1)S(1)}, u32[]{:S(2)}, u32[]{:S(2)}) collective-permute-start(bf16[3,6,64,128]{3,2,1,0:T(8,128)(2,1)S(1)} %add_convert_fusion), channel_id=1, source_target_pairs={{0,2},{2,0},{1,3},{3,1},{4,6},{6,4},{5,7},{7,5},{8,10},{10,8},{9,1... | collective-permute-start | bytes 884744 | tf_op jit(solution)/shard_map/ppermute | solution.py:332
  123.2 1.6 %collective-permute-start.20 = (bf16[2,6,64,128]{3,2,1,0:T(8,128)(2,1)S(1)}, bf16[2,6,64,128]{3,2,1,0:T(8,128)(2,1)S(1)}, u32[]{:S(2)}, u32[]{:S(2)}) collective-permute-start(bf16[2,6,64,128]{3,2,1,0:T(8,128)(2,1)S(1)} %add_convert_fusion.4), channel_id=1, source_target_pairs={{0,2},{2,0},{1,3},{3,1},{4,6},{6,4},{5,7},{7,5},{8,10},{10,8},{9,1... | collective-permute-start | bytes 589832 | tf_op jit(solution)/shard_map/ppermute | solution.py:332
  124.7 5.3 %collective-permute-done.17.refs_3_ = bf16[3,6,64,128]{3,2,1,0:T(8,128)(2,1)S(1)} collective-permute-done((bf16[3,6,64,128]{3,2,1,0:T(8,128)(2,1)S(1)}, bf16[3,6,64,128]{3,2,1,0:T(8,128)(2,1)S(1)}, u32[]{:S(2)}, u32[]{:S(2)}) %collective-permute-start.17) | collective-permute-done | bytes 294944 | tf_op jit(solution)/shard_map/ppermute | solution.py:332
  130.8 2.7 %combine.8.refs_0_ = bf16[16,6,64,128]{3,2,1,0:T(8,128)(2,1)} custom-call(s32[64]{0:T(128)} %plan.1, bf16[16,6,64,128]{3,2,1,0:T(8,128)(2,1)} %combine.7.refs_0_, f32[3,6,128,128]{3,2,1,0:T(8,128)} %get-tuple-element.45.refs_1_, bf16[3,6,128,128]{3,2,1,0:T(8,128)(2,1)} %copy-done.6, bf16[3,6,64,128]{3,2,1,0:T(8,128)(2,1)} %copy-done.16), custom_call_target="tpu_custom_call", output_to_operand_aliasing={{}: (1, {})} | custom-call | flops 1 | bytes 1024 | tf_op jit(solution)/shard_map/combine/pallas_call | solution.py:226
  134.5 1.8 %combine.9 = bf16[16,6,64,128]{3,2,1,0:T(8,128)(2,1)} custom-call(s32[64]{0:T(128)} %plan.1, bf16[16,6,64,128]{3,2,1,0:T(8,128)(2,1)} %combine.8.refs_0_, f32[2,6,128,128]{3,2,1,0:T(8,128)} %get-tuple-element.51.refs_1_, bf16[2,6,128,128]{3,2,1,0:T(8,128)(2,1)} %copy-done.9, bf16[2,6,64,128]{3,2,1,0:T(8,128)(2,1)} %copy-done.17), custom_call_target="tpu_custom_call", output_to_operand_aliasing={{}: (1, {})} | custom-call | flops 1 | bytes 1024 | tf_op jit(solution)/shard_map/combine/pallas_call | solution.py:226
  (107 shorter events, 18.2 us)
Async XLA Ops:
  2.5 6.8 %copy-start.22 = (s32[6]{0:T(128)S(1)}, s32[6]{0:T(128)}, u32[]{:S(2)}) copy-start(s32[6]{0:T(128)} %param.6) | copy-start | bytes 76
  5.5 25.7 %collective-permute-start.5 = (bf16[5,720,128]{2,1,0:T(8,128)(2,1)}, bf16[5,720,128]{2,1,0:T(8,128)(2,1)S(1)}, u32[]{:S(2)}, u32[]{:S(2)}) collective-permute-start(bf16[5,720,128]{2,1,0:T(8,128)(2,1)} %pick.4), channel_id=1, source_target_pairs={{0,4},{4,8},{8,12},{12,0},{1,5},{5,9},{9,13},{13,1},{2,6},{6,10},{... | collective-permute-start | bytes 2764808 | tf_op jit(solution)/shard_map/ppermute | solution.py:312
  8.6 1.7 %collective-permute-start = (f32[3,3,240]{2,1,0:T(4,128)S(1)}, f32[3,3,240]{2,1,0:T(4,128)S(1)}, u32[]{:S(2)}, u32[]{:S(2)}) collective-permute-start(f32[3,3,240]{2,1,0:T(4,128)S(1)} %bitcast.29), channel_id=1, source_target_pairs={{0,1},{1,0},{2,3},{3,2},{4,5},{5,4},{6,7},{7,6},{8,9},{9,8},{10,11... | collective-permute-start | bytes 25928 | tf_op jit(solution)/shard_map/ppermute | solution.py:289
  23.2 8.1 %collective-permute-start.1 = (bf16[3,6,128,128]{3,2,1,0:T(8,128)(2,1)}, bf16[3,6,128,128]{3,2,1,0:T(8,128)(2,1)S(1)}, u32[]{:S(2)}, u32[]{:S(2)}) collective-permute-start(bf16[3,6,128,128]{3,2,1,0:T(8,128)(2,1)} %slice.78), channel_id=1, source_target_pairs={{0,1},{1,0},{2,3},{3,2},{4,5},{5,4},{6,7},{7,6},{8,9},{9,8},{10,11... | collective-permute-start | bytes 1769480 | tf_op jit(solution)/shard_map/ppermute | solution.py:320
  25.4 5.8 %collective-permute-start.2 = (bf16[2,6,128,128]{3,2,1,0:T(8,128)(2,1)}, bf16[2,6,128,128]{3,2,1,0:T(8,128)(2,1)S(1)}, u32[]{:S(2)}, u32[]{:S(2)}) collective-permute-start(bf16[2,6,128,128]{3,2,1,0:T(8,128)(2,1)} %slice.79), channel_id=1, source_target_pairs={{0,1},{1,0},{2,3},{3,2},{4,5},{5,4},{6,7},{7,6},{8,9},{9,8},{10,11... | collective-permute-start | bytes 1179656 | tf_op jit(solution)/shard_map/ppermute | solution.py:320
  28.4 32.9 %collective-permute-start.10 = (bf16[5,720,128]{2,1,0:T(8,128)(2,1)}, bf16[5,720,128]{2,1,0:T(8,128)(2,1)}, u32[]{:S(2)}, u32[]{:S(2)}) collective-permute-start(bf16[5,720,128]{2,1,0:T(8,128)(2,1)} %pick.5), channel_id=1, source_target_pairs={{0,12},{4,0},{8,4},{12,8},{1,13},{5,1},{9,5},{13,9},{2,14},{6,2},{... | collective-permute-start | bytes 2764808 | tf_op jit(solution)/shard_map/ppermute | solution.py:312
  31.3 11.7 %copy-start.2 = (f32[5,6,128,128]{3,2,1,0:T(8,128)S(1)}, f32[5,6,128,128]{3,2,1,0:T(8,128)}, u32[]{:S(2)}) copy-start(f32[5,6,128,128]{3,2,1,0:T(8,128)} %get-tuple-element.30.refs_0_) | copy-start | bytes 5898244
  31.3 9.6 %copy-start.12 = (bf16[2,6,128,128]{3,2,1,0:T(8,128)(2,1)}, bf16[2,6,128,128]{3,2,1,0:T(8,128)(2,1)S(1)}, u32[]{:S(2)}) copy-start(bf16[2,6,128,128]{3,2,1,0:T(8,128)(2,1)S(1)} %collective-permute-done.2.refs_2_) | copy-start | bytes 1179652
  32.3 10.7 %copy-start.7 = (bf16[3,6,128,128]{3,2,1,0:T(8,128)(2,1)}, bf16[3,6,128,128]{3,2,1,0:T(8,128)(2,1)S(1)}, u32[]{:S(2)}) copy-start(bf16[3,6,128,128]{3,2,1,0:T(8,128)(2,1)S(1)} %collective-permute-done.1.refs_1_) | copy-start | bytes 1769476
  43.0 19.2 %collective-permute-start.6 = (bf16[3,6,128,128]{3,2,1,0:T(8,128)(2,1)}, bf16[3,6,128,128]{3,2,1,0:T(8,128)(2,1)S(1)}, u32[]{:S(2)}, u32[]{:S(2)}) collective-permute-start(bf16[3,6,128,128]{3,2,1,0:T(8,128)(2,1)} %slice.84), channel_id=1, source_target_pairs={{0,1},{1,0},{2,3},{3,2},{4,5},{5,4},{6,7},{7,6},{8,9},{9,8},{10,11... | collective-permute-start | bytes 1769480 | tf_op jit(solution)/shard_map/ppermute | solution.py:320
  43.8 13.8 %collective-permute-start.3 = (bf16[3,6,64,128]{3,2,1,0:T(8,128)(2,1)}, bf16[3,6,64,128]{3,2,1,0:T(8,128)(2,1)}, u32[]{:S(2)}, u32[]{:S(2)}) collective-permute-start(bf16[3,6,64,128]{3,2,1,0:T(8,128)(2,1)} %add_convert_fusion.3), channel_id=1, source_target_pairs={{0,2},{2,0},{1,3},{3,1},{4,6},{6,4},{5,7},{7,5},{8,10},{10,8},{9,1... | collective-permute-start | bytes 884744 | tf_op jit(solution)/shard_map/ppermute | solution.py:332
  46.3 15.8 %collective-permute-start.7 = (bf16[2,6,128,128]{3,2,1,0:T(8,128)(2,1)S(1)}, bf16[2,6,128,128]{3,2,1,0:T(8,128)(2,1)S(1)}, u32[]{:S(2)}, u32[]{:S(2)}) collective-permute-start(bf16[2,6,128,128]{3,2,1,0:T(8,128)(2,1)S(1)} %slice.85), channel_id=1, source_target_pairs={{0,1},{1,0},{2,3},{3,2},{4,5},{5,4},{6,7},{7,6},{8,9},{9,8},{10,11... | collective-permute-start | bytes 1179656 | tf_op jit(solution)/shard_map/ppermute | solution.py:320
  46.6 11.0 %collective-permute-start.4 = (bf16[2,6,64,128]{3,2,1,0:T(8,128)(2,1)S(1)}, bf16[2,6,64,128]{3,2,1,0:T(8,128)(2,1)S(1)}, u32[]{:S(2)}, u32[]{:S(2)}) collective-permute-start(bf16[2,6,64,128]{3,2,1,0:T(8,128)(2,1)S(1)} %add_convert_fusion.7), channel_id=1, source_target_pairs={{0,2},{2,0},{1,3},{3,1},{4,6},{6,4},{5,7},{7,5},{8,10},{10,8},{9,1... | collective-permute-start | bytes 589832 | tf_op jit(solution)/shard_map/ppermute | solution.py:332
  61.3 26.4 %collective-permute-start.15 = (bf16[3,720,128]{2,1,0:T(8,128)(2,1)}, bf16[3,720,128]{2,1,0:T(8,128)(2,1)}, u32[]{:S(2)}, u32[]{:S(2)}) collective-permute-start(bf16[3,720,128]{2,1,0:T(8,128)(2,1)} %pick.6), channel_id=1, source_target_pairs={{0,8},{4,12},{8,0},{12,4},{1,9},{5,13},{9,1},{13,5},{2,10},{6,14},... | collective-permute-start | bytes 1658888 | tf_op jit(solution)/shard_map/ppermute | solution.py:312
  62.1 9.8 %copy-start = (f32[5,6,128,128]{3,2,1,0:T(8,128)S(1)}, f32[5,6,128,128]{3,2,1,0:T(8,128)}, u32[]{:S(2)}) copy-start(f32[5,6,128,128]{3,2,1,0:T(8,128)} %get-tuple-element.34.refs_1_) | copy-start | bytes 5898244
  62.1 13.4 %copy-start.10 = (bf16[2,6,128,128]{3,2,1,0:T(8,128)(2,1)}, bf16[2,6,128,128]{3,2,1,0:T(8,128)(2,1)S(1)}, u32[]{:S(2)}) copy-start(bf16[2,6,128,128]{3,2,1,0:T(8,128)(2,1)S(1)} %collective-permute-done.7.refs_3_) | copy-start | bytes 1179652
  62.1 9.8 %copy-start.4 = (bf16[3,6,128,128]{3,2,1,0:T(8,128)(2,1)}, bf16[3,6,128,128]{3,2,1,0:T(8,128)(2,1)S(1)}, u32[]{:S(2)}) copy-start(bf16[3,6,128,128]{3,2,1,0:T(8,128)(2,1)S(1)} %collective-permute-done.6.refs_2_) | copy-start | bytes 1769476
  71.9 19.6 %collective-permute-start.11 = (bf16[3,6,128,128]{3,2,1,0:T(8,128)(2,1)}, bf16[3,6,128,128]{3,2,1,0:T(8,128)(2,1)S(1)}, u32[]{:S(2)}, u32[]{:S(2)}) collective-permute-start(bf16[3,6,128,128]{3,2,1,0:T(8,128)(2,1)} %slice.90), channel_id=1, source_target_pairs={{0,1},{1,0},{2,3},{3,2},{4,5},{5,4},{6,7},{7,6},{8,9},{9,8},{10,11... | collective-permute-start | bytes 1769480 | tf_op jit(solution)/shard_map/ppermute | solution.py:320
  73.7 14.1 %collective-permute-start.8 = (bf16[3,6,64,128]{3,2,1,0:T(8,128)(2,1)}, bf16[3,6,64,128]{3,2,1,0:T(8,128)(2,1)}, u32[]{:S(2)}, u32[]{:S(2)}) collective-permute-start(bf16[3,6,64,128]{3,2,1,0:T(8,128)(2,1)} %add_convert_fusion.2), channel_id=1, source_target_pairs={{0,2},{2,0},{1,3},{3,1},{4,6},{6,4},{5,7},{7,5},{8,10},{10,8},{9,1... | collective-permute-start | bytes 884744 | tf_op jit(solution)/shard_map/ppermute | solution.py:332
  75.3 16.2 %collective-permute-start.12 = (bf16[2,6,128,128]{3,2,1,0:T(8,128)(2,1)S(1)}, bf16[2,6,128,128]{3,2,1,0:T(8,128)(2,1)S(1)}, u32[]{:S(2)}, u32[]{:S(2)}) collective-permute-start(bf16[2,6,128,128]{3,2,1,0:T(8,128)(2,1)S(1)} %slice.91), channel_id=1, source_target_pairs={{0,1},{1,0},{2,3},{3,2},{4,5},{5,4},{6,7},{7,6},{8,9},{9,8},{10,11... | collective-permute-start | bytes 1179656 | tf_op jit(solution)/shard_map/ppermute | solution.py:320
  75.6 12.2 %collective-permute-start.9 = (bf16[2,6,64,128]{3,2,1,0:T(8,128)(2,1)S(1)}, bf16[2,6,64,128]{3,2,1,0:T(8,128)(2,1)S(1)}, u32[]{:S(2)}, u32[]{:S(2)}) collective-permute-start(bf16[2,6,64,128]{3,2,1,0:T(8,128)(2,1)S(1)} %add_convert_fusion.6), channel_id=1, source_target_pairs={{0,2},{2,0},{1,3},{3,1},{4,6},{6,4},{5,7},{7,5},{8,10},{10,8},{9,1... | collective-permute-start | bytes 589832 | tf_op jit(solution)/shard_map/ppermute | solution.py:332
  87.8 19.4 %collective-permute-start.18 = (bf16[2,720,128]{2,1,0:T(8,128)(2,1)}, bf16[2,720,128]{2,1,0:T(8,128)(2,1)S(1)}, u32[]{:S(2)}, u32[]{:S(2)}) collective-permute-start(bf16[2,720,128]{2,1,0:T(8,128)(2,1)} %pick.7), channel_id=1, source_target_pairs={{0,8},{4,12},{8,0},{12,4},{1,9},{5,13},{9,1},{13,5},{2,10},{6,14},... | collective-permute-start | bytes 1105928 | tf_op jit(solution)/shard_map/ppermute | solution.py:312
  91.5 6.6 %copy-start.1 = (f32[5,6,128,128]{3,2,1,0:T(8,128)S(1)}, f32[5,6,128,128]{3,2,1,0:T(8,128)}, u32[]{:S(2)}) copy-start(f32[5,6,128,128]{3,2,1,0:T(8,128)} %get-tuple-element.39.refs_1_) | copy-start | bytes 5898244
  91.5 8.3 %copy-start.11 = (bf16[2,6,128,128]{3,2,1,0:T(8,128)(2,1)}, bf16[2,6,128,128]{3,2,1,0:T(8,128)(2,1)S(1)}, u32[]{:S(2)}) copy-start(bf16[2,6,128,128]{3,2,1,0:T(8,128)(2,1)S(1)} %collective-permute-done.12.refs_3_) | copy-start | bytes 1179652
  98.1 18.2 %collective-permute-start.16 = (bf16[3,6,128,128]{3,2,1,0:T(8,128)(2,1)}, bf16[3,6,128,128]{3,2,1,0:T(8,128)(2,1)S(1)}, u32[]{:S(2)}, u32[]{:S(2)}) collective-permute-start(bf16[3,6,128,128]{3,2,1,0:T(8,128)(2,1)} %get-tuple-element.46), channel_id=1, source_target_pairs={{0,1},{1,0},{2,3},{3,2},{4,5},{5,4},{6,7},{7,6},{8,9},{9,8},{10,11... | collective-permute-start | bytes 1769480 | tf_op jit(solution)/shard_map/ppermute | solution.py:320
  98.2 13.7 %collective-permute-start.13 = (bf16[3,6,64,128]{3,2,1,0:T(8,128)(2,1)S(1)}, bf16[3,6,64,128]{3,2,1,0:T(8,128)(2,1)S(1)}, u32[]{:S(2)}, u32[]{:S(2)}) collective-permute-start(bf16[3,6,64,128]{3,2,1,0:T(8,128)(2,1)S(1)} %add_convert_fusion.1), channel_id=1, source_target_pairs={{0,2},{2,0},{1,3},{3,1},{4,6},{6,4},{5,7},{7,5},{8,10},{10,8},{9,1... | collective-permute-start | bytes 884744 | tf_op jit(solution)/shard_map/ppermute | solution.py:332
  99.8 12.1 %collective-permute-start.14 = (bf16[2,6,64,128]{3,2,1,0:T(8,128)(2,1)S(1)}, bf16[2,6,64,128]{3,2,1,0:T(8,128)(2,1)S(1)}, u32[]{:S(2)}, u32[]{:S(2)}) collective-permute-start(bf16[2,6,64,128]{3,2,1,0:T(8,128)(2,1)S(1)} %add_convert_fusion.5), channel_id=1, source_target_pairs={{0,2},{2,0},{1,3},{3,1},{4,6},{6,4},{5,7},{7,5},{8,10},{10,8},{9,1... | collective-permute-start | bytes 589832 | tf_op jit(solution)/shard_map/ppermute | solution.py:332
  107.1 9.1 %copy-start.14 = (bf16[2,720,128]{2,1,0:T(8,128)(2,1)}, bf16[2,720,128]{2,1,0:T(8,128)(2,1)S(1)}, u32[]{:S(2)}) copy-start(bf16[2,720,128]{2,1,0:T(8,128)(2,1)S(1)} %collective-permute-done.18.other) | copy-start | bytes 1105924
  120.1 1.9 %collective-permute-start.19 = (bf16[2,6,128,128]{3,2,1,0:T(8,128)(2,1)}, bf16[2,6,128,128]{3,2,1,0:T(8,128)(2,1)S(1)}, u32[]{:S(2)}, u32[]{:S(2)}) collective-permute-start(bf16[2,6,128,128]{3,2,1,0:T(8,128)(2,1)} %get-tuple-element.52), channel_id=1, source_target_pairs={{0,1},{1,0},{2,3},{3,2},{4,5},{5,4},{6,7},{7,6},{8,9},{9,8},{10,11... | collective-permute-start | bytes 1179656 | tf_op jit(solution)/shard_map/ppermute | solution.py:320
  120.2 9.9 %collective-permute-start.17 = (bf16[3,6,64,128]{3,2,1,0:T(8,128)(2,1)S(1)}, bf16[3,6,64,128]{3,2,1,0:T(8,128)(2,1)S(1)}, u32[]{:S(2)}, u32[]{:S(2)}) collective-permute-start(bf16[3,6,64,128]{3,2,1,0:T(8,128)(2,1)S(1)} %add_convert_fusion), channel_id=1, source_target_pairs={{0,2},{2,0},{1,3},{3,1},{4,6},{6,4},{5,7},{7,5},{8,10},{10,8},{9,1... | collective-permute-start | bytes 884744 | tf_op jit(solution)/shard_map/ppermute | solution.py:332
  122.0 11.5 %copy-start.9 = (bf16[2,6,128,128]{3,2,1,0:T(8,128)(2,1)}, bf16[2,6,128,128]{3,2,1,0:T(8,128)(2,1)S(1)}, u32[]{:S(2)}) copy-start(bf16[2,6,128,128]{3,2,1,0:T(8,128)(2,1)S(1)} %collective-permute-done.19.refs_2_) | copy-start | bytes 1179652
  123.2 10.7 %collective-permute-start.20 = (bf16[2,6,64,128]{3,2,1,0:T(8,128)(2,1)S(1)}, bf16[2,6,64,128]{3,2,1,0:T(8,128)(2,1)S(1)}, u32[]{:S(2)}, u32[]{:S(2)}) collective-permute-start(bf16[2,6,64,128]{3,2,1,0:T(8,128)(2,1)S(1)} %add_convert_fusion.4), channel_id=1, source_target_pairs={{0,2},{2,0},{1,3},{3,1},{4,6},{6,4},{5,7},{7,5},{8,10},{10,8},{9,1... | collective-permute-start | bytes 589832 | tf_op jit(solution)/shard_map/ppermute | solution.py:332
  (12 other events, 31.2 us)

commit v5 on v4

--- a/solution.py
+++ b/solution.py
@@ -112,8 +112,13 @@
     return [jnp.concatenate(part, axis=0).astype(BF16) for part in parts]
 
 
-def couple_kernel(shape, plan, ids, table, pots, own, other, keep, give):
-    number, first, groups, z_points = shape
+def piece_of(count):
+    return max(1, count // 2)
+
+
+def couple_kernel(shape, plan, ids, table, pots, own, other, keep, *rest):
+    number, first, size, groups, z_points = shape
+    gives, hold = rest[:-1], rest[-1]
 
     @pl.when(first + pl.program_id(0) < plan[number])
     def _():
@@ -143,7 +148,13 @@
                         keep[0, 2 * j + part, pl.ds(starts[g], share), :] = rows
                     else:
                         place = 2 * (j - mine) + part
-                        give[0, place, pl.ds(starts[g], share), :] = rows.astype(BF16)
+                        hold[place, pl.ds(starts[g], share), :] = rows.astype(BF16)
+
+        for at, give in enumerate(gives):
+
+            @pl.when(pl.program_id(0) // size == at)
+            def _(give=give):
+                give[0] = hold[...]
 
 
 def couple(plan, ids, table, pots, waves, other, chunk, pools, cap, groups):
@@ -159,8 +170,10 @@
         )
     else:
         other_block = pl.BlockSpec(block, lambda i, plan, ids: (i, 0, 0))
-    out_block = pl.BlockSpec((1, parts, bands, bands), lambda i, plan, ids: (i, 0, 0, 0))
-    shape = (3 * pools * cap + shift, first, groups, table.shape[0] // 2)
+    out_block = (1, parts, bands, bands)
+    size = piece_of(count)
+    pieces = [(at, min(size, count - at)) for at in range(0, count, size)]
+    shape = (3 * pools * cap + shift, first, size, groups, table.shape[0] // 2)
     return pl.pallas_call(
         functools.partial(couple_kernel, shape),
         grid_spec=pltpu.PrefetchScalarGridSpec(
@@ -171,11 +184,17 @@
                 pl.BlockSpec(pots.shape, lambda i, plan, ids: (0, 0, 0, 0)),
                 own_block, other_block,
             ],
-            out_specs=[out_block] * 2,
+            out_specs=[pl.BlockSpec(out_block, lambda i, plan, ids: (i, 0, 0, 0))] + [
+                pl.BlockSpec(
+                    out_block,
+                    lambda i, plan, ids, at=at, size=size: (jnp.clip(i - at, 0, size - 1), 0, 0, 0),
+                )
+                for at, size in pieces
+            ],
+            scratch_shapes=[pltpu.VMEM((parts, bands, bands), BF16)],
         ),
-        out_shape=[
-            jax.ShapeDtypeStruct((count, parts, bands, bands), F32),
-            jax.ShapeDtypeStruct((count, parts, bands, bands), BF16),
+        out_shape=[jax.ShapeDtypeStruct((count, parts, bands, bands), F32)] + [
+            jax.ShapeDtypeStruct((size, parts, bands, bands), BF16) for _, size in pieces
         ],
         compiler_params=PARAMS,
         cost_estimate=LIGHT,
@@ -183,56 +202,59 @@
     )(plan, ids, table, pots, waves, other)
 
 
-def combine_kernel(shape, scaling, plan, *refs):
-    number, base, first, total, pieces, others = shape
+def combine_kernel(shapes, others, scaling, plan, *refs):
     result, stage, sems = refs[-3:]
-    summands = refs[-3 - 1 - pieces * (1 + others) : -3]
-    size = summands[1].shape[0]
+    terms = list(refs[-3 - sum(1 + shape[4] + others for shape in shapes) : -3])
+    blocks = []
+    for number, base, first, count, pieces in shapes:
+        kept = terms.pop(0)
+        added = [([terms.pop(0) for _ in range(pieces)], piece_of(count))]
+        added += [([terms.pop(0)], count) for _ in range(others)]
+        for i in range(count):
+            blocks.append((number, base + i, first + i, kept, added, i))
 
     def each(action):
-        for i in range(total):
-
-            @pl.when(first + i < plan[number])
-            def _(i=i):
-                action(i, pltpu.make_async_copy(
-                    stage.at[i], result.at[plan[base + i]], sems.at[i]
-                ))
-
-    def add(i, copy):
-        value = summands[0][i]
-        for group in range(1 + others):
-            value = value + summands[1 + group * pieces + i // size][i % size].astype(F32)
-        stage[i] = (value * scaling).astype(BF16)
+        for at, (number, entry, slot, kept, added, i) in enumerate(blocks):
+
+            @pl.when(slot < plan[number])
+            def _(at=at, entry=entry, kept=kept, added=added, i=i):
+                copy = pltpu.make_async_copy(stage.at[at], result.at[plan[entry]], sems.at[at])
+                action(at, copy, kept, added, i)
+
+    def add(at, copy, kept, added, i):
+        value = kept[i]
+        for pieces, size in added:
+            value = value + pieces[i // size][i % size].astype(F32)
+        stage[at] = (value * scaling).astype(BF16)
         copy.start()
 
     each(add)
-    each(lambda i, copy: copy.wait())
-
-
-def combine(plan, before, kept, got, arrived, local_k, chunk, pools, cap, scaling):
-    shift, first, count = chunk
-    _, parts, _, bands = kept.shape
-    share = arrived[0].shape[2]
-    terms = [kept, *got, *arrived]
+    each(lambda at, copy, kept, added, i: copy.wait())
+
+
+def combine(plan, before, parcels, local_k, pools, cap, scaling):
+    terms, shapes, total = [], [], 0
+    for (shift, first, count), kept, got, arrived in parcels:
+        terms += [kept, *got, *arrived]
+        shapes.append((3 * pools * cap + shift, shift * cap + first, first, count, len(got)))
+        total += count
+        others = len(arrived)
+        parts, share, bands = arrived[0].shape[1:]
     blocks = [
         pl.BlockSpec((term.shape[0], parts, share, bands), lambda i, plan: (0, 0, 0, 0))
         for term in terms
     ]
     operands = ([] if before is None else [before]) + terms
-    shape = (
-        3 * pools * cap + shift, shift * cap + first, first, count, len(got),
-        len(arrived) // len(got),
-    )
     return pl.pallas_call(
-        functools.partial(combine_kernel, shape, scaling),
+        functools.partial(combine_kernel, shapes, others, scaling),
         grid_spec=pltpu.PrefetchScalarGridSpec(
             num_scalar_prefetch=1,
             grid=(1,),
             in_specs=([] if before is None else [ANY]) + blocks,
             out_specs=ANY,
             scratch_shapes=[
-                pltpu.VMEM((count, parts, share, bands), BF16),
-                pltpu.SemaphoreType.DMA((count,)),
+                pltpu.VMEM((total, parts, share, bands), BF16),
+                pltpu.SemaphoreType.DMA((total,)),
             ],
         ),
         out_shape=jax.ShapeDtypeStruct((local_k, parts, share, bands), BF16),
@@ -248,16 +270,13 @@
 
 
 def transfers(pools, cap):
-    moves, waits = [], []
+    moves = []
     for s in range(1, (pools + 1) // 2):
-        for shift in (s, pools - s):
-            moves.append((shift, 0, cap))
-            waits.append(len(moves) - 3 if s > 1 else None)
+        moves += [(s, 0, cap), (pools - s, 0, cap)]
     if pools % 2 == 0:
         large = (3 * cap + 2) // 5
-        for first, count in ((0, large), (large, cap - large)):
-            moves.append((pools // 2, first, count))
-            waits.append(len(moves) - 2 if len(moves) > 1 else None)
+        moves += [(pools // 2, 0, large), (pools // 2, large, cap - large)]
+    waits = [i - WINDOW if i >= WINDOW else None for i in range(len(moves))]
     return moves, waits
 
 
@@ -315,28 +334,30 @@
     kept, got, terms = [], [], []
     result = None
 
-    def swap(give):
-        return [
-            lax.ppermute(give[first : first + PIECE], "pert", swap_cores)
-            for first in range(0, give.shape[0], PIECE)
-        ]
-
     def exchange(i):
         sent = []
+        size = piece_of(kept[i].shape[0])
         for step in range(1, groups):
             rows = slice(step * share, (step + 1) * share)
             pairs = [(g, (g + step) % groups) for g in range(groups)]
-            for at, piece in enumerate(got[i]):
-                mine = kept[i][at * PIECE : at * PIECE + piece.shape[0]]
-                total = (mine[:, :, rows] + piece[:, :, rows].astype(F32)).astype(BF16)
-                sent.append(lax.ppermute(total, "ga", pairs))
+            total = jnp.concatenate(
+                [
+                    kept[i][at * size : at * size + piece.shape[0], :, rows]
+                    + piece[:, :, rows].astype(F32)
+                    for at, piece in enumerate(got[i])
+                ],
+                axis=0,
+            )
+            sent.append(lax.ppermute(total.astype(BF16), "ga", pairs))
         terms.append(sent)
 
-    def finish(i, result):
-        return combine(
-            plan, result, kept[i], got[i], terms[i], local_k, chunks[i][0], pools, cap, scaling
-        )
-
+    finished = 0
+
+    def finish(until, result):
+        parcels = [(chunks[i][0], kept[i], got[i], terms[i]) for i in range(finished, until)]
+        return combine(plan, result, parcels, local_k, pools, cap, scaling)
+
+    last = len(chunks) - 1
     for i, (chunk, other) in enumerate(chunks):
         if i >= 1:
             other = after(other, kept[i - 1])
@@ -344,20 +365,23 @@
             exchange(i - LAG_CORE)
             other = after(other, *got[i - LAG_CORE])
         if i >= LAG_GROUP:
-            result = finish(i - LAG_GROUP, result)
+            other = after(other, *terms[i - LAG_GROUP])
+        if last - i in COMBINE and i - LAG_GROUP + 1 > finished:
+            result = finish(i - LAG_GROUP + 1, result)
+            finished = i - LAG_GROUP + 1
             other = after(other, result)
-        keep, give = couple(plan, ids, table, pots, waves, other, chunk, pools, cap, groups)
+        keep, *gives_now = couple(plan, ids, table, pots, waves, other, chunk, pools, cap, groups)
         kept.append(keep)
-        got.append(swap(give))
+        got.append([lax.ppermute(give, "pert", swap_cores) for give in gives_now])
     for i in range(len(terms), len(chunks)):
         exchange(i)
-    for i in range(max(0, len(chunks) - LAG_GROUP), len(chunks)):
-        result = finish(i, result)
+    result = finish(len(chunks), result)
     return result.reshape(local_k, per_device, 2, share, bands)
 
 
 LAG_CORE, LAG_GROUP = 1, 2
-PIECE = 3
+WINDOW = 2
+COMBINE = (1,)
 
 
 def solution(mesh):

time: 138 us -> 135 us (0.978)
  starting transfers between devices: 16.6 us -> 29.6 us
  local copies, waits for them, and re-layouts: 17.4 us -> 4.92 us
  Pallas kernels: 61.4 us -> 56 us
  waiting for transfers between devices: 35.1 us -> 37.1 us
    ppermute x4, starting transfers between devices: 5.98 us -> 19 us  [body(): landed.append(lax.ppermute(give, 'pool', pairs))]
    slice x6 -> x0, local copies, waits for them, and re-layouts: 9.78 us -> none  [swap(): give[first:first + PIECE]]
    ppermute x4, waiting for transfers between devices: 16.6 us -> 24.9 us  [body(): landed.append(lax.ppermute(give, 'pool', pairs))]
    ppermute x16 -> x19, waiting for transfers between devices: 18.5 us -> 12.1 us  [the longest x5 10.5 us: exchange(): sent.append(lax.ppermute(total.astype(BF16), 'ga', pairs))]
    pallas_call x5 -> x2, Pallas kernels: 13.5 us -> 7.62 us  [combine(): pl.pallas_call(functools.partial(combine_kernel, shapes, others, scaling)...]
    convert_element_type x8 -> x0, other arithmetic: 3.08 us -> none  [exchange(): total = (mine[:, :, rows] + piece[:, :, rows].astype(F32)).astype(BF16)]
    unnamed x46 -> x52, local copies, waits for them, and re-layouts: 5.2 us -> 2.48 us
    another operation x2 -> x10, other arithmetic: 0.54 us -> 3.14 us
  transfers between devices with their start and end apart: 21 -> 24, of which waited for: 8 -> 8; matrix products, arithmetic and copies ran while one was open for 12% -> 6% of each run, Pallas kernels for 37% -> 32%
where the time goes in v5:
time: 135 us; the launch traced here: 134 us
  Pallas kernels  56 us (41%)
  waiting for transfers between devices  37.1 us (27%)
  starting transfers between devices  29.6 us (22%)
  other arithmetic  5.81 us (4%)
  local copies, waits for them, and re-layouts  4.92 us (4%)
    pallas_call x5, Pallas kernels, couple(): pl.pallas_call(functools.partial(couple_kernel, shape), grid_spec=pltpu.P...  35.3 us
    ppermute x4, waiting for transfers between devices, body(): landed.append(lax.ppermute(give, 'pool', pairs))  24.9 us
    ppermute x4, starting transfers between devices, body(): landed.append(lax.ppermute(give, 'pool', pairs))  19 us
    pallas_call x4, Pallas kernels, pick(): pl.pallas_call(functools.partial(pick_kernel, (2 * pools + shift) * cap +...  11.3 us
    ppermute x5, waiting for transfers between devices, exchange(): sent.append(lax.ppermute(total.astype(BF16), 'ga', pairs))  10.5 us
    pallas_call x2, Pallas kernels, combine(): pl.pallas_call(functools.partial(combine_kernel, shapes, others, scaling)...  7.62 us
    ppermute x5, starting transfers between devices, exchange(): sent.append(lax.ppermute(total.astype(BF16), 'ga', pairs))  6.96 us
    ppermute x14, starting transfers between devices, body(): got.append([lax.ppermute(give, 'pert', swap_cores) for give in gives_now])  3.55 us
  transfers between devices with their start and end apart: 24, of which 8 were waited for; matrix products, arithmetic and copies ran while one was open for 6% of the time, Pallas kernels for 32%

profile of v5, /device:TPU:0, one launch (start us, length us, event | category | flops | bytes accessed | tf_op | source)
XLA Modules:
  0.0 133.9 jit_solution(7158012050800985215)
XLA Ops:
  0.6 1.8 %plan.1 = s32[64]{0:T(128)} custom-call(s32[3]{0:T(128)} %pad_add_fusion.1.ids, s32[64]{0:T(128)} %partners.1), custom_call_target="tpu_custom_call" | custom-call | flops 1 | bytes 1024 | tf_op jit(solution)/shard_map/plan/pallas_call | solution.py:65
  2.5 3.0 %pick.4 = bf16[5,720,128]{2,1,0:T(8,128)(2,1)} custom-call(s32[64]{0:T(128)} %plan.1, s32[3]{0:T(128)} %pad_add_fusion.1.ids, bf16[32,720,128]{2,1,0:T(8,128)(2,1)} %bitcast.15), custom_call_target="tpu_custom_call" | custom-call | flops 1 | bytes 1024 | tf_op jit(solution)/shard_map/pick/pallas_call | solution.py:88
  5.5 3.1 %collective-permute-start.5 = (bf16[5,720,128]{2,1,0:T(8,128)(2,1)}, bf16[5,720,128]{2,1,0:T(8,128)(2,1)S(1)}, u32[]{:S(2)}, u32[]{:S(2)}) collective-permute-start(bf16[5,720,128]{2,1,0:T(8,128)(2,1)} %pick.4), channel_id=1, source_target_pairs={{0,4},{4,8},{8,12},{12,0},{1,5},{5,9},{9,13},{13,1},{2,6},{6,10},{... | collective-permute-start | bytes 2764808 | tf_op jit(solution)/shard_map/ppermute | solution.py:331
  10.8 2.0 %broadcast_in_dim.35.pots = f32[6,2,360,128]{3,2,1,0:T(8,128)} broadcast(f32[6,2,360]{2,1,0:T(2,128)S(1)} %broadcast_in_dim.34), dimensions={0,1,2} | broadcast | bytes 2229120 | tf_op jit(solution)/shard_map/broadcast_in_dim | solution.py:322
  12.8 7.8 %couple.5 = (f32[5,6,128,128]{3,2,1,0:T(8,128)}, bf16[2,6,128,128]{3,2,1,0:T(8,128)(2,1)}, bf16[2,6,128,128]{3,2,1,0:T(8,128)(2,1)}, bf16[1,6,128,128]{3,2,1,0:T(8,128)(2,1)}) custom-call(s32[64]{0:T(128)} %plan.1, s32[3]{0:T(128)} %pad_add_fusion.1.ids, bf16[240,240]{1,0:T(8,128)(2,1)} %maximum_maximum_fusion.table, ...), custom_call_target="tpu_custom_call" | custom-call | flops 1 | bytes 1024 | tf_op jit(solution)/shard_map/couple/pallas_call | solution.py:177
  21.6 3.0 %pick.5 = bf16[5,720,128]{2,1,0:T(8,128)(2,1)} custom-call(s32[64]{0:T(128)} %plan.1, s32[3]{0:T(128)} %pad_add_fusion.1.ids, bf16[32,720,128]{2,1,0:T(8,128)(2,1)} %bitcast.18), custom_call_target="tpu_custom_call" | custom-call | flops 1 | bytes 1024 | tf_op jit(solution)/shard_map/pick/pallas_call | solution.py:88
  24.7 2.1 %collective-permute-start.10 = (bf16[5,720,128]{2,1,0:T(8,128)(2,1)}, bf16[5,720,128]{2,1,0:T(8,128)(2,1)S(1)}, u32[]{:S(2)}, u32[]{:S(2)}) collective-permute-start(bf16[5,720,128]{2,1,0:T(8,128)(2,1)} %pick.5), channel_id=1, source_target_pairs={{0,12},{4,0},{8,4},{12,8},{1,13},{5,1},{9,5},{13,9},{2,14},{6,2},{... | collective-permute-start | bytes 2764808 | tf_op jit(solution)/shard_map/ppermute | solution.py:331
  26.8 1.2 add_convert_fusion.5
  28.0 0.8 pad_maximum_fusion
  28.8 1.7 %collective-permute-start.4 = (bf16[5,6,64,128]{3,2,1,0:T(8,128)(2,1)}, bf16[5,6,64,128]{3,2,1,0:T(8,128)(2,1)}, u32[]{:S(2)}, u32[]{:S(2)}) collective-permute-start(bf16[5,6,64,128]{3,2,1,0:T(8,128)(2,1)} %pad_maximum_fusion), channel_id=1, source_target_pairs={{0,2},{2,0},{1,3},{3,1},{4,6},{6,4},{5,7},{7,5},{8,10},{10,8},{9,1... | collective-permute-start | bytes 1474568 | tf_op jit(solution)/shard_map/ppermute | solution.py:351
  30.5 1.6 %collective-permute-done.5.other = bf16[5,720,128]{2,1,0:T(8,128)(2,1)S(1)} collective-permute-done((bf16[5,720,128]{2,1,0:T(8,128)(2,1)}, bf16[5,720,128]{2,1,0:T(8,128)(2,1)S(1)}, u32[]{:S(2)}, u32[]{:S(2)}) %collective-permute-start.5) | collective-permute-done | bytes 921632 | tf_op jit(solution)/shard_map/ppermute | solution.py:331
  32.1 0.9 copy-done.5
  33.0 7.8 %couple.6 = (f32[5,6,128,128]{3,2,1,0:T(8,128)}, bf16[2,6,128,128]{3,2,1,0:T(8,128)(2,1)}, bf16[2,6,128,128]{3,2,1,0:T(8,128)(2,1)}, bf16[1,6,128,128]{3,2,1,0:T(8,128)(2,1)}) custom-call(s32[64]{0:T(128)} %plan.1, s32[3]{0:T(128)} %pad_add_fusion.1.ids, bf16[240,240]{1,0:T(8,128)(2,1)} %maximum_maximum_fusion.table, ...), custom_call_target="tpu_custom_call" | custom-call | flops 1 | bytes 1024 | tf_op jit(solution)/shard_map/couple/pallas_call | solution.py:177
  41.5 2.7 %pick.6 = bf16[3,720,128]{2,1,0:T(8,128)(2,1)} custom-call(s32[64]{0:T(128)} %plan.1, s32[3]{0:T(128)} %pad_add_fusion.1.ids, bf16[32,720,128]{2,1,0:T(8,128)(2,1)} %bitcast.20), custom_call_target="tpu_custom_call" | custom-call | flops 1 | bytes 1024 | tf_op jit(solution)/shard_map/pick/pallas_call | solution.py:88
  44.2 6.8 %collective-permute-done.10.other = bf16[5,720,128]{2,1,0:T(8,128)(2,1)S(1)} collective-permute-done((bf16[5,720,128]{2,1,0:T(8,128)(2,1)}, bf16[5,720,128]{2,1,0:T(8,128)(2,1)S(1)}, u32[]{:S(2)}, u32[]{:S(2)}) %collective-permute-start.10) | collective-permute-done | bytes 921632 | tf_op jit(solution)/shard_map/ppermute | solution.py:331
  51.0 12.9 %collective-permute-start.15 = (bf16[3,720,128]{2,1,0:T(8,128)(2,1)}, bf16[3,720,128]{2,1,0:T(8,128)(2,1)}, u32[]{:S(2)}, u32[]{:S(2)}) collective-permute-start(bf16[3,720,128]{2,1,0:T(8,128)(2,1)} %pick.6), channel_id=1, source_target_pairs={{0,8},{4,12},{8,0},{12,4},{1,9},{5,13},{9,1},{13,5},{2,10},{6,14},... | collective-permute-start | bytes 1658888 | tf_op jit(solution)/shard_map/ppermute | solution.py:331
  64.0 8.7 %couple.7 = (f32[5,6,128,128]{3,2,1,0:T(8,128)}, bf16[2,6,128,128]{3,2,1,0:T(8,128)(2,1)}, bf16[2,6,128,128]{3,2,1,0:T(8,128)(2,1)}, bf16[1,6,128,128]{3,2,1,0:T(8,128)(2,1)}) custom-call(s32[64]{0:T(128)} %plan.1, s32[3]{0:T(128)} %pad_add_fusion.1.ids, bf16[240,240]{1,0:T(8,128)(2,1)} %maximum_maximum_fusion.table, ...), custom_call_target="tpu_custom_call" | custom-call | flops 1 | bytes 1024 | tf_op jit(solution)/shard_map/couple/pallas_call | solution.py:177
  73.5 1.1 add_convert_fusion.3
  74.7 1.6 %collective-permute-start.9 = (bf16[5,6,64,128]{3,2,1,0:T(8,128)(2,1)S(1)}, bf16[5,6,64,128]{3,2,1,0:T(8,128)(2,1)S(1)}, u32[]{:S(2)}, u32[]{:S(2)}) collective-permute-start(bf16[5,6,64,128]{3,2,1,0:T(8,128)(2,1)S(1)} %pad_maximum_fusion.1), channel_id=1, source_target_pairs={{0,2},{2,0},{1,3},{3,1},{4,6},{6,4},{5,7},{7,5},{8,10},{10,8},{9,1... | collective-permute-start | bytes 1474568 | tf_op jit(solution)/shard_map/ppermute | solution.py:351
  76.5 0.9 collective-permute-start.14
  77.4 2.5 %pick.7 = bf16[2,720,128]{2,1,0:T(8,128)(2,1)} custom-call(s32[64]{0:T(128)} %plan.1, s32[3]{0:T(128)} %pad_add_fusion.1.ids, bf16[32,720,128]{2,1,0:T(8,128)(2,1)} %bitcast.22), custom_call_target="tpu_custom_call" | custom-call | flops 1 | bytes 1024 | tf_op jit(solution)/shard_map/pick/pallas_call | solution.py:88
  79.9 0.9 collective-permute-start.20
  80.8 16.6 %collective-permute-done.15.other = bf16[3,720,128]{2,1,0:T(8,128)(2,1)} collective-permute-done((bf16[3,720,128]{2,1,0:T(8,128)(2,1)}, bf16[3,720,128]{2,1,0:T(8,128)(2,1)}, u32[]{:S(2)}, u32[]{:S(2)}) %collective-permute-start.15) | collective-permute-done | bytes 552992 | tf_op jit(solution)/shard_map/ppermute | solution.py:331
  98.2 3.8 %combine.2.refs_0_ = bf16[16,6,64,128]{3,2,1,0:T(8,128)(2,1)} custom-call(s32[64]{0:T(128)} %plan.1, f32[5,6,128,128]{3,2,1,0:T(8,128)} %get-tuple-element.40.refs_0_, bf16[2,6,128,128]{3,2,1,0:T(8,128)(2,1)} %collective-permute-done.1.refs_1_, bf16[2,6,128,128]{3,2,1,0:T(8,128)(2,1)} %collective-permute-done.2.refs_2_, bf16[1,6,128,128]{3,2,1,0:T(8,128)(2,1)} %copy-done.19, ...), custom_call_target="tpu_custom_call" | custom-call | flops 1 | bytes 1024 | tf_op jit(solution)/shard_map/combine/pallas_call | solution.py:248
  102.0 6.5 %couple.8 = (f32[3,6,128,128]{3,2,1,0:T(8,128)}, bf16[1,6,128,128]{3,2,1,0:T(8,128)(2,1)}, bf16[1,6,128,128]{3,2,1,0:T(8,128)(2,1)}, bf16[1,6,128,128]{3,2,1,0:T(8,128)(2,1)}) custom-call(s32[64]{0:T(128)} %plan.1, s32[3]{0:T(128)} %pad_add_fusion.1.ids, bf16[240,240]{1,0:T(8,128)(2,1)} %maximum_maximum_fusion.table, ...), custom_call_target="tpu_custom_call" | custom-call | flops 1 | bytes 1024 | tf_op jit(solution)/shard_map/couple/pallas_call | solution.py:177
  109.1 1.1 collective-permute-done.16.refs_7_
  110.7 4.5 %couple.9 = (f32[2,6,128,128]{3,2,1,0:T(8,128)}, bf16[1,6,128,128]{3,2,1,0:T(8,128)(2,1)}, bf16[1,6,128,128]{3,2,1,0:T(8,128)(2,1)}) custom-call(s32[64]{0:T(128)} %plan.1, s32[3]{0:T(128)} %pad_add_fusion.1.ids, bf16[240,240]{1,0:T(8,128)(2,1)} %maximum_maximum_fusion.table, f32[6,2,360,128]{3,2,1,0:T(8,128)} %broadcast_in_dim.35.pots, ...), custom_call_target="tpu_custom_call" | custom-call | flops 1 | bytes 1024 | tf_op jit(solution)/shard_map/couple/pallas_call | solution.py:177
  116.0 1.6 %collective-permute-start.19 = (bf16[3,6,64,128]{3,2,1,0:T(8,128)(2,1)S(1)}, bf16[3,6,64,128]{3,2,1,0:T(8,128)(2,1)S(1)}, u32[]{:S(2)}, u32[]{:S(2)}) collective-permute-start(bf16[3,6,64,128]{3,2,1,0:T(8,128)(2,1)S(1)} %pad_maximum_fusion.3), channel_id=1, source_target_pairs={{0,2},{2,0},{1,3},{3,1},{4,6},{6,4},{5,7},{7,5},{8,10},{10,8},{9,1... | collective-permute-start | bytes 884744 | tf_op jit(solution)/shard_map/ppermute | solution.py:351
  117.6 1.3 collective-permute-start.23
  118.9 7.0 %collective-permute-done.19.refs_10_ = bf16[3,6,64,128]{3,2,1,0:T(8,128)(2,1)S(1)} collective-permute-done((bf16[3,6,64,128]{3,2,1,0:T(8,128)(2,1)S(1)}, bf16[3,6,64,128]{3,2,1,0:T(8,128)(2,1)S(1)}, u32[]{:S(2)}, u32[]{:S(2)}) %collective-permute-start.19) | collective-permute-done | bytes 294944 | tf_op jit(solution)/shard_map/ppermute | solution.py:351
  125.9 3.5 %collective-permute-done.23.refs_14_ = bf16[2,6,64,128]{3,2,1,0:T(8,128)(2,1)S(1)} collective-permute-done((bf16[2,6,64,128]{3,2,1,0:T(8,128)(2,1)S(1)}, bf16[2,6,64,128]{3,2,1,0:T(8,128)(2,1)S(1)}, u32[]{:S(2)}, u32[]{:S(2)}) %collective-permute-start.23) | collective-permute-done | bytes 196640 | tf_op jit(solution)/shard_map/ppermute | solution.py:351
  130.1 3.8 %combine.3 = bf16[16,6,64,128]{3,2,1,0:T(8,128)(2,1)} custom-call(s32[64]{0:T(128)} %plan.1, bf16[16,6,64,128]{3,2,1,0:T(8,128)(2,1)} %combine.2.refs_0_, f32[5,6,128,128]{3,2,1,0:T(8,128)} %get-tuple-element.53.refs_1_, bf16[2,6,128,128]{3,2,1,0:T(8,128)(2,1)} %copy-done.7, bf16[2,6,128,128]{3,2,1,0:T(8,128)(2,1)} %copy-done.8, ...), custom_call_target="tpu_custom_call", output_to_operand_aliasing={{}: (1, {})} | custom-call | flops 1 | bytes 1024 | tf_op jit(solution)/shard_map/combine/pallas_call | solution.py:248
  (115 shorter events, 8.9 us)
Async XLA Ops:
  5.5 26.6 %collective-permute-start.5 = (bf16[5,720,128]{2,1,0:T(8,128)(2,1)}, bf16[5,720,128]{2,1,0:T(8,128)(2,1)S(1)}, u32[]{:S(2)}, u32[]{:S(2)}) collective-permute-start(bf16[5,720,128]{2,1,0:T(8,128)(2,1)} %pick.4), channel_id=1, source_target_pairs={{0,4},{4,8},{8,12},{12,0},{1,5},{5,9},{9,13},{13,1},{2,6},{6,10},{... | collective-permute-start | bytes 2764808 | tf_op jit(solution)/shard_map/ppermute | solution.py:331
  8.6 1.7 %collective-permute-start = (f32[3,3,240]{2,1,0:T(4,128)S(1)}, f32[3,3,240]{2,1,0:T(4,128)S(1)}, u32[]{:S(2)}, u32[]{:S(2)}) collective-permute-start(f32[3,3,240]{2,1,0:T(4,128)S(1)} %bitcast.29), channel_id=1, source_target_pairs={{0,1},{1,0},{2,3},{3,2},{4,5},{5,4},{6,7},{7,6},{8,9},{9,8},{10,11... | collective-permute-start | bytes 25928 | tf_op jit(solution)/shard_map/ppermute | solution.py:308
  20.6 6.2 %collective-permute-start.3 = (bf16[1,6,128,128]{3,2,1,0:T(8,128)(2,1)}, bf16[1,6,128,128]{3,2,1,0:T(8,128)(2,1)S(1)}, u32[]{:S(2)}, u32[]{:S(2)}) collective-permute-start(bf16[1,6,128,128]{3,2,1,0:T(8,128)(2,1)} %get-tuple-element.43), channel_id=1, source_target_pairs={{0,1},{1,0},{2,3},{3,2},{4,5},{5,4},{6,7},{7,6},{8,9},{9,8},{10,11... | collective-permute-start | bytes 589832 | tf_op jit(solution)/shard_map/ppermute | solution.py:375
  21.1 5.7 %collective-permute-start.1 = (bf16[2,6,128,128]{3,2,1,0:T(8,128)(2,1)}, bf16[2,6,128,128]{3,2,1,0:T(8,128)(2,1)}, u32[]{:S(2)}, u32[]{:S(2)}) collective-permute-start(bf16[2,6,128,128]{3,2,1,0:T(8,128)(2,1)} %get-tuple-element.41), channel_id=1, source_target_pairs={{0,1},{1,0},{2,3},{3,2},{4,5},{5,4},{6,7},{7,6},{8,9},{9,8},{10,11... | collective-permute-start | bytes 1179656 | tf_op jit(solution)/shard_map/ppermute | solution.py:375
  21.2 5.6 %collective-permute-start.2 = (bf16[2,6,128,128]{3,2,1,0:T(8,128)(2,1)}, bf16[2,6,128,128]{3,2,1,0:T(8,128)(2,1)}, u32[]{:S(2)}, u32[]{:S(2)}) collective-permute-start(bf16[2,6,128,128]{3,2,1,0:T(8,128)(2,1)} %get-tuple-element.42), channel_id=1, source_target_pairs={{0,1},{1,0},{2,3},{3,2},{4,5},{5,4},{6,7},{7,6},{8,9},{9,8},{10,11... | collective-permute-start | bytes 1179656 | tf_op jit(solution)/shard_map/ppermute | solution.py:375
  24.7 26.3 %collective-permute-start.10 = (bf16[5,720,128]{2,1,0:T(8,128)(2,1)}, bf16[5,720,128]{2,1,0:T(8,128)(2,1)S(1)}, u32[]{:S(2)}, u32[]{:S(2)}) collective-permute-start(bf16[5,720,128]{2,1,0:T(8,128)(2,1)} %pick.5), channel_id=1, source_target_pairs={{0,12},{4,0},{8,4},{12,8},{1,13},{5,1},{9,5},{13,9},{2,14},{6,2},{... | collective-permute-start | bytes 2764808 | tf_op jit(solution)/shard_map/ppermute | solution.py:331
  26.8 14.1 %copy-start.19 = (bf16[1,6,128,128]{3,2,1,0:T(8,128)(2,1)}, bf16[1,6,128,128]{3,2,1,0:T(8,128)(2,1)S(1)}, u32[]{:S(2)}) copy-start(bf16[1,6,128,128]{3,2,1,0:T(8,128)(2,1)S(1)} %collective-permute-done.3.refs_3_) | copy-start | bytes 589828
  28.8 35.2 %collective-permute-start.4 = (bf16[5,6,64,128]{3,2,1,0:T(8,128)(2,1)}, bf16[5,6,64,128]{3,2,1,0:T(8,128)(2,1)}, u32[]{:S(2)}, u32[]{:S(2)}) collective-permute-start(bf16[5,6,64,128]{3,2,1,0:T(8,128)(2,1)} %pad_maximum_fusion), channel_id=1, source_target_pairs={{0,2},{2,0},{1,3},{3,1},{4,6},{6,4},{5,7},{7,5},{8,10},{10,8},{9,1... | collective-permute-start | bytes 1474568 | tf_op jit(solution)/shard_map/ppermute | solution.py:351
  40.8 23.1 %collective-permute-start.8 = (bf16[1,6,128,128]{3,2,1,0:T(8,128)(2,1)}, bf16[1,6,128,128]{3,2,1,0:T(8,128)(2,1)S(1)}, u32[]{:S(2)}, u32[]{:S(2)}) collective-permute-start(bf16[1,6,128,128]{3,2,1,0:T(8,128)(2,1)} %get-tuple-element.49), channel_id=1, source_target_pairs={{0,1},{1,0},{2,3},{3,2},{4,5},{5,4},{6,7},{7,6},{8,9},{9,8},{10,11... | collective-permute-start | bytes 589832 | tf_op jit(solution)/shard_map/ppermute | solution.py:375
  40.9 23.1 %collective-permute-start.6 = (bf16[2,6,128,128]{3,2,1,0:T(8,128)(2,1)}, bf16[2,6,128,128]{3,2,1,0:T(8,128)(2,1)S(1)}, u32[]{:S(2)}, u32[]{:S(2)}) collective-permute-start(bf16[2,6,128,128]{3,2,1,0:T(8,128)(2,1)} %get-tuple-element.47), channel_id=1, source_target_pairs={{0,1},{1,0},{2,3},{3,2},{4,5},{5,4},{6,7},{7,6},{8,9},{9,8},{10,11... | collective-permute-start | bytes 1179656 | tf_op jit(solution)/shard_map/ppermute | solution.py:375
  41.4 22.5 %copy-start.2 = (f32[5,6,128,128]{3,2,1,0:T(8,128)S(1)}, f32[5,6,128,128]{3,2,1,0:T(8,128)}, u32[]{:S(2)}) copy-start(f32[5,6,128,128]{3,2,1,0:T(8,128)} %get-tuple-element.46.refs_5_) | copy-start | bytes 5898244
  41.4 22.6 %collective-permute-start.7 = (bf16[2,6,128,128]{3,2,1,0:T(8,128)(2,1)}, bf16[2,6,128,128]{3,2,1,0:T(8,128)(2,1)S(1)}, u32[]{:S(2)}, u32[]{:S(2)}) collective-permute-start(bf16[2,6,128,128]{3,2,1,0:T(8,128)(2,1)} %get-tuple-element.48), channel_id=1, source_target_pairs={{0,1},{1,0},{2,3},{3,2},{4,5},{5,4},{6,7},{7,6},{8,9},{9,8},{10,11... | collective-permute-start | bytes 1179656 | tf_op jit(solution)/shard_map/ppermute | solution.py:375
  51.0 13.0 %copy-start.6 = (bf16[5,720,128]{2,1,0:T(8,128)(2,1)}, bf16[5,720,128]{2,1,0:T(8,128)(2,1)S(1)}, u32[]{:S(2)}) copy-start(bf16[5,720,128]{2,1,0:T(8,128)(2,1)S(1)} %collective-permute-done.10.other) | copy-start | bytes 2764804
  51.0 46.4 %collective-permute-start.15 = (bf16[3,720,128]{2,1,0:T(8,128)(2,1)}, bf16[3,720,128]{2,1,0:T(8,128)(2,1)}, u32[]{:S(2)}, u32[]{:S(2)}) collective-permute-start(bf16[3,720,128]{2,1,0:T(8,128)(2,1)} %pick.6), channel_id=1, source_target_pairs={{0,8},{4,12},{8,0},{12,4},{1,9},{5,13},{9,1},{13,5},{2,10},{6,14},... | collective-permute-start | bytes 1658888 | tf_op jit(solution)/shard_map/ppermute | solution.py:331
  63.9 8.8 %copy-start.20 = (bf16[1,6,128,128]{3,2,1,0:T(8,128)(2,1)}, bf16[1,6,128,128]{3,2,1,0:T(8,128)(2,1)S(1)}, u32[]{:S(2)}) copy-start(bf16[1,6,128,128]{3,2,1,0:T(8,128)(2,1)S(1)} %collective-permute-done.8.refs_8_) | copy-start | bytes 589828
  64.0 8.8 %copy-start.9 = (bf16[2,6,128,128]{3,2,1,0:T(8,128)(2,1)}, bf16[2,6,128,128]{3,2,1,0:T(8,128)(2,1)S(1)}, u32[]{:S(2)}) copy-start(bf16[2,6,128,128]{3,2,1,0:T(8,128)(2,1)S(1)} %collective-permute-done.6.refs_6_) | copy-start | bytes 1179652
  64.0 9.0 %copy-start.10 = (bf16[2,6,128,128]{3,2,1,0:T(8,128)(2,1)}, bf16[2,6,128,128]{3,2,1,0:T(8,128)(2,1)S(1)}, u32[]{:S(2)}) copy-start(bf16[2,6,128,128]{3,2,1,0:T(8,128)(2,1)S(1)} %collective-permute-done.7.refs_7_) | copy-start | bytes 1179652
  72.8 3.5 %collective-permute-start.11 = (bf16[2,6,128,128]{3,2,1,0:T(8,128)(2,1)}, bf16[2,6,128,128]{3,2,1,0:T(8,128)(2,1)S(1)}, u32[]{:S(2)}, u32[]{:S(2)}) collective-permute-start(bf16[2,6,128,128]{3,2,1,0:T(8,128)(2,1)} %get-tuple-element.54), channel_id=1, source_target_pairs={{0,1},{1,0},{2,3},{3,2},{4,5},{5,4},{6,7},{7,6},{8,9},{9,8},{10,11... | collective-permute-start | bytes 1179656 | tf_op jit(solution)/shard_map/ppermute | solution.py:375
  73.0 3.3 %collective-permute-start.12 = (bf16[2,6,128,128]{3,2,1,0:T(8,128)(2,1)}, bf16[2,6,128,128]{3,2,1,0:T(8,128)(2,1)S(1)}, u32[]{:S(2)}, u32[]{:S(2)}) collective-permute-start(bf16[2,6,128,128]{3,2,1,0:T(8,128)(2,1)} %get-tuple-element.55), channel_id=1, source_target_pairs={{0,1},{1,0},{2,3},{3,2},{4,5},{5,4},{6,7},{7,6},{8,9},{9,8},{10,11... | collective-permute-start | bytes 1179656 | tf_op jit(solution)/shard_map/ppermute | solution.py:375
  73.3 2.9 %collective-permute-start.13 = (bf16[1,6,128,128]{3,2,1,0:T(8,128)(2,1)}, bf16[1,6,128,128]{3,2,1,0:T(8,128)(2,1)S(1)}, u32[]{:S(2)}, u32[]{:S(2)}) collective-permute-start(bf16[1,6,128,128]{3,2,1,0:T(8,128)(2,1)} %get-tuple-element.56), channel_id=1, source_target_pairs={{0,1},{1,0},{2,3},{3,2},{4,5},{5,4},{6,7},{7,6},{8,9},{9,8},{10,11... | collective-permute-start | bytes 589832 | tf_op jit(solution)/shard_map/ppermute | solution.py:375
  74.7 22.7 %collective-permute-start.9 = (bf16[5,6,64,128]{3,2,1,0:T(8,128)(2,1)S(1)}, bf16[5,6,64,128]{3,2,1,0:T(8,128)(2,1)S(1)}, u32[]{:S(2)}, u32[]{:S(2)}) collective-permute-start(bf16[5,6,64,128]{3,2,1,0:T(8,128)(2,1)S(1)} %pad_maximum_fusion.1), channel_id=1, source_target_pairs={{0,2},{2,0},{1,3},{3,1},{4,6},{6,4},{5,7},{7,5},{8,10},{10,8},{9,1... | collective-permute-start | bytes 1474568 | tf_op jit(solution)/shard_map/ppermute | solution.py:351
  76.5 34.2 %collective-permute-start.14 = (bf16[5,6,64,128]{3,2,1,0:T(8,128)(2,1)S(1)}, bf16[5,6,64,128]{3,2,1,0:T(8,128)(2,1)S(1)}, u32[]{:S(2)}, u32[]{:S(2)}) collective-permute-start(bf16[5,6,64,128]{3,2,1,0:T(8,128)(2,1)S(1)} %pad_maximum_fusion.2), channel_id=1, source_target_pairs={{0,2},{2,0},{1,3},{3,1},{4,6},{6,4},{5,7},{7,5},{8,10},{10,8},{9,1... | collective-permute-start | bytes 1474568 | tf_op jit(solution)/shard_map/ppermute | solution.py:351
  79.9 29.2 %collective-permute-start.20 = (bf16[2,720,128]{2,1,0:T(8,128)(2,1)}, bf16[2,720,128]{2,1,0:T(8,128)(2,1)S(1)}, u32[]{:S(2)}, u32[]{:S(2)}) collective-permute-start(bf16[2,720,128]{2,1,0:T(8,128)(2,1)} %pick.7), channel_id=1, source_target_pairs={{0,8},{4,12},{8,0},{12,4},{1,9},{5,13},{9,1},{13,5},{2,10},{6,14},... | collective-permute-start | bytes 1105928 | tf_op jit(solution)/shard_map/ppermute | solution.py:331
  108.5 1.7 %collective-permute-start.16 = (bf16[1,6,128,128]{3,2,1,0:T(8,128)(2,1)}, bf16[1,6,128,128]{3,2,1,0:T(8,128)(2,1)S(1)}, u32[]{:S(2)}, u32[]{:S(2)}) collective-permute-start(bf16[1,6,128,128]{3,2,1,0:T(8,128)(2,1)} %get-tuple-element.63), channel_id=1, source_target_pairs={{0,1},{1,0},{2,3},{3,2},{4,5},{5,4},{6,7},{7,6},{8,9},{9,8},{10,11... | collective-permute-start | bytes 589832 | tf_op jit(solution)/shard_map/ppermute | solution.py:375
  108.5 1.9 %collective-permute-start.17 = (bf16[1,6,128,128]{3,2,1,0:T(8,128)(2,1)}, bf16[1,6,128,128]{3,2,1,0:T(8,128)(2,1)S(1)}, u32[]{:S(2)}, u32[]{:S(2)}) collective-permute-start(bf16[1,6,128,128]{3,2,1,0:T(8,128)(2,1)} %get-tuple-element.64), channel_id=1, source_target_pairs={{0,1},{1,0},{2,3},{3,2},{4,5},{5,4},{6,7},{7,6},{8,9},{9,8},{10,11... | collective-permute-start | bytes 589832 | tf_op jit(solution)/shard_map/ppermute | solution.py:375
  109.0 1.7 %collective-permute-start.18 = (bf16[1,6,128,128]{3,2,1,0:T(8,128)(2,1)}, bf16[1,6,128,128]{3,2,1,0:T(8,128)(2,1)S(1)}, u32[]{:S(2)}, u32[]{:S(2)}) collective-permute-start(bf16[1,6,128,128]{3,2,1,0:T(8,128)(2,1)} %get-tuple-element.65), channel_id=1, source_target_pairs={{0,1},{1,0},{2,3},{3,2},{4,5},{5,4},{6,7},{7,6},{8,9},{9,8},{10,11... | collective-permute-start | bytes 589832 | tf_op jit(solution)/shard_map/ppermute | solution.py:375
  115.2 2.3 %collective-permute-start.21 = (bf16[1,6,128,128]{3,2,1,0:T(8,128)(2,1)}, bf16[1,6,128,128]{3,2,1,0:T(8,128)(2,1)S(1)}, u32[]{:S(2)}, u32[]{:S(2)}) collective-permute-start(bf16[1,6,128,128]{3,2,1,0:T(8,128)(2,1)} %get-tuple-element.71), channel_id=1, source_target_pairs={{0,1},{1,0},{2,3},{3,2},{4,5},{5,4},{6,7},{7,6},{8,9},{9,8},{10,11... | collective-permute-start | bytes 589832 | tf_op jit(solution)/shard_map/ppermute | solution.py:375
  115.5 2.0 %collective-permute-start.22 = (bf16[1,6,128,128]{3,2,1,0:T(8,128)(2,1)}, bf16[1,6,128,128]{3,2,1,0:T(8,128)(2,1)S(1)}, u32[]{:S(2)}, u32[]{:S(2)}) collective-permute-start(bf16[1,6,128,128]{3,2,1,0:T(8,128)(2,1)} %get-tuple-element.72), channel_id=1, source_target_pairs={{0,1},{1,0},{2,3},{3,2},{4,5},{5,4},{6,7},{7,6},{8,9},{9,8},{10,11... | collective-permute-start | bytes 589832 | tf_op jit(solution)/shard_map/ppermute | solution.py:375
  116.0 9.9 %collective-permute-start.19 = (bf16[3,6,64,128]{3,2,1,0:T(8,128)(2,1)S(1)}, bf16[3,6,64,128]{3,2,1,0:T(8,128)(2,1)S(1)}, u32[]{:S(2)}, u32[]{:S(2)}) collective-permute-start(bf16[3,6,64,128]{3,2,1,0:T(8,128)(2,1)S(1)} %pad_maximum_fusion.3), channel_id=1, source_target_pairs={{0,2},{2,0},{1,3},{3,1},{4,6},{6,4},{5,7},{7,5},{8,10},{10,8},{9,1... | collective-permute-start | bytes 884744 | tf_op jit(solution)/shard_map/ppermute | solution.py:351
  117.5 11.9 %copy-start.16 = (bf16[1,6,128,128]{3,2,1,0:T(8,128)(2,1)}, bf16[1,6,128,128]{3,2,1,0:T(8,128)(2,1)S(1)}, u32[]{:S(2)}) copy-start(bf16[1,6,128,128]{3,2,1,0:T(8,128)(2,1)S(1)} %collective-permute-done.21.refs_12_) | copy-start | bytes 589828
  117.5 11.9 %copy-start.17 = (bf16[1,6,128,128]{3,2,1,0:T(8,128)(2,1)}, bf16[1,6,128,128]{3,2,1,0:T(8,128)(2,1)S(1)}, u32[]{:S(2)}) copy-start(bf16[1,6,128,128]{3,2,1,0:T(8,128)(2,1)S(1)} %collective-permute-done.22.refs_13_) | copy-start | bytes 589828
  117.6 11.7 %collective-permute-start.23 = (bf16[2,6,64,128]{3,2,1,0:T(8,128)(2,1)S(1)}, bf16[2,6,64,128]{3,2,1,0:T(8,128)(2,1)S(1)}, u32[]{:S(2)}, u32[]{:S(2)}) collective-permute-start(bf16[2,6,64,128]{3,2,1,0:T(8,128)(2,1)S(1)} %pad_maximum_fusion.4), channel_id=1, source_target_pairs={{0,2},{2,0},{1,3},{3,1},{4,6},{6,4},{5,7},{7,5},{8,10},{10,8},{9,1... | collective-permute-start | bytes 589832 | tf_op jit(solution)/shard_map/ppermute | solution.py:351
  (18 other events, 70.2 us)
